TPU v7x, 32 devices: a whole 2x2x4 slice. The times are simulated.
32 devices in a mesh: tm: 4 (over y, x), area: 8 (over z, core).
Axes of the slice: x: 2, y: 2, z: 4, core: 2. Of those that a mesh axis runs over, the one named last changes fastest.
Arguments:
- gradient: float32 [168, 32, 512], P('tm', 'area'), may hold values from -72 to 72
- barrier: float32 [1], replicated, may hold values from 0.5 to 2
- slack: float32 [168, 32, 512], P('tm', 'area'), may hold values from 0.5 to 2
- hess_diag: float32 [168, 32, 512], P('tm', 'area'), may hold values from 0.5 to 2
- tile: float32 [32, 512, 512], P('area'), may hold values from -0.1 to 4.1, as said below
- ramp_weight: float32 [32, 512], P('area'), may hold values from 0.5 to 2
- bus_coupling: float32 [32, 512], P('area'), may hold values from 0.5 to 2
- tie_offset: int32 [32, 4], replicated, may hold values from 1 to 4, as said below
- tie_admittance: float32 [32, 4], replicated, may hold values from 0.5 to 2
- con_sens: float32 [2048, 512], P('area'), may hold values from -0.9 to 0.9
- con_weight: float32 [2048, 168], P('area', 'tm'), may hold values from 0.5 to 2
- con_owner: int32 [2048, 1], P('area'), may hold values from 0 to 31; in each aligned block of 256 rows (0 to 255, 256 to 511, ...) at most 16 rows name the same one
- step_guess: float32 [168, 32, 512], P('tm', 'area'), may hold values from -1.2 to 1.2
Outputs:
- newton_step: float32 [168, 32, 512], P('tm', 'area')
- residual: float32 [168, 32, 512], P('tm', 'area')
Inputs may be any that keep to these rules, and one draw needn't show every extreme that they name: `tie_offset`: each tie partner lies 1 to 4 areas above its area; a partner past the last area is absent. `con_owner`: on the rows of one index of area, no area owns more than 16 blocks. Each area's tile is symmetric.
All inputs are finite; a program needn't handle non-finite values.
Results may differ from a plain program's by a relative error of at most 0.00028.
Values sent between devices are 32-bit elements; how exact they have to be, the bound alone decides.
No kernel may reach another device: no remote copies, remote signals or barrier semaphores. Data moves between devices by JAX's collectives and lax.ppermute only.
A program may use at most 64 MiB of HBM per device.

v0:
```python
import jax
import jax.numpy as jnp
from jax import lax
from jax.sharding import PartitionSpec as P

TIES = 4
ITERS = 2


def extended_2(array, sides, width):
    for axis, dim in sides:
        size, length = (lax.axis_size(axis), array.shape[dim])
        up = [(i, (i + 1) % size) for i in range(size - 1)]
        down = [(j, i) for i, j in up]
        last = lax.slice_in_dim(array, length - width, length, axis=dim)
        leading = lax.slice_in_dim(array, 0, width, axis=dim)
        before = lax.ppermute(last, axis, up)
        after = lax.ppermute(leading, axis, down)
        array = jnp.concatenate([before, array, after], axis=dim)
    return array


def from_behind(value, axis, steps):
    count = lax.axis_size(axis)
    leading, last = (max(0, -steps), min(count, count - steps))
    return lax.ppermute(value, axis, [(source, source + steps) for source in range(leading, last)])


def tie_terms(
    extended, base_area, source_count, tie_offset, tie_admittance, span_areas, hour_count
):
    extended_count = extended.shape[1]
    pad_offset = jnp.concatenate(
        [
            jnp.ones((span_areas, TIES), jnp.int32),
            tie_offset,
            jnp.ones((span_areas, TIES), jnp.int32),
        ],
        0,
    )
    pad_gain = jnp.concatenate(
        [
            jnp.zeros((span_areas, TIES), jnp.float32),
            tie_admittance,
            jnp.zeros((span_areas, TIES), jnp.float32),
        ],
        0,
    )
    start_row = base_area + span_areas
    offsets = lax.dynamic_slice(pad_offset, (start_row, jnp.int32(0)), (source_count, TIES))
    gain_rows = lax.dynamic_slice(pad_gain, (start_row, jnp.int32(0)), (source_count, TIES))
    target = jnp.arange(source_count, dtype=jnp.int32)[:, None] + offsets
    select = (
        target[:, :, None] == jnp.arange(extended_count, dtype=jnp.int32)[None, None, :]
    ).astype(jnp.float32)
    scaled_field = extended[:hour_count]
    coupling = extended[hour_count]
    far_field = jnp.einsum("skj,tjb->tskb", select, scaled_field, precision=lax.Precision.HIGHEST)
    far_coupling = jnp.einsum("skj,jb->skb", select, coupling, precision=lax.Precision.HIGHEST)
    near_field = scaled_field[:, :source_count]
    near_coupling = coupling[:source_count]
    tie_flows = gain_rows[None, :, :, None] * (
        far_coupling[None] * near_field[:, :, None, :] - near_coupling[None, :, None, :] * far_field
    )
    summed = -jnp.einsum("skj,tskb->tjb", select, tie_flows, precision=lax.Precision.HIGHEST)
    return summed.at[:, :source_count].add(jnp.sum(tie_flows, axis=2))


def paired(residual, applied):
    return lax.psum((jnp.sum(residual * residual), jnp.sum(residual * applied)), ("tm", "area"))


def body(
    gradient,
    barrier,
    slack,
    hess_diag,
    tile,
    ramp_weight,
    bus_coupling,
    tie_offset,
    tie_admittance,
    con_sens,
    con_weight,
    con_owner,
    step_guess,
):
    hour_count, span_areas, var_width = gradient.shape
    area_total = tie_offset.shape[0]
    groups = lax.axis_size("area")
    first_area = lax.axis_index("area") * span_areas
    rows_held = con_sens.shape[0]
    capacity = max(2, (2 * rows_held + area_total - 1) // area_total)
    owner_area = con_owner[:, 0]
    owner_marks = (owner_area[:, None] == jnp.arange(area_total, dtype=jnp.int32)[None, :]).astype(
        jnp.int32
    )
    before = jnp.cumsum(owner_marks, axis=0) - owner_marks
    slot_rank = jnp.sum(before * owner_marks, axis=1)
    slot_index = owner_area * capacity + slot_rank
    send_sens = (
        jnp.zeros((area_total * capacity, var_width), jnp.float32).at[slot_index].set(con_sens)
    )
    send_weight = (
        jnp.zeros((area_total * capacity, hour_count), jnp.float32).at[slot_index].set(con_weight)
    )
    send_sens = send_sens.reshape(groups, span_areas * capacity, var_width)
    send_weight = send_weight.reshape(groups, span_areas * capacity, hour_count)
    got_sensitivity, got_weight = (
        lax.all_to_all(send_sens, "area", split_axis=0, concat_axis=0, tiled=True),
        lax.all_to_all(send_weight, "area", split_axis=0, concat_axis=0, tiled=True),
    )
    owned_sens = got_sensitivity.reshape(groups, span_areas, capacity, var_width)
    owned_weight = jnp.transpose(
        got_weight.reshape(groups, span_areas, capacity, hour_count), (3, 1, 0, 2)
    )
    diagonal_entries = hess_diag + barrier[0] / (slack * slack)
    right_side = barrier[0] / slack - gradient

    def operate(input_vector):
        operator_output = diagonal_entries * input_vector + jnp.einsum(
            "uog,ogn->uon", input_vector, tile, precision=lax.Precision.HIGHEST
        )
        padded = extended_2(input_vector, (("tm", 0),), 1)
        operator_output = operator_output + ramp_weight[None] * (
            2.0 * input_vector - padded[:-2] - padded[2:]
        )
        packed = jnp.concatenate([bus_coupling[None] * input_vector, bus_coupling[None]], 0)
        upper_block = from_behind(packed, "area", -1)
        extended = jnp.concatenate([packed, upper_block], 1)
        summed = tie_terms(
            extended, first_area, span_areas, tie_offset, tie_admittance, span_areas, hour_count
        )
        tie_part = summed[:, :span_areas] + from_behind(summed[:, span_areas:], "area", 1)
        operator_output = operator_output + tie_part
        flows_owned = jnp.einsum(
            "slcb,tlb->tlsc", owned_sens, input_vector, precision=lax.Precision.HIGHEST
        )
        return operator_output + jnp.einsum(
            "tlsc,slcb->tlb",
            flows_owned * owned_weight,
            owned_sens,
            precision=lax.Precision.HIGHEST,
        )

    solution = step_guess
    residual = right_side - operate(solution)
    applied = operate(residual)
    norm_now, product = paired(residual, applied)
    step_size = norm_now / product
    search_direction = residual
    applied_dir = applied
    for iteration in range(ITERS):
        solution = solution + step_size * search_direction
        residual = residual - step_size * applied_dir
        if iteration + 1 < ITERS:
            applied = operate(residual)
            norm_next, product = paired(residual, applied)
            beta_ratio = norm_next / norm_now
            step_size = norm_next / (product - beta_ratio * norm_next / step_size)
            search_direction = residual + beta_ratio * search_direction
            applied_dir = applied + beta_ratio * applied_dir
            norm_now = norm_next
    return (solution, residual)


def solution(mesh):
    placed = (
        P("tm", "area", None),
        P(),
        P("tm", "area", None),
        P("tm", "area", None),
        P("area", None, None),
        P("area", None),
        P("area", None),
        P(),
        P(),
        P("area", None),
        P("area", "tm"),
        P("area", None),
        P("tm", "area", None),
    )
    return jax.shard_map(
        body,
        mesh=mesh,
        in_specs=placed,
        out_specs=(P("tm", "area", None), P("tm", "area", None)),
        check_vma=False,
    )
```

profile of v0, /device:TPU:0, one launch (start us, length us, event | category | flops | bytes accessed | tf_op | source)
XLA Modules:
  0.0 194.4 jit_solution(10002892934741415470)
XLA Ops:
  0.6 0.7 fusion.56
  1.4 0.6 reduce-window.6
  2.0 0.2 slice_reduce_fusion
  2.2 0.8 fusion.55
  3.0 0.7 compare_select_fusion
  3.7 0.9 copy.134
  4.6 1.2 scatter_custom_fusion.1
  5.8 0.2 copy.135
  5.9 0.8 reshape.185
  6.7 6.3 %all-to-all-start.1 = ((f32[8,1,2688]{2,1,0:T(1,128)}), f32[8,1,2688]{2,1,0:T(1,128)S(1)}, u32[]{:S(2)}, u32[]{:S(2)}) async-start(f32[8,1,2688]{2,1,0:T(1,128)} %reshape.185), calls=%async_computation.1 | async-start | bytes 172032 | tf_op jit(solution)/shard_map/all_to_all | solution.py:111
  13.1 0.1 pad_maximum_fusion.5
  13.2 1.3 collective-permute-start.2
  14.5 2.9 %scatter_custom_fusion = f32[512,512]{1,0:T(8,128)} fusion(s32[256]{0:T(256)S(1)} %bitcast.258, f32[256,512]{1,0:T(8,128)} %param.28, f32[]{:T(128)} %constant.87.clone.1), kind=kCustom, calls=%fused_computation.44 | custom fusion | bytes 1049088 | tf_op jit(solution)/shard_map/scatter | solution.py:102
  17.5 1.8 all-to-all-done.1
  19.2 4.2 %all-to-all-start = ((f32[8,64,512]{2,1,0:T(8,128)}), f32[8,64,512]{2,1,0:T(8,128)S(1)}, u32[]{:S(2)}, u32[]{:S(2)}) async-start(f32[8,64,512]{2,1,0:T(8,128)} %bitcast.17), calls=%async_computation | async-start | bytes 2097152 | tf_op jit(solution)/shard_map/all_to_all | solution.py:110
  23.5 1.3 collective-permute-start.1
  24.8 4.5 %collective-permute-start = (f32[1,4,512]{2,1,0:T(4,128)S(1)}, f32[1,4,512]{2,1,0:T(4,128)S(1)}, u32[]{:S(2)}, u32[]{:S(2)}) collective-permute-start(f32[1,4,512]{2,1,0:T(4,128)S(1)} %get-tuple-element.64), channel_id=1, source_target_pairs={{0,8},{8,16},{16,24},{1,9},{9,17},{17,25},{2,10},{10,18},{18,26},{... | collective-permute-start | bytes 24584 | tf_op jit(solution)/shard_map/ppermute | solution.py:17
  29.7 0.1 copy.131
  29.8 0.1 copy.130
  30.5 5.7 %fusion.27 = f32[4,512,42]{1,2,0:T(8,128)} fusion(f32[4,512,512]{2,1,0:T(8,128)} %param.23, f32[42,4,512]{2,1,0:T(4,128)S(1)} %copy-done.1), kind=kOutput, calls=%fused_computation.53 | convolution fusion | flops 528482304 | bytes 4882432 | tf_op jit(solution)/shard_map/uog,ogn->uon/dot_general | solution.py:121
  36.2 0.5 broadcast.115
  36.7 0.8 reduce.8
  37.6 0.1 reshape.186
  37.7 0.1 copy.136
  37.8 0.2 fusion.18
  38.0 0.2 fusion.59
  38.2 3.2 %fusion.76 = (f32[42,4,512]{2,1,0:T(4,128)}, f32[42,4,4,512]{3,2,1,0:T(4,128)S(1)}) fusion(s32[4,4]{1,0:T(4,128)S(1)} %copy.131, f32[43,8,512]{2,1,0:T(8,128)S(1)} %fusion.18, f32[4,512]{1,0:T(4,128)S(1)} %copy-done.7, f32[42,4,512]{2,1,0:T(4,128)S(1)} %bitcast.239, f32[4,4,512]{2,1,0:T(4,128)S(1)} %fusion.59, f32[4,4]{1,0:T(4,128)S(1)} %copy.130), kind=kOutput, calls=%fused_computation.131 | convolution fusion | flops 34664576 | bytes 2797568 | tf_op jit(solution)/shard_map/skj,tjb->tskb/dot_general | solution.py:58
  41.4 1.3 fusion.10
  42.7 0.1 slice.200
  42.8 0.8 copy-done.4
  43.6 2.0 %collective-permute-start.3 = (f32[42,4,512]{2,1,0:T(4,128)S(1)}, f32[42,4,512]{2,1,0:T(4,128)S(1)}, u32[]{:S(2)}, u32[]{:S(2)}) collective-permute-start(f32[42,4,512]{2,1,0:T(4,128)S(1)} %slice.200), channel_id=1, source_target_pairs={{0,1},{1,2},{2,3},{3,4},{4,5},{5,6},{6,7},{8,9},{9,10},{10,11},{11... | collective-permute-start | bytes 1032200 | tf_op jit(solution)/shard_map/ppermute | solution.py:26
  45.6 4.5 %all-to-all-done = f32[8,64,512]{2,1,0:T(8,128)S(1)} async-done(((f32[8,64,512]{2,1,0:T(8,128)}), f32[8,64,512]{2,1,0:T(8,128)S(1)}, u32[]{:S(2)}, u32[]{:S(2)}) %all-to-all-start) | async-done | bytes 1048608 | tf_op jit(solution)/shard_map/all_to_all | solution.py:110
  50.1 1.1 fusion.17
  51.2 0.7 convolution_bitcast_fusion.8
  52.1 0.8 broadcast_multiply_fusion.1
  52.9 1.4 collective-permute-start.6
  54.4 1.3 collective-permute-start.5
  55.7 4.5 %collective-permute-start.4 = (f32[1,4,512]{2,1,0:T(4,128)S(1)}, f32[1,4,512]{2,1,0:T(4,128)S(1)}, u32[]{:S(2)}, u32[]{:S(2)}) collective-permute-start(f32[1,4,512]{2,1,0:T(4,128)S(1)} %get-tuple-element.62), channel_id=1, source_target_pairs={{0,8},{8,16},{16,24},{1,9},{9,17},{17,25},{2,10},{10,18},{18,26},{... | collective-permute-start | bytes 24584 | tf_op jit(solution)/shard_map/ppermute | solution.py:17
  60.2 2.6 %fusion.25 = f32[4,42,512]{2,1,0:T(8,128)S(1)} fusion(f32[4,512,512]{2,1,0:T(8,128)S(1)} %copy-done, f32[42,4,512]{2,1,0:T(4,128)S(1)} %get-tuple-element.57), kind=kOutput, calls=%fused_computation.50 | convolution fusion | flops 528482304 | bytes 4882432 | tf_op jit(solution)/shard_map/uog,ogn->uon/dot_general | solution.py:121
  62.9 0.2 fusion.19
  63.1 0.2 fusion.58
  63.3 2.4 %fusion.77 = (f32[42,4,512]{2,1,0:T(4,128)S(1)}, f32[42,4,4,512]{3,2,1,0:T(4,128)S(1)}) fusion(s32[4,4]{1,0:T(4,128)S(1)} %copy.131, f32[43,8,512]{2,1,0:T(8,128)S(1)} %fusion.19, f32[4,512]{1,0:T(4,128)S(1)} %copy-done.7, f32[42,4,512]{2,1,0:T(4,128)S(1)} %get-tuple-element.56, f32[4,4,512]{2,1,0:T(4,128)S(1)} %fusion.58, f32[4,4]{1,0:T(4,128)S(1)} %copy.130), kind=kOutput, calls=%fused_computation.132 | convolution fusion | flops 34664576 | bytes 2797568 | tf_op jit(solution)/shard_map/skj,tjb->tskb/dot_general | solution.py:58
  65.7 1.3 fusion.12
  67.0 0.1 slice.207
  67.1 2.5 %collective-permute-start.7 = (f32[42,4,512]{2,1,0:T(4,128)S(1)}, f32[42,4,512]{2,1,0:T(4,128)S(1)}, u32[]{:S(2)}, u32[]{:S(2)}) collective-permute-start(f32[42,4,512]{2,1,0:T(4,128)S(1)} %slice.207), channel_id=1, source_target_pairs={{0,1},{1,2},{2,3},{3,4},{4,5},{5,6},{6,7},{8,9},{9,10},{10,11},{11... | collective-permute-start | bytes 1032200 | tf_op jit(solution)/shard_map/ppermute | solution.py:26
  69.6 1.1 fusion.16
  70.7 0.7 convolution_bitcast_fusion.7
  71.5 1.5 multiply_reduce_fusion.2
  73.0 46.5 %all-reduce.1 = (f32[]{:T(128)}, f32[]{:T(128)}) all-reduce(f32[]{:T(128)} %get-tuple-element.47, f32[]{:T(128)} %get-tuple-element.46), channel_id=1, replica_groups=mesh['tm'=4,'area'=8] {'tm','area'}, use_global_device_ids=true, to_apply=%region_7.8 | all-reduce | flops 2 | bytes 16 | tf_op jit(solution)/shard_map/psum | solution.py:70
  121.1 1.3 collective-permute-start.10
  122.4 1.3 collective-permute-start.9
  123.7 4.8 %collective-permute-start.8 = (f32[1,4,512]{2,1,0:T(4,128)S(1)}, f32[1,4,512]{2,1,0:T(4,128)S(1)}, u32[]{:S(2)}, u32[]{:S(2)}) collective-permute-start(f32[1,4,512]{2,1,0:T(4,128)S(1)} %get-tuple-element.60), channel_id=1, source_target_pairs={{0,8},{8,16},{16,24},{1,9},{9,17},{17,25},{2,10},{10,18},{18,26},{... | collective-permute-start | bytes 24584 | tf_op jit(solution)/shard_map/ppermute | solution.py:17
  128.5 4.8 %fusion.23 = f32[4,42,512]{2,1,0:T(8,128)S(1)} fusion(f32[4,512,512]{2,1,0:T(8,128)} %param.23, f32[42,4,512]{2,1,0:T(4,128)S(1)} %bitcast.224), kind=kOutput, calls=%fused_computation.47 | convolution fusion | flops 528482304 | bytes 4882432 | tf_op jit(solution)/shard_map/uog,ogn->uon/dot_general | solution.py:121
  133.3 0.2 fusion.20
  133.5 0.2 fusion.57
  133.7 2.4 %fusion.78 = (f32[42,4,512]{2,1,0:T(4,128)S(1)}, f32[42,4,4,512]{3,2,1,0:T(4,128)S(1)}) fusion(s32[4,4]{1,0:T(4,128)S(1)} %copy.131, f32[43,8,512]{2,1,0:T(8,128)S(1)} %fusion.20, f32[4,512]{1,0:T(4,128)S(1)} %copy-done.7, f32[42,4,512]{2,1,0:T(4,128)S(1)} %bitcast.236, f32[4,4,512]{2,1,0:T(4,128)S(1)} %fusion.57, f32[4,4]{1,0:T(4,128)S(1)} %copy.130), kind=kOutput, calls=%fused_computation.133 | convolution fusion | flops 34664576 | bytes 2797568 | tf_op jit(solution)/shard_map/skj,tjb->tskb/dot_general | solution.py:58
  136.1 1.3 fusion.14
  137.4 0.1 slice.213
  137.5 2.8 %collective-permute-start.11 = (f32[42,4,512]{2,1,0:T(4,128)S(1)}, f32[42,4,512]{2,1,0:T(4,128)S(1)}, u32[]{:S(2)}, u32[]{:S(2)}) collective-permute-start(f32[42,4,512]{2,1,0:T(4,128)S(1)} %slice.213), channel_id=1, source_target_pairs={{0,1},{1,2},{2,3},{3,4},{4,5},{5,6},{6,7},{8,9},{9,10},{10,11},{11... | collective-permute-start | bytes 1032200 | tf_op jit(solution)/shard_map/ppermute | solution.py:26
  140.3 1.1 fusion.15
  141.4 0.7 convolution_bitcast_fusion.6
  142.2 1.6 multiply_reduce_fusion
  143.8 44.9 %all-reduce = (f32[]{:T(128)}, f32[]{:T(128)}) all-reduce(f32[]{:T(128)} %get-tuple-element.45, f32[]{:T(128)} %get-tuple-element.44), channel_id=1, replica_groups=mesh['tm'=4,'area'=8] {'tm','area'}, use_global_device_ids=true, to_apply=%region_12.13 | all-reduce | flops 2 | bytes 16 | tf_op jit(solution)/shard_map/psum | solution.py:70
  193.3 1.0 multiply_subtract_fusion
  (54 shorter events, 0.7 us)
Async XLA Ops:
  0.6 12.4 %copy-start.1 = (f32[42,4,512]{2,1,0:T(4,128)S(1)}, f32[42,4,512]{2,1,0:T(4,128)}, u32[]{:S(2)}) copy-start(f32[42,4,512]{2,1,0:T(4,128)} %param.31) | copy-start | bytes 1032196
  0.6 12.4 %copy-start.7 = (f32[4,512]{1,0:T(4,128)S(1)}, f32[4,512]{1,0:T(4,128)}, u32[]{:S(2)}) copy-start(f32[4,512]{1,0:T(4,128)} %param.25) | copy-start | bytes 24580
  6.7 12.5 %all-to-all-start.1 = ((f32[8,1,2688]{2,1,0:T(1,128)}), f32[8,1,2688]{2,1,0:T(1,128)S(1)}, u32[]{:S(2)}, u32[]{:S(2)}) async-start(f32[8,1,2688]{2,1,0:T(1,128)} %reshape.185), calls=%async_computation.1 | async-start | bytes 172032 | tf_op jit(solution)/shard_map/all_to_all | solution.py:111
  13.2 16.2 %copy-start.11 = (s32[32,4]{0,1:T(4,128)S(1)}, s32[32,4]{0,1:T(4,128)}, u32[]{:S(2)}) copy-start(s32[32,4]{0,1:T(4,128)} %param.26) | copy-start | bytes 1540
  13.2 16.3 %copy-start.12 = (f32[32,4]{0,1:T(4,128)S(1)}, f32[32,4]{0,1:T(4,128)}, u32[]{:S(2)}) copy-start(f32[32,4]{0,1:T(4,128)} %param.27) | copy-start | bytes 1540
  13.2 24.6 %collective-permute-start.2 = (f32[43,4,512]{2,1,0:T(4,128)S(1)}, f32[43,4,512]{2,1,0:T(4,128)S(1)}, u32[]{:S(2)}, u32[]{:S(2)}) collective-permute-start(f32[43,4,512]{2,1,0:T(4,128)S(1)} %pad_maximum_fusion.5), channel_id=1, source_target_pairs={{1,0},{2,1},{3,2},{4,3},{5,4},{6,5},{7,6},{9,8},{10,9},{11,10},{12... | collective-permute-start | bytes 1056776 | tf_op jit(solution)/shard_map/ppermute | solution.py:26
  19.2 30.8 %all-to-all-start = ((f32[8,64,512]{2,1,0:T(8,128)}), f32[8,64,512]{2,1,0:T(8,128)S(1)}, u32[]{:S(2)}, u32[]{:S(2)}) async-start(f32[8,64,512]{2,1,0:T(8,128)} %bitcast.17), calls=%async_computation | async-start | bytes 2097152 | tf_op jit(solution)/shard_map/all_to_all | solution.py:110
  23.5 28.5 %collective-permute-start.1 = (f32[1,4,512]{2,1,0:T(4,128)S(1)}, f32[1,4,512]{2,1,0:T(4,128)S(1)}, u32[]{:S(2)}, u32[]{:S(2)}) collective-permute-start(f32[1,4,512]{2,1,0:T(4,128)S(1)} %get-tuple-element.65), channel_id=1, source_target_pairs={{8,0},{16,8},{24,16},{9,1},{17,9},{25,17},{10,2},{18,10},{26,18},{... | collective-permute-start | bytes 24584 | tf_op jit(solution)/shard_map/ppermute | solution.py:18
  24.8 27.2 %collective-permute-start = (f32[1,4,512]{2,1,0:T(4,128)S(1)}, f32[1,4,512]{2,1,0:T(4,128)S(1)}, u32[]{:S(2)}, u32[]{:S(2)}) collective-permute-start(f32[1,4,512]{2,1,0:T(4,128)S(1)} %get-tuple-element.64), channel_id=1, source_target_pairs={{0,8},{8,16},{16,24},{1,9},{9,17},{17,25},{2,10},{10,18},{18,26},{... | collective-permute-start | bytes 24584 | tf_op jit(solution)/shard_map/ppermute | solution.py:17
  42.7 0.9 copy-start.4
  43.6 8.4 %collective-permute-start.3 = (f32[42,4,512]{2,1,0:T(4,128)S(1)}, f32[42,4,512]{2,1,0:T(4,128)S(1)}, u32[]{:S(2)}, u32[]{:S(2)}) collective-permute-start(f32[42,4,512]{2,1,0:T(4,128)S(1)} %slice.200), channel_id=1, source_target_pairs={{0,1},{1,2},{2,3},{3,4},{4,5},{5,6},{6,7},{8,9},{9,10},{10,11},{11... | collective-permute-start | bytes 1032200 | tf_op jit(solution)/shard_map/ppermute | solution.py:26
  50.1 1.9 copy-start.2
  50.1 1.9 copy-start.3
  50.1 1.9 copy-start.5
  50.1 1.9 copy-start.6
  50.1 1.9 copy-start.8
  50.1 1.9 copy-start.9
  50.1 1.9 copy-start.10
  52.0 8.2 %copy-start = (f32[4,512,512]{2,1,0:T(8,128)S(1)}, f32[4,512,512]{2,1,0:T(8,128)}, u32[]{:S(2)}) copy-start(f32[4,512,512]{2,1,0:T(8,128)} %param.23) | copy-start | bytes 12582916
  52.9 9.9 %collective-permute-start.6 = (f32[43,4,512]{2,1,0:T(4,128)S(1)}, f32[43,4,512]{2,1,0:T(4,128)S(1)}, u32[]{:S(2)}, u32[]{:S(2)}) collective-permute-start(f32[43,4,512]{2,1,0:T(4,128)S(1)} %pad_maximum_fusion.4), channel_id=1, source_target_pairs={{1,0},{2,1},{3,2},{4,3},{5,4},{6,5},{7,6},{9,8},{10,9},{11,10},{12... | collective-permute-start | bytes 1056776 | tf_op jit(solution)/shard_map/ppermute | solution.py:26
  54.4 17.1 %collective-permute-start.5 = (f32[1,4,512]{2,1,0:T(4,128)S(1)}, f32[1,4,512]{2,1,0:T(4,128)S(1)}, u32[]{:S(2)}, u32[]{:S(2)}) collective-permute-start(f32[1,4,512]{2,1,0:T(4,128)S(1)} %get-tuple-element.63), channel_id=1, source_target_pairs={{8,0},{16,8},{24,16},{9,1},{17,9},{25,17},{10,2},{18,10},{26,18},{... | collective-permute-start | bytes 24584 | tf_op jit(solution)/shard_map/ppermute | solution.py:18
  55.7 15.8 %collective-permute-start.4 = (f32[1,4,512]{2,1,0:T(4,128)S(1)}, f32[1,4,512]{2,1,0:T(4,128)S(1)}, u32[]{:S(2)}, u32[]{:S(2)}) collective-permute-start(f32[1,4,512]{2,1,0:T(4,128)S(1)} %get-tuple-element.62), channel_id=1, source_target_pairs={{0,8},{8,16},{16,24},{1,9},{9,17},{17,25},{2,10},{10,18},{18,26},{... | collective-permute-start | bytes 24584 | tf_op jit(solution)/shard_map/ppermute | solution.py:17
  67.1 4.4 %collective-permute-start.7 = (f32[42,4,512]{2,1,0:T(4,128)S(1)}, f32[42,4,512]{2,1,0:T(4,128)S(1)}, u32[]{:S(2)}, u32[]{:S(2)}) collective-permute-start(f32[42,4,512]{2,1,0:T(4,128)S(1)} %slice.207), channel_id=1, source_target_pairs={{0,1},{1,2},{2,3},{3,4},{4,5},{5,6},{6,7},{8,9},{9,10},{10,11},{11... | collective-permute-start | bytes 1032200 | tf_op jit(solution)/shard_map/ppermute | solution.py:26
  121.1 12.2 %collective-permute-start.10 = (f32[43,4,512]{2,1,0:T(4,128)S(1)}, f32[43,4,512]{2,1,0:T(4,128)S(1)}, u32[]{:S(2)}, u32[]{:S(2)}) collective-permute-start(f32[43,4,512]{2,1,0:T(4,128)S(1)} %pad_maximum_fusion.3), channel_id=1, source_target_pairs={{1,0},{2,1},{3,2},{4,3},{5,4},{6,5},{7,6},{9,8},{10,9},{11,10},{12... | collective-permute-start | bytes 1056776 | tf_op jit(solution)/shard_map/ppermute | solution.py:26
  122.4 19.8 %collective-permute-start.9 = (f32[1,4,512]{2,1,0:T(4,128)S(1)}, f32[1,4,512]{2,1,0:T(4,128)S(1)}, u32[]{:S(2)}, u32[]{:S(2)}) collective-permute-start(f32[1,4,512]{2,1,0:T(4,128)S(1)} %get-tuple-element.61), channel_id=1, source_target_pairs={{8,0},{16,8},{24,16},{9,1},{17,9},{25,17},{10,2},{18,10},{26,18},{... | collective-permute-start | bytes 24584 | tf_op jit(solution)/shard_map/ppermute | solution.py:18
  123.7 18.5 %collective-permute-start.8 = (f32[1,4,512]{2,1,0:T(4,128)S(1)}, f32[1,4,512]{2,1,0:T(4,128)S(1)}, u32[]{:S(2)}, u32[]{:S(2)}) collective-permute-start(f32[1,4,512]{2,1,0:T(4,128)S(1)} %get-tuple-element.60), channel_id=1, source_target_pairs={{0,8},{8,16},{16,24},{1,9},{9,17},{17,25},{2,10},{10,18},{18,26},{... | collective-permute-start | bytes 24584 | tf_op jit(solution)/shard_map/ppermute | solution.py:17
  137.5 4.7 %collective-permute-start.11 = (f32[42,4,512]{2,1,0:T(4,128)S(1)}, f32[42,4,512]{2,1,0:T(4,128)S(1)}, u32[]{:S(2)}, u32[]{:S(2)}) collective-permute-start(f32[42,4,512]{2,1,0:T(4,128)S(1)} %slice.213), channel_id=1, source_target_pairs={{0,1},{1,2},{2,3},{3,4},{4,5},{5,6},{6,7},{8,9},{9,10},{10,11},{11... | collective-permute-start | bytes 1032200 | tf_op jit(solution)/shard_map/ppermute | solution.py:26
where the time goes:
time: 195 us; the launch traced here: 194 us
  blocking collectives  91.5 us (47%)
  starting transfers between devices  39.6 us (20%)
  matrix products  31.2 us (16%)
  other arithmetic  9.66 us (5%)
  local copies, waits for them, and re-layouts  8.28 us (4%)
  between operations  7.89 us (4%)
  waiting for transfers between devices  6.29 us (3%)
    psum x2, blocking collectives, paired(): lax.psum((jnp.sum(residual * residual), jnp.sum(residual * applied)), ('t...  91.5 us
    ppermute x3, starting transfers between devices, extended_2(): before = lax.ppermute(last, axis, up)  13.9 us
    dot_general x3, matrix products, operate(): jnp.einsum('uog,ogn->uon', input_vector, tile, precision=lax.Precision.HI...  13.1 us
    ppermute x6, starting transfers between devices, from_behind(): lax.ppermute(value, axis, [(source, source + steps) for source in range(l...  11.3 us
    dot_general x3, matrix products, tie_terms(): jnp.einsum('skj,tjb->tskb', select, scaled_field, precision=lax.Precision...  8.04 us
    all_to_all x1, starting transfers between devices, body(): lax.all_to_all(send_weight, 'area', split_axis=0, concat_axis=0, tiled=True)  6.33 us
    all_to_all x1, waiting for transfers between devices, body(): lax.all_to_all(send_sens, 'area', split_axis=0, concat_axis=0, tiled=True)  4.47 us
    all_to_all x1, starting transfers between devices, body(): lax.all_to_all(send_sens, 'area', split_axis=0, concat_axis=0, tiled=True)  4.24 us
  transfers between devices with their start and end apart: 14, of which 2 were waited for; matrix products, arithmetic and copies ran while one was open for 19% of the time, Pallas kernels for 0%

commit v1 on v0

v1 whole, which is shorter than its diff:
```python
import functools
import jax
import jax.numpy as jnp
from jax import lax
from jax.experimental import pallas as pl
from jax.experimental.pallas import tpu as pltpu
from jax.sharding import PartitionSpec as P

TIES = 4
HOUR_LANES = 64
F32 = jnp.float32
BF16 = jnp.bfloat16
VMEM_LIMIT = 40 * 1024 * 1024

WHOLE = pl.BlockSpec(memory_space=pltpu.VMEM)
SCALARS = pl.BlockSpec(memory_space=pltpu.SMEM)


def call(kernel, out_shape, in_specs, flops, moved, scratch=()):
    many = isinstance(out_shape, (tuple, list))
    return pl.pallas_call(
        kernel,
        out_shape=out_shape,
        in_specs=in_specs,
        out_specs=jax.tree.map(lambda _: WHOLE, out_shape) if many else WHOLE,
        scratch_shapes=scratch,
        compiler_params=pltpu.CompilerParams(vmem_limit_bytes=VMEM_LIMIT),
        cost_estimate=pl.CostEstimate(flops=flops, bytes_accessed=moved, transcendentals=0),
    )


def f32_shape(*shape):
    return jax.ShapeDtypeStruct(shape, F32)


def two_parts(value):
    high = value.astype(BF16)
    return high, (value - high.astype(F32)).astype(BF16)


def three_parts(value):
    high = value.astype(BF16)
    rest = value - high.astype(F32)
    middle = rest.astype(BF16)
    return high, middle, (rest - middle.astype(F32)).astype(BF16)


def dot(left, right, contract_right=0):
    return lax.dot_general(
        left, right, (((1,), (contract_right,)), ((), ())), preferred_element_type=F32
    )


def split_dot(left, right_high, right_low, contract_right=0):
    high, low = two_parts(left)
    return (
        dot(high, right_high, contract_right)
        + dot(low, right_high, contract_right)
        + dot(high, right_low, contract_right)
    )


def pack_kernel(span, cap, index, owner, sens, weight, sens_out, weight_out):
    rows = owner.shape[0]
    groups = sens_out.shape[0] // cap
    owner_column = owner[...].astype(F32)
    wide = jnp.broadcast_to(owner_column, (rows, 128))
    owner_row = jnp.transpose(wide)[0:1, :]
    earlier = lax.broadcasted_iota(jnp.int32, (rows, rows), 0) < lax.broadcasted_iota(
        jnp.int32, (rows, rows), 1
    )
    same = jnp.where(earlier & (owner_column == owner_row), 1.0, 0.0)
    rank_row = jnp.sum(same, axis=0, keepdims=True)
    key_row = owner_row * cap + rank_row
    slots = groups * cap
    slot = lax.broadcasted_iota(jnp.int32, (slots, rows), 0)
    group, rank = slot // cap, slot % cap

    def marks(area):
        wanted = ((group * span + area) * cap + rank).astype(F32)
        return jnp.where(wanted == key_row, 1.0, 0.0).astype(BF16)

    mine = marks(index[0])
    high, middle, low = three_parts(sens[...])
    sens_out[...] = (dot(mine, high) + dot(mine, middle)) + dot(mine, low)
    hours = weight.shape[1]
    gap = jnp.zeros((rows, HOUR_LANES - hours), F32)
    blank = jnp.zeros((rows, HOUR_LANES), F32)
    left = jnp.concatenate([weight[...], gap, blank], axis=1)
    right = jnp.concatenate([blank, weight[...], gap], axis=1)
    left_parts, right_parts = three_parts(left), three_parts(right)
    for pair in range(span // 2):
        first, second = marks(2 * pair), marks(2 * pair + 1)
        total = None
        for a, b in zip(left_parts, right_parts):
            term = dot(first, a) + dot(second, b)
            total = term if total is None else total + term
        weight_out[:, pl.ds(128 * pair, 128)] = total


def take(ref, area, span):
    rows = pl.ds(area, ref.shape[1] // span, stride=span)
    return jnp.concatenate([ref[k, rows, :] for k in range(ref.shape[0])], axis=1)


def put(ref, area, span, value):
    rows = pl.ds(area, ref.shape[1] // span, stride=span)
    for k in range(ref.shape[0]):
        ref[k, rows, :] = value[:, 128 * k : 128 * (k + 1)]


def ties_from(coefficients, fields, couplings):
    total = None
    for coefficient, field, coupling in zip(coefficients, fields, couplings):
        term = coefficient * (coupling * field)
        total = term if total is None else total + term
    return total


def upper(ties, span, i, j):
    return ties[span + i, j + span - i - 1] if j <= i else 0.0


def lower(ties, span, i, j):
    return ties[j, i + span - j - 1] if j >= i else 0.0


def local_tie(ties, span, i, j):
    a, b = min(i, j), max(i, j)
    return ties[span + a, b - a - 1]


def cross_coefficients(ties, odd, span, i):
    near, far = [], []
    for j in range(span):
        up, down = upper(ties, span, i, j), lower(ties, span, i, j)
        near.append(jnp.where(odd, down, up))
        far.append(jnp.where(odd, up, down))
    return near, far


def halo_terms(ramp, before, after, target, sign):
    span = ramp.shape[0]
    blocks, rows = target.shape[:2]
    for k in range(blocks):
        weight = sign * ramp[:, 128 * k : 128 * (k + 1)]
        target[k, 0:span, :] = target[k, 0:span, :] - weight * before[k]
        target[k, rows - span : rows, :] = target[k, rows - span : rows, :] - weight * after[k]


def interior_ramp(ramp, field, target, span):
    hours = field.shape[1] // span
    for i in range(span):
        own = take(field, i, span)
        blank = jnp.zeros((1, own.shape[1]), F32)
        neighbours = jnp.concatenate([blank, own[: hours - 1]], axis=0) + jnp.concatenate(
            [own[1:], blank], axis=0
        )
        target[i] = ramp[i : i + 1, :] * neighbours


def first_kernel(
    span,
    index,
    ties,
    guess,
    right_side,
    diagonal_in,
    tile,
    ramp,
    coupling,
    near,
    far,
    near_coupling,
    far_coupling,
    before,
    after,
    partial,
    diagonal,
    tile_high,
    tile_low,
    ramped,
):
    odd = index[1] == 1
    interior_ramp(ramp, guess, ramped, span)
    for i in range(span):
        high, low = two_parts(tile[i])
        tile_high[i] = high
        tile_low[i] = low
        own = take(guess, i, span)
        own_coupling = coupling[i : i + 1, :]
        near_of, far_of = cross_coefficients(ties, odd, span, i)
        others = [j for j in range(span) if j != i]
        strength = jnp.zeros_like(own_coupling)
        pull = jnp.zeros_like(own)
        for j in others:
            w = local_tie(ties, span, i, j)
            strength = strength + w * coupling[j : j + 1, :]
            pull = pull + w * (coupling[j : j + 1, :] * take(guess, j, span))
        for j in range(span):
            strength = strength + near_of[j] * near_coupling[j : j + 1, :]
            strength = strength + far_of[j] * far_coupling[j : j + 1, :]
            pull = pull + near_of[j] * (near_coupling[j : j + 1, :] * take(near, j, span))
            pull = pull + far_of[j] * (far_coupling[j : j + 1, :] * take(far, j, span))
        folded = take(diagonal_in, i, span) + (
            2.0 * ramp[i : i + 1, :] + own_coupling * strength
        )
        put(diagonal, i, span, folded)
        image = folded * own + split_dot(own, high, low) - ramped[i] - own_coupling * pull
        put(partial, i, span, take(right_side, i, span) - image)
    halo_terms(ramp, before, after, partial, -1.0)


def security(own, high, low, weight):
    flows = split_dot(own, high, low, 1)
    return split_dot(flows * weight, high, low)


def owned_kernel(span, index, guess, partial, weights, *refs):
    pieces, (residual, high_out, low_out, weight_out) = refs[:span], refs[span:]
    hours = guess.shape[1] // span
    for pair in range(span // 2):
        turned = jnp.transpose(weights[:, pl.ds(128 * pair, 128)])
        weight_out[2 * pair] = turned[:hours]
        weight_out[2 * pair + 1] = turned[HOUR_LANES : HOUR_LANES + hours]
    for step in range(span):
        area = index[0] ^ step
        high, low = two_parts(pieces[step][...])
        high_out[step] = high
        low_out[step] = low
        term = security(take(guess, area, span), high, low, weight_out[area])
        put(residual, area, span, take(partial, area, span) - term)


def local_kernel(
    span,
    with_sums,
    index,
    ties,
    field,
    diagonal,
    ramp,
    coupling,
    tile_high,
    tile_low,
    sens_high,
    sens_low,
    weights,
    *refs,
):
    if with_sums:
        earlier, image, sums, ramped = refs
    else:
        image, ramped = refs
    interior_ramp(ramp, field, ramped, span)
    for i in range(span):
        own = take(field, i, span)
        pull = jnp.zeros_like(own)
        for j in range(span):
            if j != i:
                pull = pull + local_tie(ties, span, i, j) * (
                    coupling[j : j + 1, :] * take(field, j, span)
                )
        value = (
            take(diagonal, i, span) * own
            + split_dot(own, tile_high[i], tile_low[i])
            - ramped[i]
            - coupling[i : i + 1, :] * pull
        )
        put(image, i, span, value)
    for step in range(span):
        area = index[0] ^ step
        term = security(
            take(field, area, span), sens_high[step], sens_low[step], weights[area]
        )
        put(image, area, span, take(image, area, span) + term)
    if with_sums:
        a, b = earlier[...], field[...]
        sums[...] = lanes_of([jnp.sum(a * a), jnp.sum(a * b), jnp.sum(b * b)])


def lanes_of(values):
    lane = lax.broadcasted_iota(jnp.int32, (1, 128), 1)
    row = jnp.zeros((1, 128), F32)
    for position, value in enumerate(values):
        row = jnp.where(lane == position, value, row)
    return row


def cross_kernel(
    span,
    with_sums,
    index,
    ties,
    image,
    near,
    far,
    near_coupling,
    far_coupling,
    before,
    after,
    ramp,
    coupling,
    *refs,
):
    if with_sums:
        earlier, sums, total, spread = refs
    else:
        (total,) = refs
    odd = index[1] == 1
    near_fields = [near_coupling[j : j + 1, :] * take(near, j, span) for j in range(span)]
    far_fields = [far_coupling[j : j + 1, :] * take(far, j, span) for j in range(span)]
    for i in range(span):
        near_of, far_of = cross_coefficients(ties, odd, span, i)
        pull = near_of[0] * near_fields[0] + far_of[0] * far_fields[0]
        for j in range(1, span):
            pull = pull + near_of[j] * near_fields[j] + far_of[j] * far_fields[j]
        put(total, i, span, take(image, i, span) - coupling[i : i + 1, :] * pull)
    halo_terms(ramp, before, after, total, 1.0)
    if with_sums:
        last = jnp.sum(earlier[...] * total[...])
        lane = lax.broadcasted_iota(jnp.int32, (1, 128), 1)
        spread[...] = jnp.broadcast_to(jnp.where(lane == 3, last, sums[...]), spread.shape)


def last_kernel(gathered, guess, residual, image, second, step_out, residual_out):
    sums = jnp.sum(gathered[...], axis=0, keepdims=True)
    rr, ra, aa, ab = (sums[:, k : k + 1] for k in range(4))
    alpha = rr / ra
    rr_next = alpha * (alpha * aa - ra)
    beta = rr_next / rr
    product = ra - 2.0 * alpha * aa + alpha * alpha * ab
    alpha_next = rr_next / (product - beta * rr_next / alpha)
    one = alpha + alpha_next * (1.0 + beta)
    two = alpha_next * alpha
    hours, span, width = step_out.shape
    for k in range(width // 128):
        lanes = pl.ds(128 * k, 128)
        step = guess[k] + one * residual[k] - two * image[k]
        left = residual[k] - one * image[k] + two * second[k]
        step_out[:, :, lanes] = step.reshape(hours, span, 128)
        residual_out[:, :, lanes] = left.reshape(hours, span, 128)


def exchange(field, groups):
    far_pairs = [(i, i + 1) for i in range(1, groups - 1, 2)]
    far = lax.ppermute(field, "area", far_pairs + [(j, i) for i, j in far_pairs])
    near = lax.ppermute(field, "area", [(i, i ^ 1) for i in range(groups)])
    return near, far


def hour_halo(field, span):
    count = lax.axis_size("tm")
    rows = field.shape[1]
    up = [(i, i + 1) for i in range(count - 1)]
    before = lax.ppermute(field[:, rows - span :], "tm", up)
    after = lax.ppermute(field[:, :span], "tm", [(j, i) for i, j in up])
    return before, after


def body(
    gradient,
    barrier,
    slack,
    hess_diag,
    tile,
    ramp_weight,
    bus_coupling,
    tie_offset,
    tie_admittance,
    con_sens,
    con_weight,
    con_owner,
    step_guess,
):
    hours, span, width = gradient.shape
    total_areas = tie_offset.shape[0]
    groups, members = lax.axis_size("area"), lax.axis_size("tm")
    assert members == span and members & (members - 1) == 0 and hours <= HOUR_LANES
    rows_held = con_sens.shape[0]
    cap = max(2, (2 * rows_held + total_areas - 1) // total_areas)
    slots = groups * cap
    rows = hours * span
    member, group = lax.axis_index("tm"), lax.axis_index("area")
    index = jnp.stack([member, group % 2]).astype(jnp.int32)

    sens_send, weight_send = call(
        functools.partial(pack_kernel, span, cap),
        (f32_shape(slots, width), f32_shape(slots, span * HOUR_LANES)),
        [SCALARS, WHOLE, WHOLE, WHOLE],
        6 * slots * rows_held * width,
        4 * rows_held * width * 2,
    )(index, con_owner, con_sens, con_weight)
    piece = lax.all_to_all(
        sens_send.reshape(groups, cap, width), "area", split_axis=0, concat_axis=0, tiled=True
    )
    weights = lax.all_to_all(
        weight_send.reshape(groups, cap, span * HOUR_LANES),
        "area",
        split_axis=0,
        concat_axis=0,
        tiled=True,
    ).reshape(slots, span * HOUR_LANES)
    piece = piece.reshape(slots, width)
    pieces = [piece] + [
        lax.ppermute(piece, "tm", [(i, i ^ step) for i in range(members)])
        for step in range(1, members)
    ]

    padded = (jnp.pad(tie_offset, ((span, 0), (0, 0))), jnp.pad(tie_admittance, ((span, 0), (0, 0))))
    offsets, gains = (
        lax.dynamic_slice(a, (group * span, jnp.int32(0)), (2 * span, TIES)) for a in padded
    )
    steps_up = jnp.arange(1, span + 1, dtype=jnp.int32)
    ties = jnp.sum(
        jnp.where(offsets[:, :, None] == steps_up[None, None, :], gains[:, :, None], 0.0), axis=1
    )

    def blocked(value):
        return jnp.swapaxes(value.reshape(rows, width // 128, 128), 0, 1)

    guess = blocked(step_guess)
    diagonal_in = blocked(hess_diag + barrier[0] / (slack * slack))
    right_side = blocked(barrier[0] / slack - gradient)
    near_guess, far_guess = exchange(guess, groups)
    near_coupling, far_coupling = exchange(bus_coupling, groups)
    before, after = hour_halo(guess, span)
    ramped = [pltpu.VMEM((span, hours, width), F32)]
    field_shape = f32_shape(width // 128, rows, 128)
    tile_shape = jax.ShapeDtypeStruct(tile.shape, BF16)
    tile_flops = 6 * rows * width * width
    partial, diagonal, tile_high, tile_low = call(
        functools.partial(first_kernel, span),
        (field_shape, field_shape, tile_shape, tile_shape),
        [SCALARS, SCALARS] + [WHOLE] * 12,
        tile_flops,
        8 * span * width * width,
        ramped,
    )(
        index,
        ties,
        guess,
        right_side,
        diagonal_in,
        tile,
        ramp_weight,
        bus_coupling,
        near_guess,
        far_guess,
        near_coupling,
        far_coupling,
        before,
        after,
    )

    sens_shape = jax.ShapeDtypeStruct((span, slots, width), BF16)
    residual, sens_high, sens_low, owned_weight = call(
        functools.partial(owned_kernel, span),
        (field_shape, sens_shape, sens_shape, f32_shape(span, hours, slots)),
        [SCALARS] + [WHOLE] * (3 + span),
        12 * rows * slots * width,
        6 * span * slots * width,
    )(index, guess, partial, weights, *pieces)

    def apply(field, earlier=None):
        near, far = exchange(field, groups)
        before, after = hour_halo(field, span)
        summed = earlier is not None
        image = call(
            functools.partial(local_kernel, span, summed),
            (field_shape, f32_shape(1, 128)) if summed else field_shape,
            [SCALARS, SCALARS] + [WHOLE] * (9 + summed),
            tile_flops + 12 * rows * slots * width,
            4 * span * width * width,
            ramped,
        )(
            index,
            ties,
            field,
            diagonal,
            ramp_weight,
            bus_coupling,
            tile_high,
            tile_low,
            sens_high,
            sens_low,
            owned_weight,
            *([earlier] if summed else []),
        )
        more = ()
        if summed:
            image, sums = image
            more = (field, sums)
        return call(
            functools.partial(cross_kernel, span, summed),
            (field_shape, f32_shape(groups * members, 128)) if summed else field_shape,
            [SCALARS, SCALARS] + [WHOLE] * (9 + len(more)),
            64 * rows * width,
            16 * rows * width,
        )(
            index,
            ties,
            image,
            near,
            far,
            near_coupling,
            far_coupling,
            before,
            after,
            ramp_weight,
            bus_coupling,
            *more,
        )

    image = apply(residual)
    second, spread = apply(image, residual)
    gathered = lax.all_to_all(spread, ("tm", "area"), split_axis=0, concat_axis=0, tiled=True)
    out_shape = f32_shape(hours, span, width)
    return call(
        last_kernel,
        (out_shape, out_shape),
        [WHOLE] * 5,
        8 * rows * width,
        24 * rows * width,
    )(gathered, guess, residual, image, second)


def solution(mesh):
    field = P("tm", "area", None)
    placed = (
        field,
        P(),
        field,
        field,
        P("area", None, None),
        P("area", None),
        P("area", None),
        P(),
        P(),
        P("area", None),
        P("area", "tm"),
        P("area", None),
        field,
    )
    return jax.shard_map(
        body, mesh=mesh, in_specs=placed, out_specs=(field, field), check_vma=False
    )
```

time: 195 us -> 95.6 us (0.49)
  blocking collectives: 91.5 us -> 11.1 us
  matrix products: 31.2 us -> 0 us
  Pallas kernels: 0 us -> 17.8 us
  other arithmetic: 9.66 us -> 1.27 us
  local copies, waits for them, and re-layouts: 8.28 us -> 15.3 us
  starting transfers between devices: 39.6 us -> 46.1 us
  between operations: 7.89 us -> 1.7 us
  waiting for transfers between devices: 6.29 us -> 1.33 us
    psum x2 -> x0, blocking collectives: 91.5 us -> none  [paired(): lax.psum((jnp.sum(residual * residual), jnp.sum(residual * applied)), ('t...]
    dot_general x18 -> x0, matrix products: 31.2 us -> none  [the longest x3 13.1 us: operate(): jnp.einsum('uog,ogn->uon', input_vector, tile, precision=lax.Precision.HI...]
    pallas_call x0 -> x8, Pallas kernels: none -> 17.8 us  [the longest x2 6.96 us: apply(): call(functools.partial(local_kernel, span, summed), (field_shape, f32_sha...]
    all_to_all x0 -> x1, blocking collectives: none -> 11.1 us  [body(): lax.all_to_all(spread, ('tm', 'area'), split_axis=0, concat_axis=0, tiled...]
    unnamed x31 -> x46, local copies, waits for them, and re-layouts: 2.63 us -> 13.4 us
    ppermute x12 -> x17, starting transfers between devices: 29.1 us -> 38.9 us  [the longest x3 14.5 us: hour_halo(): before = lax.ppermute(field[:, rows - span:], 'tm', up)]
    all_to_all x2, waiting for transfers between devices: 6.26 us -> 1.28 us  [the longest x1 1.28 us: body(): lax.all_to_all(sens_send.reshape(groups, cap, width), 'area', split_axis=...]
    scatter x2 -> x0, local copies, waits for them, and re-layouts: 4.14 us -> none  [the longest x1 2.93 us: body(): jnp.zeros((area_total * capacity, var_width), jnp.float32).at[slot_index]]
  transfers between devices with their start and end apart: 14 -> 19, of which waited for: 2 -> 1; matrix products, arithmetic and copies ran while one was open for 19% -> 5% of each run, Pallas kernels for 0% -> 12%
where the time goes in v1:
time: 95.6 us; the launch traced here: 94.6 us
  starting transfers between devices  46.1 us (48%)
  Pallas kernels  17.8 us (19%)
  local copies, waits for them, and re-layouts  15.3 us (16%)
  blocking collectives  11.1 us (12%)
  between operations  1.7 us (2%)
  waiting for transfers between devices  1.33 us (1%)
  other arithmetic  1.27 us (1%)
    ppermute x3, starting transfers between devices, hour_halo(): before = lax.ppermute(field[:, rows - span:], 'tm', up)  14.5 us
    ppermute x4, starting transfers between devices, exchange(): near = lax.ppermute(field, 'area', [(i, i ^ 1) for i in range(groups)])  13.7 us
    unnamed x46, local copies, waits for them, and re-layouts  13.4 us
    all_to_all x1, blocking collectives, body(): lax.all_to_all(spread, ('tm', 'area'), split_axis=0, concat_axis=0, tiled...  11.1 us
    pallas_call x2, Pallas kernels, apply(): call(functools.partial(local_kernel, span, summed), (field_shape, f32_sha...  6.96 us
    ppermute x3, starting transfers between devices, body(): lax.ppermute(piece, 'tm', [(i, i ^ step) for i in range(members)])  3.92 us
    ppermute x3, starting transfers between devices, hour_halo(): after = lax.ppermute(field[:, :span], 'tm', [(j, i) for i, j in up])  3.85 us
    all_to_all x1, starting transfers between devices, body(): lax.all_to_all(weight_send.reshape(groups, cap, span * HOUR_LANES), 'area...  3.79 us
  transfers between devices with their start and end apart: 19, of which 1 were waited for; matrix products, arithmetic and copies ran while one was open for 5% of the time, Pallas kernels for 12%

profile of v1, /device:TPU:0, one launch (start us, length us, event | category | flops | bytes accessed | tf_op | source)
XLA Modules:
  0.0 94.6 jit_solution(13339857572874822422)
XLA Ops:
  0.7 0.8 collective-permute-start.3
  1.5 4.5 %collective-permute-start.2 = (f32[4,512]{1,0:T(4,128)}, f32[4,512]{1,0:T(4,128)S(1)}, u32[]{:S(2)}, u32[]{:S(2)}) collective-permute-start(f32[4,512]{1,0:T(4,128)} %coupling.9), channel_id=1, source_target_pairs={{0,1},{1,0},{2,3},{3,2},{4,5},{5,4},{6,7},{7,6},{8,9},{9,8},{10,11... | collective-permute-start | bytes 24584 | tf_op jit(solution)/shard_map/ppermute | solution.py:348
  5.9 1.2 %reshape.33 = f32[168,4,128]{2,1,0:T(4,128)S(1)} reshape(f32[42,4,512]{2,1,0:T(4,128)} %param.25) | data formatting | bytes 688128 | tf_op jit(solution)/shard_map/reshape | solution.py:420
  7.1 0.7 collective-permute-start.1
  7.8 3.0 %collective-permute-start = (f32[4,168,128]{2,1,0:T(8,128)S(1)}, f32[4,168,128]{2,1,0:T(8,128)S(1)}, u32[]{:S(2)}, u32[]{:S(2)}) collective-permute-start(f32[4,168,128]{2,1,0:T(8,128)S(1)} %bitcast.25), channel_id=1, source_target_pairs={{0,1},{1,0},{2,3},{3,2},{4,5},{5,4},{6,7},{7,6},{8,9},{9,8},{10,11... | collective-permute-start | bytes 1032200 | tf_op jit(solution)/shard_map/ppermute | solution.py:348
  10.8 0.9 copy.39.weight
  11.7 0.8 copy.38.owner
  12.5 0.1 pad_add_fusion.index
  12.6 1.0 %copy-done.4 = f32[256,512]{1,0:T(8,128)S(1)} copy-done((f32[256,512]{1,0:T(8,128)S(1)}, f32[256,512]{1,0:T(8,128)}, u32[]{:S(2)}) %copy-start.4) | copy-done | bytes 524312
  13.7 1.9 %shard_map.141 = (f32[128,512]{1,0:T(8,128)}, f32[128,256]{1,0:T(8,128)}) custom-call(s32[2]{0:T(128)S(1)} %pad_add_fusion.index, s32[256,1]{1,0:T(8,128)S(1)} %copy.38.owner, f32[256,512]{1,0:T(8,128)S(1)} %copy-done.4, f32[256,42]{1,0:T(8,128)S(1)} %copy.39.weight), custom_call_target="tpu_custom_call" | custom-call | flops 100663296 | bytes 1048576 | tf_op jit(solution)/shard_map/pallas_call | solution.py:387
  15.6 3.4 %all-to-all-start.1 = ((f32[8,16,512]{2,1,0:T(8,128)}), f32[8,16,512]{2,1,0:T(8,128)S(1)}, u32[]{:S(2)}, u32[]{:S(2)}) async-start(f32[8,16,512]{2,1,0:T(8,128)} %bitcast.8), calls=%async_computation.1 | async-start | bytes 524288 | tf_op jit(solution)/shard_map/all_to_all | solution.py:394
  19.0 1.3 %collective-permute-start.5 = (f32[4,4,128]{2,1,0:T(4,128)S(1)}, f32[4,4,128]{2,1,0:T(4,128)S(1)}, u32[]{:S(2)}, u32[]{:S(2)}) collective-permute-start(f32[4,4,128]{2,1,0:T(4,128)S(1)} %get-tuple-element.34), channel_id=1, source_target_pairs={{8,0},{16,8},{24,16},{9,1},{17,9},{25,17},{10,2},{18,10},{26,18},{... | collective-permute-start | bytes 24584 | tf_op jit(solution)/shard_map/ppermute | solution.py:357
  20.9 0.1 pad_dynamic-slice_fusion.1
  21.0 0.1 pad_dynamic-slice_fusion
  21.1 1.1 %divide_add_fusion = (f32[21,8,512]{2,1,0:T(8,128)S(1)}, f32[21,8,512]{2,1,0:T(8,128)S(1)}) fusion(f32[21,8,512]{2,1,0:T(8,128)S(1)} %bitcast.39, f32[21,8,512]{2,1,0:T(8,128)S(1)} %bitcast.40, f32[]{:T(128)} %bitcast.23, f32[21,8,512]{2,1,0:T(8,128)} %bitcast.41), kind=kLoop, calls=%fused_computation | loop fusion | flops 430080 | bytes 1720324 | tf_op jit(solution)/shard_map/add | solution.py:423
  22.2 0.0 collective-permute-done.3.far_coupling
  22.3 4.5 %collective-permute-start.4 = (f32[4,4,128]{2,1,0:T(4,128)S(1)}, f32[4,4,128]{2,1,0:T(4,128)S(1)}, u32[]{:S(2)}, u32[]{:S(2)}) collective-permute-start(f32[4,4,128]{2,1,0:T(4,128)S(1)} %get-tuple-element.35), channel_id=1, source_target_pairs={{0,8},{8,16},{16,24},{1,9},{9,17},{17,25},{2,10},{10,18},{18,26},{... | collective-permute-start | bytes 24584 | tf_op jit(solution)/shard_map/ppermute | solution.py:356
  26.8 0.1 select_reduce_fusion
  26.9 0.1 copy.43.ties
  27.0 0.2 reshape.34
  27.2 0.2 reshape.35
  27.4 1.3 %all-to-all-done.1 = f32[8,16,512]{2,1,0:T(8,128)S(1)} async-done(((f32[8,16,512]{2,1,0:T(8,128)}), f32[8,16,512]{2,1,0:T(8,128)S(1)}, u32[]{:S(2)}, u32[]{:S(2)}) %all-to-all-start.1) | async-done | bytes 262176 | tf_op jit(solution)/shard_map/all_to_all | solution.py:394
  28.7 3.8 %all-to-all-start = ((f32[8,16,256]{2,1,0:T(8,128)}), f32[8,16,256]{2,1,0:T(8,128)S(1)}, u32[]{:S(2)}, u32[]{:S(2)}) async-start(f32[8,16,256]{2,1,0:T(8,128)} %bitcast.6), calls=%async_computation | async-start | bytes 262144 | tf_op jit(solution)/shard_map/all_to_all | solution.py:397
  32.5 0.0 collective-permute-done.2.near_coupling
  32.5 2.1 %collective-permute-start.8 = (f32[128,512]{1,0:T(8,128)S(1)}, f32[128,512]{1,0:T(8,128)}, u32[]{:S(2)}, u32[]{:S(2)}) collective-permute-start(f32[128,512]{1,0:T(8,128)S(1)} %bitcast.30), channel_id=1, source_target_pairs={{0,24},{8,16},{16,8},{24,0},{1,25},{9,17},{17,9},{25,1},{2,26},{10... | collective-permute-start | bytes 786440 | tf_op jit(solution)/shard_map/ppermute | solution.py:406
  34.6 0.0 collective-permute-done.5.after
  34.6 1.8 %collective-permute-start.7 = (f32[128,512]{1,0:T(8,128)S(1)}, f32[128,512]{1,0:T(8,128)}, u32[]{:S(2)}, u32[]{:S(2)}) collective-permute-start(f32[128,512]{1,0:T(8,128)S(1)} %bitcast.31), channel_id=1, source_target_pairs={{0,16},{8,24},{16,0},{24,8},{1,17},{9,25},{17,1},{25,9},{2,18},{10... | collective-permute-start | bytes 786440 | tf_op jit(solution)/shard_map/ppermute | solution.py:406
  36.4 0.0 collective-permute-done.4.before
  36.4 0.0 collective-permute-start.6
  36.5 0.0 copy-start.5
  36.5 0.7 copy-done.5
  37.2 0.7 copy-done.7
  38.0 0.0 copy-start.3
  38.0 2.2 %copy-done.3 = f32[4,512,512]{2,1,0:T(8,128)S(1)} copy-done((f32[4,512,512]{2,1,0:T(8,128)S(1)}, f32[4,512,512]{2,1,0:T(8,128)}, u32[]{:S(2)}) %copy-start.3) | copy-done | bytes 4194328
  40.2 1.0 %copy-done.6 = f32[4,168,128]{2,1,0:T(8,128)S(1)} copy-done((f32[4,168,128]{2,1,0:T(8,128)S(1)}, f32[4,168,128]{2,1,0:T(8,128)}, u32[]{:S(2)}) %copy-start.6) | copy-done | bytes 344088
  41.1 1.0 %copy-done.8 = f32[4,168,128]{2,1,0:T(8,128)S(1)} copy-done((f32[4,168,128]{2,1,0:T(8,128)S(1)}, f32[4,168,128]{2,1,0:T(8,128)}, u32[]{:S(2)}) %copy-start.8) | copy-done | bytes 344088
  42.1 0.7 copy-done.12
  42.8 0.7 copy-done.15
  43.5 0.7 copy-done.17
  44.2 2.6 %shard_map.140 = (f32[4,168,128]{2,1,0:T(8,128)S(1)}, f32[4,168,128]{2,1,0:T(8,128)S(1)}, bf16[4,512,512]{2,1,0:T(8,128)(2,1)S(1)}, bf16[4,512,512]{2,1,0:T(8,128)(2,1)S(1)}) custom-call(s32[2]{0:T(128)S(1)} %pad_add_fusion.index, f32[8,4]{1,0:T(8,128)S(1)} %copy.43.ties, f32[4,168,128]{2,1,0:T(8,128)S(1)} %bitcast.27, ...), custom_call_target="tpu_custom_call" | custom-call | flops 264241152 | bytes 8388608 | tf_op jit(solution)/shard_map/pallas_call | solution.py:432
  46.8 1.3 %copy-done = bf16[4,512,512]{2,1,0:T(8,128)(2,1)} copy-done((bf16[4,512,512]{2,1,0:T(8,128)(2,1)}, bf16[4,512,512]{2,1,0:T(8,128)(2,1)S(1)}, u32[]{:S(2)}) %copy-start) | copy-done | bytes 2097176
  48.1 0.0 all-to-all-done
  48.1 0.0 collective-permute-done.6.refs_1_
  48.2 2.9 %shard_map.142 = (f32[4,168,128]{2,1,0:T(8,128)S(1)}, bf16[4,128,512]{2,1,0:T(8,128)(2,1)S(1)}, bf16[4,128,512]{2,1,0:T(8,128)(2,1)S(1)}, f32[4,42,128]{2,1,0:T(8,128)S(1)}) custom-call(s32[2]{0:T(128)S(1)} %pad_add_fusion.index, f32[4,168,128]{2,1,0:T(8,128)S(1)} %bitcast.28, f32[4,168,128]{2,1,0:T(8,128)S(1)} %get-tuple-element.16.partial, ...), custom_call_target="tpu_custom_call" | custom-call | flops 132120576 | bytes 1572864 | tf_op jit(solution)/shard_map/pallas_call | solution.py:457
  51.0 0.7 collective-permute-start.10
  51.7 3.4 %collective-permute-start.9 = (f32[4,168,128]{2,1,0:T(8,128)S(1)}, f32[4,168,128]{2,1,0:T(8,128)S(1)}, u32[]{:S(2)}, u32[]{:S(2)}) collective-permute-start(f32[4,168,128]{2,1,0:T(8,128)S(1)} %get-tuple-element.19.field.refs_0_.residual), channel_id=1, source_target_pairs={{0,1},{1,0},{2,3},{3,2},{4,5},{5,4},{6,7},{7,6},{8,9},{9,8},{10,11... | collective-permute-start | bytes 1032200 | tf_op jit(solution)/shard_map/ppermute | solution.py:348
  55.2 1.3 %collective-permute-start.12 = (f32[4,4,128]{2,1,0:T(4,128)S(1)}, f32[4,4,128]{2,1,0:T(4,128)S(1)}, u32[]{:S(2)}, u32[]{:S(2)}) collective-permute-start(f32[4,4,128]{2,1,0:T(4,128)S(1)} %get-tuple-element.32), channel_id=1, source_target_pairs={{8,0},{16,8},{24,16},{9,1},{17,9},{25,17},{10,2},{18,10},{26,18},{... | collective-permute-start | bytes 24584 | tf_op jit(solution)/shard_map/ppermute | solution.py:357
  56.5 4.5 %collective-permute-start.11 = (f32[4,4,128]{2,1,0:T(4,128)S(1)}, f32[4,4,128]{2,1,0:T(4,128)S(1)}, u32[]{:S(2)}, u32[]{:S(2)}) collective-permute-start(f32[4,4,128]{2,1,0:T(4,128)S(1)} %get-tuple-element.33), channel_id=1, source_target_pairs={{0,8},{8,16},{16,24},{1,9},{9,17},{17,25},{2,10},{10,18},{18,26},{... | collective-permute-start | bytes 24584 | tf_op jit(solution)/shard_map/ppermute | solution.py:356
  61.0 1.6 %copy-done.1 = bf16[4,512,512]{2,1,0:T(8,128)(2,1)S(1)} copy-done((bf16[4,512,512]{2,1,0:T(8,128)(2,1)S(1)}, bf16[4,512,512]{2,1,0:T(8,128)(2,1)}, u32[]{:S(2)}) %copy-start.1) | copy-done | bytes 2097176
  62.6 3.5 %shard_map.143.image = f32[4,168,128]{2,1,0:T(8,128)S(1)} custom-call(s32[2]{0:T(128)S(1)} %pad_add_fusion.index, f32[8,4]{1,0:T(8,128)S(1)} %copy.43.ties, f32[4,168,128]{2,1,0:T(8,128)S(1)} %get-tuple-element.19.field.refs_0_.residual, f32[4,168,128]{2,1,0:T(8,128)S(1)} %get-tuple-element.20.diagonal, f32[4,512]{1,0:T(4,128)S(1)} %copy-done.9, ...), custom_call_target="tpu_custom_call" | custom-call | flops 396361728 | bytes 4194304 | tf_op jit(solution)/shard_map/pallas_call | solution.py:469
  66.1 0.0 collective-permute-done.12.after
  66.1 0.0 collective-permute-done.10.far
  66.1 0.0 collective-permute-done.9.near
  66.1 0.9 shard_map.144.field.refs_0_.image
  67.1 0.7 collective-permute-start.14
  67.8 2.9 %collective-permute-start.13 = (f32[4,168,128]{2,1,0:T(8,128)S(1)}, f32[4,168,128]{2,1,0:T(8,128)S(1)}, u32[]{:S(2)}, u32[]{:S(2)}) collective-permute-start(f32[4,168,128]{2,1,0:T(8,128)S(1)} %shard_map.144.field.refs_0_.image), channel_id=1, source_target_pairs={{0,1},{1,0},{2,3},{3,2},{4,5},{5,4},{6,7},{7,6},{8,9},{9,8},{10,11... | collective-permute-start | bytes 1032200 | tf_op jit(solution)/shard_map/ppermute | solution.py:348
  70.7 1.3 %collective-permute-start.16 = (f32[4,4,128]{2,1,0:T(4,128)S(1)}, f32[4,4,128]{2,1,0:T(4,128)S(1)}, u32[]{:S(2)}, u32[]{:S(2)}) collective-permute-start(f32[4,4,128]{2,1,0:T(4,128)S(1)} %get-tuple-element.30), channel_id=1, source_target_pairs={{8,0},{16,8},{24,16},{9,1},{17,9},{25,17},{10,2},{18,10},{26,18},{... | collective-permute-start | bytes 24584 | tf_op jit(solution)/shard_map/ppermute | solution.py:357
  71.9 5.4 %collective-permute-start.15 = (f32[4,4,128]{2,1,0:T(4,128)S(1)}, f32[4,4,128]{2,1,0:T(4,128)S(1)}, u32[]{:S(2)}, u32[]{:S(2)}) collective-permute-start(f32[4,4,128]{2,1,0:T(4,128)S(1)} %get-tuple-element.31), channel_id=1, source_target_pairs={{0,8},{8,16},{16,24},{1,9},{9,17},{17,25},{2,10},{10,18},{18,26},{... | collective-permute-start | bytes 24584 | tf_op jit(solution)/shard_map/ppermute | solution.py:356
  77.4 3.5 %shard_map.145 = (f32[4,168,128]{2,1,0:T(8,128)S(1)}, f32[1,128]{1,0:T(1,128)S(1)}) custom-call(s32[2]{0:T(128)S(1)} %pad_add_fusion.index, f32[8,4]{1,0:T(8,128)S(1)} %copy.43.ties, f32[4,168,128]{2,1,0:T(8,128)S(1)} %shard_map.144.field.refs_0_.image, f32[4,168,128]{2,1,0:T(8,128)S(1)} %get-tuple-element.20.diagonal, f32[4,512]{1,0:T(4,128)S(1)} %copy-done.9, ...), custom_call_target="tpu_custom_call" | custom-call | flops 396361728 | bytes 4194304 | tf_op jit(solution)/shard_map/pallas_call | solution.py:469
  80.9 0.0 collective-permute-done.15.before
  80.9 0.0 collective-permute-done.14.far
  80.9 1.2 %shard_map.146 = (f32[4,168,128]{2,1,0:T(8,128)S(1)}, f32[32,128]{1,0:T(8,128)S(1)}) custom-call(s32[2]{0:T(128)S(1)} %pad_add_fusion.index, f32[8,4]{1,0:T(8,128)S(1)} %copy.43.ties, f32[4,168,128]{2,1,0:T(8,128)S(1)} %get-tuple-element.26.image, f32[4,168,128]{2,1,0:T(8,128)S(1)} %collective-permute-done.13.near, ...), custom_call_target="tpu_custom_call" | custom-call | flops 5505024 | bytes 1376256 | tf_op jit(solution)/shard_map/pallas_call | solution.py:494
  82.1 11.1 %all_to_all.21 = f32[32,1,128]{2,1,0:T(1,128)S(1)} all-to-all(f32[32,1,128]{2,1,0:T(1,128)S(1)} %bitcast.36), channel_id=1, replica_groups=mesh['tm'=4,'area'=8] {'tm','area'}, dimensions={0} | all-to-all | bytes 32768 | tf_op jit(solution)/shard_map/all_to_all | solution.py:517
  93.2 1.4 %shard_map.147 = (f32[42,4,512]{2,1,0:T(4,128)}, f32[42,4,512]{2,1,0:T(4,128)}) custom-call(f32[32,128]{1,0:T(8,128)S(1)} %bitcast.35, f32[4,168,128]{2,1,0:T(8,128)S(1)} %bitcast.29, f32[4,168,128]{2,1,0:T(8,128)S(1)} %get-tuple-element.19.field.refs_0_.residual, f32[4,168,128]{2,1,0:T(8,128)S(1)} %shard_map.144.field.refs_0_.image, ...), custom_call_target="tpu_custom_call" | custom-call | flops 688128 | bytes 2064384 | tf_op jit(solution)/shard_map/pallas_call | solution.py:519
  (44 shorter events, 0.2 us)
Async XLA Ops:
  0.6 20.3 %copy-start.20 = (s32[32,4]{0,1:T(4,128)S(1)}, s32[32,4]{0,1:T(4,128)}, u32[]{:S(2)}) copy-start(s32[32,4]{0,1:T(4,128)} %param.20) | copy-start | bytes 1540
  0.6 20.4 %copy-start.21 = (f32[32,4]{0,1:T(4,128)S(1)}, f32[32,4]{0,1:T(4,128)}, u32[]{:S(2)}) copy-start(f32[32,4]{0,1:T(4,128)} %param.21) | copy-start | bytes 1540
  0.7 20.5 %copy-start.18 = (f32[42,4,512]{2,1,0:T(4,128)S(1)}, f32[42,4,512]{2,1,0:T(4,128)}, u32[]{:S(2)}) copy-start(f32[42,4,512]{2,1,0:T(4,128)} %param.16) | copy-start | bytes 1032196
  0.7 20.5 %copy-start.19 = (f32[42,4,512]{2,1,0:T(4,128)S(1)}, f32[42,4,512]{2,1,0:T(4,128)}, u32[]{:S(2)}) copy-start(f32[42,4,512]{2,1,0:T(4,128)} %param.15) | copy-start | bytes 1032196
  0.7 21.6 %collective-permute-start.3 = (f32[4,512]{1,0:T(4,128)}, f32[4,512]{1,0:T(4,128)S(1)}, u32[]{:S(2)}, u32[]{:S(2)}) collective-permute-start(f32[4,512]{1,0:T(4,128)} %coupling.9), channel_id=1, source_target_pairs={{1,2},{3,4},{5,6},{2,1},{4,3},{6,5},{9,10},{11,12},{13,14},{10,9},... | collective-permute-start | bytes 24584 | tf_op jit(solution)/shard_map/ppermute | solution.py:347
  1.5 31.0 %collective-permute-start.2 = (f32[4,512]{1,0:T(4,128)}, f32[4,512]{1,0:T(4,128)S(1)}, u32[]{:S(2)}, u32[]{:S(2)}) collective-permute-start(f32[4,512]{1,0:T(4,128)} %coupling.9), channel_id=1, source_target_pairs={{0,1},{1,0},{2,3},{3,2},{4,5},{5,4},{6,7},{7,6},{8,9},{9,8},{10,11... | collective-permute-start | bytes 24584 | tf_op jit(solution)/shard_map/ppermute | solution.py:348
  7.1 29.3 %collective-permute-start.1 = (f32[4,168,128]{2,1,0:T(8,128)S(1)}, f32[4,168,128]{2,1,0:T(8,128)S(1)}, u32[]{:S(2)}, u32[]{:S(2)}) collective-permute-start(f32[4,168,128]{2,1,0:T(8,128)S(1)} %bitcast.24), channel_id=1, source_target_pairs={{1,2},{3,4},{5,6},{2,1},{4,3},{6,5},{9,10},{11,12},{13,14},{10,9},... | collective-permute-start | bytes 1032200 | tf_op jit(solution)/shard_map/ppermute | solution.py:347
  7.8 29.4 %collective-permute-start = (f32[4,168,128]{2,1,0:T(8,128)S(1)}, f32[4,168,128]{2,1,0:T(8,128)S(1)}, u32[]{:S(2)}, u32[]{:S(2)}) collective-permute-start(f32[4,168,128]{2,1,0:T(8,128)S(1)} %bitcast.25), channel_id=1, source_target_pairs={{0,1},{1,0},{2,3},{3,2},{4,5},{5,4},{6,7},{7,6},{8,9},{9,8},{10,11... | collective-permute-start | bytes 1032200 | tf_op jit(solution)/shard_map/ppermute | solution.py:348
  12.6 1.0 %copy-start.4 = (f32[256,512]{1,0:T(8,128)S(1)}, f32[256,512]{1,0:T(8,128)}, u32[]{:S(2)}) copy-start(f32[256,512]{1,0:T(8,128)} %sens.1) | copy-start | bytes 1572868
  15.6 13.1 %all-to-all-start.1 = ((f32[8,16,512]{2,1,0:T(8,128)}), f32[8,16,512]{2,1,0:T(8,128)S(1)}, u32[]{:S(2)}, u32[]{:S(2)}) async-start(f32[8,16,512]{2,1,0:T(8,128)} %bitcast.8), calls=%async_computation.1 | async-start | bytes 524288 | tf_op jit(solution)/shard_map/all_to_all | solution.py:394
  19.0 15.6 %collective-permute-start.5 = (f32[4,4,128]{2,1,0:T(4,128)S(1)}, f32[4,4,128]{2,1,0:T(4,128)S(1)}, u32[]{:S(2)}, u32[]{:S(2)}) collective-permute-start(f32[4,4,128]{2,1,0:T(4,128)S(1)} %get-tuple-element.34), channel_id=1, source_target_pairs={{8,0},{16,8},{24,16},{9,1},{17,9},{25,17},{10,2},{18,10},{26,18},{... | collective-permute-start | bytes 24584 | tf_op jit(solution)/shard_map/ppermute | solution.py:357
  21.1 16.8 %copy-start.9 = (f32[4,512]{1,0:T(4,128)S(1)}, f32[4,512]{1,0:T(4,128)}, u32[]{:S(2)}) copy-start(f32[4,512]{1,0:T(4,128)} %ramp.9) | copy-start | bytes 24580
  21.1 16.8 %copy-start.10 = (f32[4,512]{1,0:T(4,128)S(1)}, f32[4,512]{1,0:T(4,128)}, u32[]{:S(2)}) copy-start(f32[4,512]{1,0:T(4,128)} %coupling.9) | copy-start | bytes 24580
  22.3 14.1 %collective-permute-start.4 = (f32[4,4,128]{2,1,0:T(4,128)S(1)}, f32[4,4,128]{2,1,0:T(4,128)S(1)}, u32[]{:S(2)}, u32[]{:S(2)}) collective-permute-start(f32[4,4,128]{2,1,0:T(4,128)S(1)} %get-tuple-element.35), channel_id=1, source_target_pairs={{0,8},{8,16},{16,24},{1,9},{9,17},{17,25},{2,10},{10,18},{18,26},{... | collective-permute-start | bytes 24584 | tf_op jit(solution)/shard_map/ppermute | solution.py:356
  28.7 19.5 %all-to-all-start = ((f32[8,16,256]{2,1,0:T(8,128)}), f32[8,16,256]{2,1,0:T(8,128)S(1)}, u32[]{:S(2)}, u32[]{:S(2)}) async-start(f32[8,16,256]{2,1,0:T(8,128)} %bitcast.6), calls=%async_computation | async-start | bytes 262144 | tf_op jit(solution)/shard_map/all_to_all | solution.py:397
  32.5 5.5 %copy-start.11 = (f32[4,512]{1,0:T(4,128)}, f32[4,512]{1,0:T(4,128)S(1)}, u32[]{:S(2)}) copy-start(f32[4,512]{1,0:T(4,128)S(1)} %collective-permute-done.2.near_coupling) | copy-start | bytes 24580
  32.5 15.7 %collective-permute-start.8 = (f32[128,512]{1,0:T(8,128)S(1)}, f32[128,512]{1,0:T(8,128)}, u32[]{:S(2)}, u32[]{:S(2)}) collective-permute-start(f32[128,512]{1,0:T(8,128)S(1)} %bitcast.30), channel_id=1, source_target_pairs={{0,24},{8,16},{16,8},{24,0},{1,25},{9,17},{17,9},{25,1},{2,26},{10... | collective-permute-start | bytes 786440 | tf_op jit(solution)/shard_map/ppermute | solution.py:406
  34.6 3.3 %copy-start.14 = (f32[4,4,128]{2,1,0:T(4,128)}, f32[4,4,128]{2,1,0:T(4,128)S(1)}, u32[]{:S(2)}) copy-start(f32[4,4,128]{2,1,0:T(4,128)S(1)} %collective-permute-done.5.after) | copy-start | bytes 24580
  34.6 13.5 %collective-permute-start.7 = (f32[128,512]{1,0:T(8,128)S(1)}, f32[128,512]{1,0:T(8,128)}, u32[]{:S(2)}, u32[]{:S(2)}) collective-permute-start(f32[128,512]{1,0:T(8,128)S(1)} %bitcast.31), channel_id=1, source_target_pairs={{0,16},{8,24},{16,0},{24,8},{1,17},{9,25},{17,1},{25,9},{2,18},{10... | collective-permute-start | bytes 786440 | tf_op jit(solution)/shard_map/ppermute | solution.py:406
  36.4 1.5 %copy-start.16 = (f32[4,4,128]{2,1,0:T(4,128)}, f32[4,4,128]{2,1,0:T(4,128)S(1)}, u32[]{:S(2)}) copy-start(f32[4,4,128]{2,1,0:T(4,128)S(1)} %collective-permute-done.4.before) | copy-start | bytes 24580
  36.4 11.7 %collective-permute-start.6 = (f32[128,512]{1,0:T(8,128)S(1)}, f32[128,512]{1,0:T(8,128)}, u32[]{:S(2)}, u32[]{:S(2)}) collective-permute-start(f32[128,512]{1,0:T(8,128)S(1)} %bitcast.32), channel_id=1, source_target_pairs={{0,8},{8,0},{16,24},{24,16},{1,9},{9,1},{17,25},{25,17},{2,10},{10... | collective-permute-start | bytes 786440 | tf_op jit(solution)/shard_map/ppermute | solution.py:406
  36.5 0.7 copy-start.5
  37.2 0.7 copy-start.7
  38.0 2.2 %copy-start.3 = (f32[4,512,512]{2,1,0:T(8,128)S(1)}, f32[4,512,512]{2,1,0:T(8,128)}, u32[]{:S(2)}) copy-start(f32[4,512,512]{2,1,0:T(8,128)} %tile.1) | copy-start | bytes 12582916
  40.2 1.0 %copy-start.6 = (f32[4,168,128]{2,1,0:T(8,128)S(1)}, f32[4,168,128]{2,1,0:T(8,128)}, u32[]{:S(2)}) copy-start(f32[4,168,128]{2,1,0:T(8,128)} %copy-done.5) | copy-start | bytes 1032196
  41.1 1.0 %copy-start.8 = (f32[4,168,128]{2,1,0:T(8,128)S(1)}, f32[4,168,128]{2,1,0:T(8,128)}, u32[]{:S(2)}) copy-start(f32[4,168,128]{2,1,0:T(8,128)} %copy-done.7) | copy-start | bytes 1032196
  42.1 0.7 copy-start.12
  42.8 0.7 copy-start.15
  43.5 0.7 copy-start.17
  46.8 1.4 %copy-start = (bf16[4,512,512]{2,1,0:T(8,128)(2,1)}, bf16[4,512,512]{2,1,0:T(8,128)(2,1)S(1)}, u32[]{:S(2)}) copy-start(bf16[4,512,512]{2,1,0:T(8,128)(2,1)S(1)} %get-tuple-element.22.tile_low) | copy-start | bytes 6291460
  51.0 15.1 %collective-permute-start.10 = (f32[4,168,128]{2,1,0:T(8,128)S(1)}, f32[4,168,128]{2,1,0:T(8,128)S(1)}, u32[]{:S(2)}, u32[]{:S(2)}) collective-permute-start(f32[4,168,128]{2,1,0:T(8,128)S(1)} %get-tuple-element.19.field.refs_0_.residual), channel_id=1, source_target_pairs={{1,2},{3,4},{5,6},{2,1},{4,3},{6,5},{9,10},{11,12},{13,14},{10,9},... | collective-permute-start | bytes 1032200 | tf_op jit(solution)/shard_map/ppermute | solution.py:347
  51.7 14.4 %collective-permute-start.9 = (f32[4,168,128]{2,1,0:T(8,128)S(1)}, f32[4,168,128]{2,1,0:T(8,128)S(1)}, u32[]{:S(2)}, u32[]{:S(2)}) collective-permute-start(f32[4,168,128]{2,1,0:T(8,128)S(1)} %get-tuple-element.19.field.refs_0_.residual), channel_id=1, source_target_pairs={{0,1},{1,0},{2,3},{3,2},{4,5},{5,4},{6,7},{7,6},{8,9},{9,8},{10,11... | collective-permute-start | bytes 1032200 | tf_op jit(solution)/shard_map/ppermute | solution.py:348
  55.2 10.9 %collective-permute-start.12 = (f32[4,4,128]{2,1,0:T(4,128)S(1)}, f32[4,4,128]{2,1,0:T(4,128)S(1)}, u32[]{:S(2)}, u32[]{:S(2)}) collective-permute-start(f32[4,4,128]{2,1,0:T(4,128)S(1)} %get-tuple-element.32), channel_id=1, source_target_pairs={{8,0},{16,8},{24,16},{9,1},{17,9},{25,17},{10,2},{18,10},{26,18},{... | collective-permute-start | bytes 24584 | tf_op jit(solution)/shard_map/ppermute | solution.py:357
  56.5 9.6 %collective-permute-start.11 = (f32[4,4,128]{2,1,0:T(4,128)S(1)}, f32[4,4,128]{2,1,0:T(4,128)S(1)}, u32[]{:S(2)}, u32[]{:S(2)}) collective-permute-start(f32[4,4,128]{2,1,0:T(4,128)S(1)} %get-tuple-element.33), channel_id=1, source_target_pairs={{0,8},{8,16},{16,24},{1,9},{9,17},{17,25},{2,10},{10,18},{18,26},{... | collective-permute-start | bytes 24584 | tf_op jit(solution)/shard_map/ppermute | solution.py:356
  61.0 1.6 %copy-start.1 = (bf16[4,512,512]{2,1,0:T(8,128)(2,1)S(1)}, bf16[4,512,512]{2,1,0:T(8,128)(2,1)}, u32[]{:S(2)}) copy-start(bf16[4,512,512]{2,1,0:T(8,128)(2,1)} %copy-done) | copy-start | bytes 6291460
  62.6 3.5 %copy-start.13 = (f32[4,512]{1,0:T(4,128)S(1)}, f32[4,512]{1,0:T(4,128)}, u32[]{:S(2)}) copy-start(f32[4,512]{1,0:T(4,128)} %copy-done.11) | copy-start | bytes 24580
  62.6 14.8 %copy-start.2 = (bf16[4,512,512]{2,1,0:T(8,128)(2,1)S(1)}, bf16[4,512,512]{2,1,0:T(8,128)(2,1)}, u32[]{:S(2)}) copy-start(bf16[4,512,512]{2,1,0:T(8,128)(2,1)} %copy-done) | copy-start | bytes 6291460
  67.1 13.8 %collective-permute-start.14 = (f32[4,168,128]{2,1,0:T(8,128)S(1)}, f32[4,168,128]{2,1,0:T(8,128)S(1)}, u32[]{:S(2)}, u32[]{:S(2)}) collective-permute-start(f32[4,168,128]{2,1,0:T(8,128)S(1)} %shard_map.144.field.refs_0_.image), channel_id=1, source_target_pairs={{1,2},{3,4},{5,6},{2,1},{4,3},{6,5},{9,10},{11,12},{13,14},{10,9},... | collective-permute-start | bytes 1032200 | tf_op jit(solution)/shard_map/ppermute | solution.py:347
  67.8 13.2 %collective-permute-start.13 = (f32[4,168,128]{2,1,0:T(8,128)S(1)}, f32[4,168,128]{2,1,0:T(8,128)S(1)}, u32[]{:S(2)}, u32[]{:S(2)}) collective-permute-start(f32[4,168,128]{2,1,0:T(8,128)S(1)} %shard_map.144.field.refs_0_.image), channel_id=1, source_target_pairs={{0,1},{1,0},{2,3},{3,2},{4,5},{5,4},{6,7},{7,6},{8,9},{9,8},{10,11... | collective-permute-start | bytes 1032200 | tf_op jit(solution)/shard_map/ppermute | solution.py:348
  70.7 10.2 %collective-permute-start.16 = (f32[4,4,128]{2,1,0:T(4,128)S(1)}, f32[4,4,128]{2,1,0:T(4,128)S(1)}, u32[]{:S(2)}, u32[]{:S(2)}) collective-permute-start(f32[4,4,128]{2,1,0:T(4,128)S(1)} %get-tuple-element.30), channel_id=1, source_target_pairs={{8,0},{16,8},{24,16},{9,1},{17,9},{25,17},{10,2},{18,10},{26,18},{... | collective-permute-start | bytes 24584 | tf_op jit(solution)/shard_map/ppermute | solution.py:357
  71.9 9.0 %collective-permute-start.15 = (f32[4,4,128]{2,1,0:T(4,128)S(1)}, f32[4,4,128]{2,1,0:T(4,128)S(1)}, u32[]{:S(2)}, u32[]{:S(2)}) collective-permute-start(f32[4,4,128]{2,1,0:T(4,128)S(1)} %get-tuple-element.31), channel_id=1, source_target_pairs={{0,8},{8,16},{16,24},{1,9},{9,17},{17,25},{2,10},{10,18},{18,26},{... | collective-permute-start | bytes 24584 | tf_op jit(solution)/shard_map/ppermute | solution.py:356

commit v2 on v1

v2 whole, which is shorter than its diff:
```python
import functools
import jax
import jax.numpy as jnp
from jax import lax
from jax.experimental import pallas as pl
from jax.experimental.pallas import tpu as pltpu
from jax.sharding import PartitionSpec as P

TIES = 4
HOUR_LANES = 64
LANES = 128
FIRST = 10**10
WIDE = 256
F32 = jnp.float32
BF16 = jnp.bfloat16
VMEM_LIMIT = 12 * 1024 * 1024

WHOLE = pl.BlockSpec(memory_space=pltpu.VMEM)
SCALARS = pl.BlockSpec(memory_space=pltpu.SMEM)
UNREAD = pl.BlockSpec(memory_space=pl.ANY)
IN_HBM = pl.BlockSpec(memory_space=pltpu.HBM)


def call(kernel, out_shape, in_specs, scratch=(), flops=1, out_specs=None):
    many = isinstance(out_shape, (tuple, list))
    if out_specs is None:
        out_specs = [WHOLE] * len(out_shape) if many else WHOLE
    inner = getattr(kernel, "func", kernel)
    return pl.pallas_call(
        kernel,
        name=inner.__name__,
        out_shape=out_shape,
        in_specs=in_specs,
        out_specs=out_specs,
        scratch_shapes=scratch,
        compiler_params=pltpu.CompilerParams(vmem_limit_bytes=VMEM_LIMIT),
        cost_estimate=pl.CostEstimate(flops=flops, bytes_accessed=1, transcendentals=0),
    )


def landing(*operands):
    return [pltpu.VMEM(a.shape, a.dtype) for a in operands] + [
        pltpu.SemaphoreType.DMA((len(operands),))
    ]


def in_hbm(*operands):
    return [pltpu.with_memory_space_constraint(a, pltpu.HBM) for a in operands]


def fetch(sources, targets, semaphores):
    copies = [
        pltpu.make_async_copy(source, target, semaphores.at[k])
        for k, (source, target) in enumerate(zip(sources, targets))
    ]
    for copy in copies:
        copy.start()
    return copies


def f32_shape(*shape):
    return jax.ShapeDtypeStruct(shape, F32)


def two_parts(value):
    high = value.astype(BF16)
    return high, (value - high.astype(F32)).astype(BF16)


def three_parts(value):
    high = value.astype(BF16)
    rest = value - high.astype(F32)
    middle = rest.astype(BF16)
    return high, middle, (rest - middle.astype(F32)).astype(BF16)


def dot(left, right, contract_right=0):
    return lax.dot_general(
        left, right, (((1,), (contract_right,)), ((), ())), preferred_element_type=F32
    )


def split_dot(left, right_high, right_low, contract_right=0):
    high, low = two_parts(left)
    return (
        dot(high, right_high, contract_right)
        + dot(low, right_high, contract_right)
        + dot(high, right_low, contract_right)
    )


def take(ref, area, span, first=0, hours=None):
    hours = ref.shape[1] // span - first if hours is None else hours
    rows = pl.ds(area + span * first, hours, stride=span)
    return jnp.concatenate([ref[k, rows, :] for k in range(ref.shape[0])], axis=1)


def put(ref, area, span, value):
    rows = pl.ds(area, value.shape[0], stride=span)
    for k in range(ref.shape[0]):
        ref[k, rows, :] = value[:, LANES * k : LANES * (k + 1)]


def row_of(ref, row):
    return jnp.concatenate([ref[k, row : row + 1, :] for k in range(ref.shape[0])], axis=1)


def keys_of(owner, cap):
    rows = owner.shape[1]
    owner_row = owner[...].astype(F32)
    owner_column = jnp.transpose(jnp.broadcast_to(owner_row, (LANES, rows)))[:, 0:1]
    earlier = lax.broadcasted_iota(jnp.int32, (rows, rows), 0) < lax.broadcasted_iota(
        jnp.int32, (rows, rows), 1
    )
    same = jnp.where(earlier & (owner_column == owner_row), 1.0, 0.0)
    return owner_row * cap + jnp.sum(same, axis=0, keepdims=True)


def marks_of(keys, area, rank, cap):
    return jnp.where((area * cap + rank).astype(F32) == keys, 1.0, 0.0).astype(BF16)


def pack_kernel(span, cap, hours, index, owner_far, sens_far, weight_far, *outs):
    *away, here, other, owner, sens, weight, semaphores = outs
    copies = fetch((owner_far, sens_far, weight_far), (owner, sens, weight), semaphores)
    chip, core, member = index[0], index[1], index[2]
    blocks = owner.shape[1]
    parts = sens.shape[1] // WIDE
    copies[0].wait()
    keys = keys_of(owner, cap)
    slot = lax.broadcasted_iota(jnp.int32, (2 * cap * (len(away) + 1), blocks), 0)
    group = (chip ^ (slot // (2 * cap))) * 2 + (core ^ (slot // cap % 2))
    local = lax.broadcasted_iota(jnp.int32, (2 * span * cap, blocks), 0)
    local_group = chip * 2 + (core ^ (local // (span * cap)))
    local_area = local_group * span + (member ^ (local // cap % span))
    sens_marks = jnp.concatenate(
        [
            marks_of(keys, group * span + member, slot % cap, cap)[2 * cap :],
            marks_of(keys, local_area, local % cap, cap),
        ],
        axis=0,
    )
    area_marks = [marks_of(keys, group * span + k, slot % cap, cap) for k in range(span)]
    copies[2].wait()
    gap = jnp.zeros((LANES - hours, blocks), F32)
    by_block = jnp.transpose(jnp.concatenate([weight[...], gap], axis=0))
    left_parts = two_parts(by_block)
    right_parts = two_parts(pltpu.roll(by_block, HOUR_LANES, 1))
    weights = jnp.concatenate(
        [
            sum(
                dot(area_marks[2 * pair], a) + dot(area_marks[2 * pair + 1], b)
                for a, b in zip(left_parts, right_parts)
            )
            for pair in range(span // 2)
        ],
        axis=1,
    )
    copies[1].wait()
    high, low = two_parts(sens[...])
    rows = dot(sens_marks, high) + dot(sens_marks, low)
    for k in range(len(away)):
        for core_step in range(2):
            row, at = cap * (2 * k + core_step), cap * (parts + 1) * core_step
            for part in range(parts):
                lanes = slice(WIDE * part, WIDE * (part + 1))
                away[k][pl.ds(at + cap * part, cap), :] = rows[row : row + cap, lanes]
            away[k][pl.ds(at + cap * parts, cap), :] = weights[2 * cap + row :][:cap]
    count = span * cap
    for core_step, out in ((0, here), (1, other)):
        row = 2 * cap * len(away) + count * core_step
        for part in range(parts):
            lanes = slice(WIDE * part, WIDE * (part + 1))
            out[pl.ds(count * part, count), :] = rows[row : row + count, lanes]
        out[pl.ds(count * parts, cap), :] = weights[cap * core_step :][:cap]


def fields_kernel(barrier, *refs):
    guess_out, right_out, diagonal_out = refs[-9:-6]
    guess, gradient, slack, hess, coupling, semaphores = landed = refs[-6:]
    for copy in fetch(refs[:5], landed[:5], semaphores):
        copy.wait()
    hours, span, width = guess.shape
    rows = hours * span
    shape = (rows, LANES)
    for k in range(width // LANES):
        lanes = pl.ds(LANES * k, LANES)
        slack_rows = slack[:, :, lanes].reshape(shape)
        guess_out[k, pl.ds(0, rows), :] = guess[:, :, lanes].reshape(shape)
        guess_out[k, pl.ds(rows, span), :] = coupling[:, LANES * k : LANES * (k + 1)]
        guess_out[k, pl.ds(rows + span, span), :] = jnp.zeros((span, LANES), F32)
        right_out[k] = barrier[0] / slack_rows - gradient[:, :, lanes].reshape(shape)
        diagonal_out[k] = hess[:, :, lanes].reshape(shape) + barrier[0] / (
            slack_rows * slack_rows
        )


def halves_kernel(index, tile_far, offsets_far, gains_far, after, *refs):
    tile_high, tile_low, ties, offsets, gains, tile, semaphores = refs
    span = tile.shape[0]
    each = [tile_far.at[i] for i in range(span)]
    copies = fetch(
        [offsets_far, gains_far] + each,
        [offsets, gains] + [tile.at[i] for i in range(span)],
        semaphores,
    )
    copies[0].wait()
    copies[1].wait()
    first = (index[0] * 2 + index[1] - 1) * span
    for i in range(2 * span):
        area = jnp.maximum(first + i, 0)
        for step in range(span):
            total = 0.0
            for k in range(offsets.shape[0]):
                total = total + jnp.where(offsets[k, area] == step + 1, gains[k, area], 0.0)
            ties[i, step] = total
    for i in range(span):
        copies[2 + i].wait()
        high, low = two_parts(tile[i])
        tile_high[i] = high
        tile_low[i] = low


def weights_kernel(span, cap, here, beside, crossed, *refs):
    *arrived, weights = refs
    hours = weights.shape[1]
    chunk = arrived[0].shape[0] // 2
    pieces = [ref[pl.ds(ref.shape[0] - cap, cap), :] for ref in (here, beside)]
    for k, ref in enumerate(arrived):
        pieces.append(ref[pl.ds(chunk - cap, cap), :])
        pieces.append(crossed[pl.ds(chunk * (k + 1) - cap, cap), :])
    by_slot = jnp.concatenate(pieces, axis=0)
    for pair in range(span // 2):
        turned = jnp.transpose(by_slot[:, LANES * pair : LANES * (pair + 1)])
        for half in range(2):
            weights[2 * pair + half] = turned[HOUR_LANES * half :][:hours]


def upper(ties, span, i, j):
    return ties[span + i, j + span - i - 1] if j <= i else 0.0


def lower(ties, span, i, j):
    return ties[j, i + span - j - 1] if j >= i else 0.0


def local_tie(ties, span, i, j):
    a, b = min(i, j), max(i, j)
    return ties[span + a, b - a - 1]


def cross_coefficients(ties, odd, span, i):
    near, far = [], []
    for j in range(span):
        up, down = upper(ties, span, i, j), lower(ties, span, i, j)
        near.append(jnp.where(odd, down, up))
        far.append(jnp.where(odd, up, down))
    return near, far


def both_hours(field, area, span, hours):
    return take(field, area, span, 0, hours) + take(field, area, span, 2, hours)


def both_hours_inside(own):
    blank = jnp.zeros((1, own.shape[1]), F32)
    earlier = jnp.concatenate([blank, own[: own.shape[0] - 1]], axis=0)
    return earlier + jnp.concatenate([own[1:], blank], axis=0)


def local_pull(ties, coupling, field, span, i, hours, first=1):
    pull = None
    for j in range(span):
        if j != i:
            term = local_tie(ties, span, i, j) * (
                coupling[j : j + 1, :] * take(field, j, span, first, hours)
            )
            pull = term if pull is None else pull + term
    return pull


def first_kernel(
    span,
    deep,
    index,
    ties,
    guess,
    right,
    diagonal_in,
    near,
    far,
    weights,
    tile_high,
    tile_low,
    ramp,
    coupling,
    partial,
    diagonal,
    up,
    down,
):
    odd = index[1] == 1
    blocks, rows = right.shape[:2]
    hours = rows // span
    near_coupling = [row_of(near, rows + j) for j in range(span)]
    far_coupling = [row_of(far, rows + j) for j in range(span)]
    near_fields = [near_coupling[j] * take(near, j, span, 0, hours) for j in range(span)]
    far_fields = [far_coupling[j] * take(far, j, span, 0, hours) for j in range(span)]
    for i in range(span):
        own = take(guess, i, span, 0, hours)
        own_coupling = coupling[i : i + 1, :]
        own_ramp = ramp[i : i + 1, :]
        near_of, far_of = cross_coefficients(ties, odd, span, i)
        strength = jnp.zeros_like(own_coupling)
        pull = local_pull(ties, coupling, guess, span, i, hours, 0)
        for j in range(span):
            if j != i:
                strength = strength + local_tie(ties, span, i, j) * coupling[j : j + 1, :]
            strength = strength + near_of[j] * near_coupling[j] + far_of[j] * far_coupling[j]
            pull = pull + near_of[j] * near_fields[j] + far_of[j] * far_fields[j]
        folded = take(diagonal_in, i, span) + (2.0 * own_ramp + own_coupling * strength)
        put(diagonal, i, span, folded)
        image = (
            folded * own
            + split_dot(own, tile_high[i], tile_low[i])
            - own_ramp * both_hours_inside(own)
            - own_coupling * pull
        )
        put(partial, i, span, take(right, i, span) - image)
    for k in range(blocks):
        for out, low in ((up, False), (down, True)):
            at = 0
            for source, count in (
                (partial, deep * span),
                (guess, deep * span),
                (diagonal, (deep - 1) * span),
            ):
                start = 0 if low else rows - count
                out[k, pl.ds(at, count), :] = source[k, pl.ds(start, count), :]
                at += count
            start = 0 if low else hours - deep
            out[k, pl.ds(at, deep), :] = weights[k, pl.ds(start, deep), :]
            out[k, pl.ds(at + deep, deep), :] = jnp.zeros((deep, LANES), F32)


def security(own, high, low, weight):
    flows = split_dot(own, high, low, 1)
    return split_dot(flows * weight, high, low)


def clear_outside(index, target, count):
    blocks, rows = target.shape[:2]
    keep_first = jnp.where(index[2] == 0, 0.0, 1.0)
    keep_last = jnp.where(index[2] == index[3] - 1, 0.0, 1.0)
    for k in range(blocks):
        target[k, 0:count, :] = target[k, 0:count, :] * keep_first
        target[k, rows - count : rows, :] = target[k, rows - count : rows, :] * keep_last


def owned_kernel(
    span,
    cap,
    deep,
    index,
    guess_in,
    partial_in,
    diagonal_in,
    weights_in,
    before,
    after,
    ramp,
    here,
    beside,
    *refs,
):
    pieces, outs = refs[:span], refs[span:]
    residual, sent, high_out, low_out, diagonal, weights, guess, partial = outs
    blocks, rows = partial_in.shape[:2]
    for k in range(blocks):
        at = 0
        for target, middle, edge in (
            (partial, partial_in, deep * span),
            (guess, guess_in, deep * span),
            (diagonal, diagonal_in, (deep - 1) * span),
        ):
            target[k, pl.ds(0, edge), :] = before[k, pl.ds(at, edge), :]
            target[k, pl.ds(edge, rows), :] = middle[k, pl.ds(0, rows), :]
            target[k, pl.ds(edge + rows, edge), :] = after[k, pl.ds(at, edge), :]
            at += edge
        edge = ramp[:, LANES * k : LANES * (k + 1)]
        for hour, other in (
            (deep - 1, deep),
            (deep, deep - 1),
            (rows // span + deep - 1, rows // span + deep),
            (rows // span + deep, rows // span + deep - 1),
        ):
            target = pl.ds(span * hour, span)
            partial[k, target, :] = (
                partial[k, target, :] + edge * guess[k, pl.ds(span * other, span), :]
            )
    for area in range(span):
        weights[area] = jnp.concatenate(
            [before[area, pl.ds(at, deep), :], weights_in[area], after[area, pl.ds(at, deep), :]],
            axis=0,
        )
    parts = guess.shape[0] * LANES // WIDE
    group = pieces[0].shape[0] // (parts * cap)
    terms = []
    for step in range(span):
        area = index[2] ^ step
        wide = []
        for part in range(parts):
            at = cap * (span * part + step)
            rows = [here[pl.ds(at, cap), :], beside[pl.ds(at, cap), :]]
            rows += [
                pieces[step][pl.ds(cap * (parts * k + part), cap), :] for k in range(group)
            ]
            wide.append(jnp.concatenate(rows, axis=0))
        high, low = two_parts(jnp.concatenate(wide, axis=1))
        high_out[step] = high
        low_out[step] = low
        term = security(take(guess, area, span), high, low, weights[area])
        terms.append(take(partial, area, span) - term)
    for step in range(span):
        put(residual, index[2] ^ step, span, terms[step])
    clear_outside(index, residual, deep * span)
    for k in range(sent.shape[0]):
        sent[k] = residual[k, pl.ds(span, sent.shape[1]), :]


def local_kernel(
    span,
    skip,
    with_sums,
    index,
    ties,
    field,
    diagonal,
    ramp,
    coupling,
    tile_high,
    tile_low,
    sens_high,
    sens_low,
    weights,
    *refs,
):
    if with_sums:
        earlier, image, sums = refs
    else:
        (image,) = refs
    hours = image.shape[1] // span
    for i in range(span):
        value = (
            take(diagonal, i, span, skip - 1, hours) * take(field, i, span, 1, hours)
            + split_dot(take(field, i, span, 1, hours), tile_high[i], tile_low[i])
            - ramp[i : i + 1, :] * both_hours(field, i, span, hours)
            - coupling[i : i + 1, :] * local_pull(ties, coupling, field, span, i, hours)
        )
        put(image, i, span, value)
    terms = []
    for step in range(span):
        area = index[2] ^ step
        weight = weights[area][skip : skip + hours]
        own = take(field, area, span, 1, hours)
        terms.append(security(own, sens_high[step], sens_low[step], weight))
    for step in range(span):
        area = index[2] ^ step
        put(image, area, span, take(image, area, span) + terms[step])
    if with_sums:
        count = image.shape[1]
        first = (earlier.shape[1] - count) // 2
        a, b = earlier[:, pl.ds(first, count), :], field[:, pl.ds(span, count), :]
        sums[...] = lanes_of([jnp.sum(a * a), jnp.sum(a * b), jnp.sum(b * b)])


def lanes_of(values):
    lane = lax.broadcasted_iota(jnp.int32, (1, LANES), 1)
    row = jnp.zeros((1, LANES), F32)
    for position, value in enumerate(values):
        row = jnp.where(lane == position, value, row)
    return row


def cross_kernel(
    span, with_sums, index, ties, image, near, far, near_first, far_first, coupling, *refs
):
    if with_sums:
        earlier, sums, total, spread = refs
    else:
        total, sent = refs
    odd = index[1] == 1
    hours = image.shape[1] // span
    count = near_first.shape[1] - 2 * span
    near_fields = [row_of(near_first, count + j) * take(near, j, span) for j in range(span)]
    far_fields = [row_of(far_first, count + j) * take(far, j, span) for j in range(span)]
    for i in range(span):
        near_of, far_of = cross_coefficients(ties, odd, span, i)
        pull = near_of[0] * near_fields[0] + far_of[0] * far_fields[0]
        for j in range(1, span):
            pull = pull + near_of[j] * near_fields[j] + far_of[j] * far_fields[j]
        put(total, i, span, take(image, i, span) - coupling[i : i + 1, :] * pull)
    if with_sums:
        first = (earlier.shape[1] - image.shape[1]) // 2
        last = jnp.sum(earlier[:, pl.ds(first, image.shape[1]), :] * total[...])
        lane = lax.broadcasted_iota(jnp.int32, (1, LANES), 1)
        spread[...] = jnp.broadcast_to(jnp.where(lane == 3, last, sums[...]), spread.shape)
    else:
        clear_outside(index, total, span)
        for k in range(sent.shape[0]):
            sent[k] = total[k, pl.ds(span, sent.shape[1]), :]


def last_kernel(gathered, guess, residual, image, second, step_out, residual_out):
    sums = jnp.sum(gathered[...], axis=0, keepdims=True)
    rr, ra, aa, ab = (sums[:, k : k + 1] for k in range(4))
    alpha = rr / ra
    rr_next = alpha * (alpha * aa - ra)
    beta = rr_next / rr
    product = ra - 2.0 * alpha * aa + alpha * alpha * ab
    alpha_next = rr_next / (product - beta * rr_next / alpha)
    one = alpha + alpha_next * (1.0 + beta)
    two = alpha_next * alpha
    hours, span, width = step_out.shape
    rows = hours * span

    def inner(ref, k):
        return ref[k, pl.ds((ref.shape[1] - rows) // 2, rows), :]

    for k in range(width // LANES):
        lanes = pl.ds(LANES * k, LANES)
        r, a = inner(residual, k), inner(image, k)
        step = guess[k, pl.ds(0, rows), :] + one * r - two * a
        left = r - one * a + two * second[k]
        step_out[:, :, lanes] = step.reshape(hours, span, LANES)
        residual_out[:, :, lanes] = left.reshape(hours, span, LANES)


def swap(value, axis, step, name):
    count = lax.axis_size(axis)
    with jax.named_scope(name):
        return lax.ppermute(value, axis, [(i, i ^ step) for i in range(count)])


def exchange(field, name):
    groups = lax.axis_size("area")
    far_pairs = [(i, i + 1) for i in range(1, groups - 1, 2)]
    with jax.named_scope(name + "_far"):
        far = lax.ppermute(field, "area", far_pairs + [(j, i) for i, j in far_pairs])
    return swap(field, "area", 1, name + "_near"), far


def adjacent_hours(up, down, name):
    ups = [(i, i + 1) for i in range(lax.axis_size("tm") - 1)]
    with jax.named_scope(name + "_before"):
        before = lax.ppermute(up, "tm", ups)
    with jax.named_scope(name + "_after"):
        after = lax.ppermute(down, "tm", [(j, i) for i, j in ups])
    return before, after


def body(
    gradient,
    barrier,
    slack,
    hess_diag,
    tile,
    ramp_weight,
    bus_coupling,
    tie_offset,
    tie_admittance,
    con_sens,
    con_weight,
    con_owner,
    step_guess,
):
    hours, span, width = gradient.shape
    total_areas = tie_offset.shape[0]
    groups, members = lax.axis_size("area"), lax.axis_size("tm")
    chips = groups // 2
    assert members == span and span == TIES and span & (span - 1) == 0
    assert chips & (chips - 1) == 0 and width % LANES == 0
    rows_held = con_sens.shape[0]
    cap = max(2, (2 * rows_held + total_areas - 1) // total_areas)
    slots = groups * cap
    deep = 2
    assert hours + 2 * deep <= HOUR_LANES and rows_held <= width
    blocks = width // LANES
    rows = hours * span
    member, group = lax.axis_index("tm"), lax.axis_index("area")
    index = jnp.stack([group // 2, group % 2, member, jnp.int32(members)]).astype(jnp.int32)

    owner = con_owner.reshape(1, rows_held)
    weight = con_weight.T
    parts = width // WIDE
    chunk = (parts + 1) * cap
    local = (parts * span + 1) * cap
    *away, here, other = call(
        functools.partial(pack_kernel, span, cap, hours),
        [f32_shape(2 * chunk, WIDE)] * (chips - 1)
        + [f32_shape(local, WIDE)] * 2,
        [SCALARS] + [IN_HBM] * 3,
        landing(owner, con_sens, weight),
    )(index, *in_hbm(owner, con_sens, weight))
    arrived = [swap(a, "area", 2 * (k + 1), "rows_chips") for k, a in enumerate(away)]
    beside = swap(other, "area", 1, "rows_beside")
    crossed = swap(jnp.concatenate([a[chunk:] for a in arrived], axis=0), "area", 1, "rows_cores")
    field_shape = f32_shape(blocks, rows, LANES)
    natural = (step_guess, gradient, slack, hess_diag)
    guess, right_side, diagonal_in = call(
        fields_kernel,
        [f32_shape(blocks, rows + 2 * span, LANES), field_shape, field_shape],
        [SCALARS] + [IN_HBM] * 5 + [UNREAD],
        landing(*natural, bus_coupling),
    )(barrier, *in_hbm(*natural, bus_coupling), here)
    near_guess, far_guess = exchange(guess, "guess")

    tile_shape = jax.ShapeDtypeStruct(tile.shape, BF16)
    tables = (tie_offset.T, tie_admittance.T)
    tile_high, tile_low, ties = call(
        halves_kernel,
        [tile_shape, tile_shape, f32_shape(2 * span, span)],
        [SCALARS] + [IN_HBM] * 3 + [UNREAD],
        [pltpu.SMEM(a.shape, a.dtype) for a in tables]
        + [pltpu.VMEM(tile.shape, F32), pltpu.SemaphoreType.DMA((2 + span,))],
        out_specs=[WHOLE, WHOLE, SCALARS],
    )(index, *in_hbm(tile, *tables), right_side)

    weights = call(
        functools.partial(weights_kernel, span, cap),
        f32_shape(span, hours, slots),
        [WHOLE] * (3 + len(arrived)),
    )(here, beside, crossed, *arrived)
    piece = jnp.concatenate(
        [
            a[at : at + parts * cap]
            for k, ref in enumerate(arrived)
            for a, at in ((ref, 0), (crossed, chunk * k))
        ],
        axis=0,
    )
    pieces = [piece] + [swap(piece, "tm", step, "rows_members") for step in range(1, members)]

    edge_rows = (3 * deep - 1) * span + 2 * deep
    partial, diagonal, up, down = call(
        functools.partial(first_kernel, span, deep),
        [field_shape] * 2 + [f32_shape(blocks, edge_rows, LANES)] * 2,
        [SCALARS] * 2 + [WHOLE] * 10,
        flops=FIRST,
    )(
        index,
        ties,
        guess,
        right_side,
        diagonal_in,
        near_guess,
        far_guess,
        weights,
        tile_high,
        tile_low,
        ramp_weight,
        bus_coupling,
    )
    before, after = adjacent_hours(up, down, "partial")

    sens_shape = jax.ShapeDtypeStruct((span, slots, width), BF16)
    deep_shape = f32_shape(blocks, rows + 2 * deep * span, LANES)
    next_shape = f32_shape(blocks, rows + 2 * (deep - 1) * span, LANES)
    residual, residual_sent, sens_high, sens_low, diagonal, owned_weight = call(
        functools.partial(owned_kernel, span, cap, deep),
        [
            deep_shape,
            next_shape,
            sens_shape,
            sens_shape,
            next_shape,
            f32_shape(span, hours + 2 * deep, slots),
        ],
        [SCALARS] + [WHOLE] * (9 + span),
        [pltpu.VMEM(deep_shape.shape, F32)] * 2,
    )(index, guess, partial, diagonal, weights, before, after, ramp_weight, here, beside, *pieces)

    def local_image(field, skip, earlier=None):
        shape = f32_shape(blocks, field.shape[1] - 2 * span, LANES)
        summed = earlier is not None
        return call(
            functools.partial(local_kernel, span, skip, summed),
            (shape, f32_shape(1, LANES)) if summed else shape,
            [SCALARS, SCALARS] + [WHOLE] * (9 + summed),
        )(
            index,
            ties,
            field,
            diagonal,
            ramp_weight,
            bus_coupling,
            tile_high,
            tile_low,
            sens_high,
            sens_low,
            owned_weight,
            *([earlier] if summed else []),
        )

    near, far = exchange(residual_sent, "residual")
    image = local_image(residual, 1)
    image, image_sent = call(
        functools.partial(cross_kernel, span, False),
        (f32_shape(*image.shape), field_shape),
        [SCALARS, SCALARS] + [WHOLE] * 6,
    )(index, ties, image, near, far, near_guess, far_guess, bus_coupling)

    near, far = exchange(image_sent, "image")
    second, sums = local_image(image, 2, residual)
    second, spread = call(
        functools.partial(cross_kernel, span, True),
        (field_shape, f32_shape(groups * members, LANES)),
        [SCALARS, SCALARS] + [WHOLE] * 8,
    )(index, ties, second, near, far, near_guess, far_guess, bus_coupling, image, sums)
    gathered = lax.all_to_all(spread, ("tm", "area"), split_axis=0, concat_axis=0, tiled=True)
    out_shape = f32_shape(hours, span, width)
    return tuple(
        call(
            last_kernel,
            (out_shape, out_shape),
            [WHOLE] * 5,
        )(gathered, guess, residual, image, second)
    )


def solution(mesh):
    field = P("tm", "area", None)
    placed = (
        field,
        P(),
        field,
        field,
        P("area", None, None),
        P("area", None),
        P("area", None),
        P(),
        P(),
        P("area", None),
        P("area", "tm"),
        P("area", None),
        field,
    )
    return jax.shard_map(
        body, mesh=mesh, in_specs=placed, out_specs=(field, field), check_vma=False
    )
```

time: 95.6 us -> 70.3 us (0.74)
  starting transfers between devices: 46.1 us -> 26.5 us
  local copies, waits for them, and re-layouts: 15.3 us -> 0.05 us
  Pallas kernels: 17.8 us -> 22.2 us
  waiting for transfers between devices: 1.33 us -> 5.72 us
  blocking collectives: 11.1 us -> 14 us
  other arithmetic: 1.27 us -> 0.09 us
    unnamed x46 -> x9, local copies, waits for them, and re-layouts: 13.4 us -> 0.03 us
    ppermute x13, starting transfers between devices: 36 us -> 24.4 us  [the longest x11 19.7 us: swap(): return lax.ppermute(value, axis, [(i, i ^ step) for i in range(count)])]
    all_to_all x2 -> x0, starting transfers between devices: 7.2 us -> none  [the longest x1 3.79 us: body(): lax.all_to_all(weight_send.reshape(groups, cap, span * HOUR_LANES), 'area...]
    ppermute x13, waiting for transfers between devices: 0.03 us -> 5.71 us  [the longest x1 2.6 us: adjacent_hours(): after = lax.ppermute(down, 'tm', [(j, i) for i, j in ups])]
    pallas_call x8 -> x11, Pallas kernels: 17.8 us -> 22.2 us  [the longest x2 6.96 us: local_image(): call(functools.partial(local_kernel, span, skip, summed), (shape, f32_sha...]
    all_to_all x1, blocking collectives: 11.1 us -> 14 us  [body(): lax.all_to_all(spread, ('tm', 'area'), split_axis=0, concat_axis=0, tiled...]
    reshape x4 -> x0, local copies, waits for them, and re-layouts: 1.59 us -> none  [blocked(): return jnp.swapaxes(value.reshape(rows, width // 128, 128), 0, 1)]
    all_to_all x2 -> x0, waiting for transfers between devices: 1.28 us -> none  [the longest x1 1.28 us: body(): lax.all_to_all(sens_send.reshape(groups, cap, width), 'area', split_axis=...]
  transfers between devices with their start and end apart: 19 -> 16, of which waited for: 1 -> 3; matrix products, arithmetic and copies ran while one was open for 5% -> 0% of each run, Pallas kernels for 12% -> 20%
where the time goes in v2:
time: 70.3 us; the launch traced here: 70 us
  starting transfers between devices  26.5 us (38%)
  Pallas kernels  22.2 us (32%)
  blocking collectives  14 us (20%)
  waiting for transfers between devices  5.72 us (8%)
  between operations  1.54 us (2%)
    ppermute x11, starting transfers between devices, swap(): return lax.ppermute(value, axis, [(i, i ^ step) for i in range(count)])  19.7 us
    all_to_all x1, blocking collectives, body(): lax.all_to_all(spread, ('tm', 'area'), split_axis=0, concat_axis=0, tiled...  14 us
    pallas_call x2, Pallas kernels, local_image(): call(functools.partial(local_kernel, span, skip, summed), (shape, f32_sha...  6.96 us
    pallas_call x1, Pallas kernels, body(): call(halves_kernel, [tile_shape, tile_shape, f32_shape(2 * span, span)],...  3.42 us
    ppermute x1, starting transfers between devices, adjacent_hours(): before = lax.ppermute(up, 'tm', ups)  3.4 us
    ppermute x1, waiting for transfers between devices, adjacent_hours(): after = lax.ppermute(down, 'tm', [(j, i) for i, j in ups])  2.6 us
    pallas_call x1, Pallas kernels, body(): call(functools.partial(owned_kernel, span, cap, deep), [deep_shape, next_...  2.39 us
    pallas_call x1, Pallas kernels, body(): call(functools.partial(pack_kernel, span, cap, hours), [f32_shape(2 * chu...  2.28 us
  transfers between devices with their start and end apart: 16, of which 3 were waited for; matrix products, arithmetic and copies ran while one was open for 0% of the time, Pallas kernels for 20%

profile of v2, /device:TPU:0, one launch (start us, length us, event | category | flops | bytes accessed | tf_op | source)
XLA Modules:
  0.0 70.0 jit_solution(6402844878179299878)
XLA Ops:
  0.6 0.1 pad_add_fusion.index
  0.7 2.3 %pack_kernel.1 = (f32[96,256]{1,0:T(8,128)S(1)}, f32[96,256]{1,0:T(8,128)S(1)}, f32[96,256]{1,0:T(8,128)S(1)}, f32[144,256]{1,0:T(8,128)S(1)}, f32[144,256]{1,0:T(8,128)S(1)}) custom-call(s32[4]{0:T(128)S(1)} %pad_add_fusion.index, s32[1,256]{1,0:T(1,128)} %bitcast.16, f32[256,512]{1,0:T(8,128)} %sens_far.1, f32[42,256]{1,0:T(8,128)} %bitcast.13), custom_call_target="tpu_custom_call" | custom-call | flops 1 | bytes 1 | tf_op jit(solution)/shard_map/pack_kernel/pallas_call | solution.py:598
  3.0 3.1 %collective-permute-start.3 = (f32[96,256]{1,0:T(8,128)S(1)}, f32[96,256]{1,0:T(8,128)S(1)}, u32[]{:S(2)}, u32[]{:S(2)}) collective-permute-start(f32[96,256]{1,0:T(8,128)S(1)} %get-tuple-element.35), channel_id=1, source_target_pairs={{0,2},{1,3},{2,0},{3,1},{4,6},{5,7},{6,4},{7,5},{8,10},{9,11},{10,... | collective-permute-start | bytes 294920 | tf_op jit(solution)/shard_map/rows_chips/ppermute | solution.py:542
  6.1 2.6 %collective-permute-start.4 = (f32[96,256]{1,0:T(8,128)S(1)}, f32[96,256]{1,0:T(8,128)S(1)}, u32[]{:S(2)}, u32[]{:S(2)}) collective-permute-start(f32[96,256]{1,0:T(8,128)S(1)} %get-tuple-element.36), channel_id=1, source_target_pairs={{0,4},{1,5},{2,6},{3,7},{4,0},{5,1},{6,2},{7,3},{8,12},{9,13},{10,... | collective-permute-start | bytes 294920 | tf_op jit(solution)/shard_map/rows_chips/ppermute | solution.py:542
  8.7 0.0 collective-permute-start.5
  9.4 1.5 %fields_kernel.1 = (f32[4,176,128]{2,1,0:T(8,128)S(1)}, f32[4,168,128]{2,1,0:T(8,128)S(1)}, f32[4,168,128]{2,1,0:T(8,128)S(1)}) custom-call(f32[1]{0:T(128)S(6)} %copy.21.barrier, f32[42,4,512]{2,1,0:T(4,128)} %refs_0_.1, f32[42,4,512]{2,1,0:T(4,128)} %refs_1_.1, f32[42,4,512]{2,1,0:T(4,128)} %refs_2_.1, f32[42,4,512]{2,1,0:T(4,128)} %refs_3_.1, ...), custom_call_target="tpu_custom_call" | custom-call | flops 1 | bytes 1 | tf_op jit(solution)/shard_map/fields_kernel/pallas_call | solution.py:610
  10.9 0.7 collective-permute-start.1
  11.6 2.3 %collective-permute-start = (f32[4,176,128]{2,1,0:T(8,128)S(1)}, f32[4,176,128]{2,1,0:T(8,128)S(1)}, u32[]{:S(2)}, u32[]{:S(2)}) collective-permute-start(f32[4,176,128]{2,1,0:T(8,128)S(1)} %get-tuple-element.32.guess.guess_in), channel_id=1, source_target_pairs={{0,1},{1,0},{2,3},{3,2},{4,5},{5,4},{6,7},{7,6},{8,9},{9,8},{10,11... | collective-permute-start | bytes 1081352 | tf_op jit(solution)/shard_map/guess_near/ppermute | solution.py:542
  13.9 0.0 copy-start
  13.9 0.0 copy-start.1
  13.9 3.4 %halves_kernel.1 = (bf16[4,512,512]{2,1,0:T(8,128)(2,1)S(1)}, bf16[4,512,512]{2,1,0:T(8,128)(2,1)S(1)}, f32[8,4]{1,0:T(8,128)S(1)}) custom-call(s32[4]{0:T(128)S(1)} %pad_add_fusion.index, f32[4,512,512]{2,1,0:T(8,128)} %tile_far.1, s32[4,32]{1,0:T(4,128)} %bitcast.14, f32[4,32]{1,0:T(4,128)} %bitcast.15, f32[4,168,128]{2,1,0:T(8,128)S(1)} %get-tuple-element.30.after.right), custom_call_target="tpu_custom_call" | custom-call | flops 1 | bytes 1 | tf_op jit(solution)/shard_map/halves_kernel/pallas_call | solution.py:620
  17.3 0.0 collective-permute-done.3.refs_0_
  17.3 0.1 collective-permute-start.2
  17.4 0.0 collective-permute-done.4.refs_1_
  17.4 0.0 collective-permute-done.5.refs_2_
  17.5 0.5 collective-permute-start.6
  18.0 1.0 %collective-permute-done.6.crossed = f32[144,256]{1,0:T(8,128)S(1)} collective-permute-done((f32[144,256]{1,0:T(8,128)S(1)}, f32[144,256]{1,0:T(8,128)S(1)}, u32[]{:S(2)}, u32[]{:S(2)}) %collective-permute-start.6) | collective-permute-done | bytes 147488 | tf_op jit(solution)/shard_map/rows_cores/ppermute | solution.py:542
  19.1 2.5 %collective-permute-start.11 = (f32[192,256]{1,0:T(8,128)S(1)}, f32[192,256]{1,0:T(8,128)S(1)}, u32[]{:S(2)}, u32[]{:S(2)}) collective-permute-start(f32[192,256]{1,0:T(8,128)S(1)} %slice_dynamic-update-slice_fusion.refs_0_), channel_id=1, source_target_pairs={{0,24},{8,16},{16,8},{24,0},{1,25},{9,17},{17,9},{25,1},{2,26},{10... | collective-permute-start | bytes 589832 | tf_op jit(solution)/shard_map/rows_members/ppermute | solution.py:542
  21.6 0.5 collective-permute-start.10
  22.1 0.0 collective-permute-done.2.beside
  22.1 0.5 collective-permute-start.9
  22.7 0.1 weights_kernel.1.weights.weights_in
  22.7 0.0 collective-permute-done.1.far.far_first
  22.8 0.0 collective-permute-done.near.near_first
  22.8 0.0 copy-done
  22.8 0.0 copy-done.1
  22.8 2.0 %first_kernel.1 = (f32[4,168,128]{2,1,0:T(8,128)S(1)}, f32[4,168,128]{2,1,0:T(8,128)S(1)}, f32[4,24,128]{2,1,0:T(8,128)S(1)}, f32[4,24,128]{2,1,0:T(8,128)S(1)}) custom-call(s32[4]{0:T(128)S(1)} %pad_add_fusion.index, f32[8,4]{1,0:T(8,128)S(1)} %get-tuple-element.31.ties, f32[4,176,128]{2,1,0:T(8,128)S(1)} %get-tuple-element.32.guess.guess_in, ...), custom_call_target="tpu_custom_call" | custom-call | flops 10000000000 | bytes 1 | tf_op jit(solution)/shard_map/first_kernel/pallas_call | solution.py:645
  24.8 3.4 %collective-permute-start.7 = (f32[4,24,128]{2,1,0:T(8,128)S(1)}, f32[4,24,128]{2,1,0:T(8,128)S(1)}, u32[]{:S(2)}, u32[]{:S(2)}) collective-permute-start(f32[4,24,128]{2,1,0:T(8,128)S(1)} %get-tuple-element.42), channel_id=1, source_target_pairs={{0,8},{8,16},{16,24},{1,9},{9,17},{17,25},{2,10},{10,18},{18,26},{... | collective-permute-start | bytes 147464 | tf_op jit(solution)/shard_map/partial_before/ppermute | solution.py:556
  28.2 1.3 %collective-permute-start.8 = (f32[4,24,128]{2,1,0:T(8,128)S(1)}, f32[4,24,128]{2,1,0:T(8,128)S(1)}, u32[]{:S(2)}, u32[]{:S(2)}) collective-permute-start(f32[4,24,128]{2,1,0:T(8,128)S(1)} %get-tuple-element.43), channel_id=1, source_target_pairs={{8,0},{16,8},{24,16},{9,1},{17,9},{25,17},{10,2},{18,10},{26,18},{... | collective-permute-start | bytes 147464 | tf_op jit(solution)/shard_map/partial_after/ppermute | solution.py:558
  29.5 2.1 %collective-permute-done.7.before = f32[4,24,128]{2,1,0:T(8,128)S(1)} collective-permute-done((f32[4,24,128]{2,1,0:T(8,128)S(1)}, f32[4,24,128]{2,1,0:T(8,128)S(1)}, u32[]{:S(2)}, u32[]{:S(2)}) %collective-permute-start.7) | collective-permute-done | bytes 49184 | tf_op jit(solution)/shard_map/partial_before/ppermute | solution.py:556
  31.6 2.6 %collective-permute-done.8.after = f32[4,24,128]{2,1,0:T(8,128)S(1)} collective-permute-done((f32[4,24,128]{2,1,0:T(8,128)S(1)}, f32[4,24,128]{2,1,0:T(8,128)S(1)}, u32[]{:S(2)}, u32[]{:S(2)}) %collective-permute-start.8) | collective-permute-done | bytes 49184 | tf_op jit(solution)/shard_map/partial_after/ppermute | solution.py:558
  34.2 0.0 collective-permute-done.11.refs_3_
  34.2 0.0 collective-permute-done.10.refs_2_
  34.2 0.0 collective-permute-done.9.refs_1_
  34.2 2.4 %owned_kernel.1 = (f32[4,184,128]{2,1,0:T(8,128)S(1)}, f32[4,176,128]{2,1,0:T(8,128)S(1)}, bf16[4,128,512]{2,1,0:T(8,128)(2,1)S(1)}, bf16[4,128,512]{2,1,0:T(8,1...) custom-call(s32[4]{0:T(128)S(1)} %pad_add_fusion.index, ...), custom_call_target="tpu_custom_call" | custom-call | flops 1 | bytes 1 | tf_op jit(solution)/shard_map/owned_kernel/pallas_call | solution.py:669
  36.6 0.7 collective-permute-start.13
  37.3 3.0 %collective-permute-start.12 = (f32[4,176,128]{2,1,0:T(8,128)S(1)}, f32[4,176,128]{2,1,0:T(8,128)S(1)}, u32[]{:S(2)}, u32[]{:S(2)}) collective-permute-start(f32[4,176,128]{2,1,0:T(8,128)S(1)} %get-tuple-element.49), channel_id=1, source_target_pairs={{0,1},{1,0},{2,3},{3,2},{4,5},{5,4},{6,7},{7,6},{8,9},{9,8},{10,11... | collective-permute-start | bytes 1081352 | tf_op jit(solution)/shard_map/residual_near/ppermute | solution.py:542
  40.3 3.5 %local_kernel.2.image = f32[4,176,128]{2,1,0:T(8,128)S(1)} custom-call(s32[4]{0:T(128)S(1)} %pad_add_fusion.index, f32[8,4]{1,0:T(8,128)S(1)} %get-tuple-element.31.ties, f32[4,184,128]{2,1,0:T(8,128)S(1)} %get-tuple-element.44.field.refs_0_.residual, f32[4,176,128]{2,1,0:T(8,128)S(1)} %get-tuple-element.45.diagonal, f32[4,512]{1,0:T(4,128)S(1)} %copy-done.1, ...), custom_call_target="tpu_custom_call" | custom-call | flops 1 | bytes 1 | tf_op jit(solution)/shard_map/local_kernel/pallas_call | solution.py:686
  43.8 0.0 collective-permute-done.13.far
  43.8 0.0 collective-permute-done.12.near
  43.8 1.0 %cross_kernel.2 = (f32[4,176,128]{2,1,0:T(8,128)S(1)}, f32[4,168,128]{2,1,0:T(8,128)S(1)}) custom-call(s32[4]{0:T(128)S(1)} %pad_add_fusion.index, f32[8,4]{1,0:T(8,128)S(1)} %get-tuple-element.31.ties, f32[4,176,128]{2,1,0:T(8,128)S(1)} %local_kernel.2.image, f32[4,176,128]{2,1,0:T(8,128)S(1)} %collective-permute-done.12.near, ...), custom_call_target="tpu_custom_call" | custom-call | flops 1 | bytes 1 | tf_op jit(solution)/shard_map/cross_kernel/pallas_call | solution.py:707
  44.8 0.7 collective-permute-start.15
  45.5 4.5 %collective-permute-start.14 = (f32[4,168,128]{2,1,0:T(8,128)S(1)}, f32[4,168,128]{2,1,0:T(8,128)S(1)}, u32[]{:S(2)}, u32[]{:S(2)}) collective-permute-start(f32[4,168,128]{2,1,0:T(8,128)S(1)} %get-tuple-element.52), channel_id=1, source_target_pairs={{0,1},{1,0},{2,3},{3,2},{4,5},{5,4},{6,7},{7,6},{8,9},{9,8},{10,11... | collective-permute-start | bytes 1032200 | tf_op jit(solution)/shard_map/image_near/ppermute | solution.py:542
  50.0 3.5 %local_kernel.3 = (f32[4,168,128]{2,1,0:T(8,128)S(1)}, f32[1,128]{1,0:T(1,128)S(1)}) custom-call(s32[4]{0:T(128)S(1)} %pad_add_fusion.index, f32[8,4]{1,0:T(8,128)S(1)} %get-tuple-element.31.ties, f32[4,176,128]{2,1,0:T(8,128)S(1)} %get-tuple-element.50.field.refs_0_.image, f32[4,176,128]{2,1,0:T(8,128)S(1)} %get-tuple-element.45.diagonal, ...), custom_call_target="tpu_custom_call" | custom-call | flops 1 | bytes 1 | tf_op jit(solution)/shard_map/local_kernel/pallas_call | solution.py:686
  53.5 0.0 collective-permute-done.15.far
  53.5 0.0 collective-permute-done.14.near
  53.5 1.2 %cross_kernel.3 = (f32[4,168,128]{2,1,0:T(8,128)S(1)}, f32[32,128]{1,0:T(8,128)S(1)}) custom-call(s32[4]{0:T(128)S(1)} %pad_add_fusion.index, f32[8,4]{1,0:T(8,128)S(1)} %get-tuple-element.31.ties, f32[4,168,128]{2,1,0:T(8,128)S(1)} %get-tuple-element.51.image, f32[4,168,128]{2,1,0:T(8,128)S(1)} %collective-permute-done.14.near, ...), custom_call_target="tpu_custom_call" | custom-call | flops 1 | bytes 1 | tf_op jit(solution)/shard_map/cross_kernel/pallas_call | solution.py:715
  54.7 14.0 %all_to_all.11 = f32[32,1,128]{2,1,0:T(1,128)S(1)} all-to-all(f32[32,1,128]{2,1,0:T(1,128)S(1)} %bitcast.12), channel_id=1, replica_groups=mesh['tm'=4,'area'=8] {'tm','area'}, dimensions={0} | all-to-all | bytes 32768 | tf_op jit(solution)/shard_map/all_to_all | solution.py:720
  68.7 1.4 %last_kernel.1 = (f32[42,4,512]{2,1,0:T(4,128)}, f32[42,4,512]{2,1,0:T(4,128)}) custom-call(f32[32,128]{1,0:T(8,128)S(1)} %bitcast.11, f32[4,176,128]{2,1,0:T(8,128)S(1)} %get-tuple-element.32.guess.guess_in, f32[4,184,128]{2,1,0:T(8,128)S(1)} %get-tuple-element.44.field.refs_0_.residual, f32[4,176,128]{2,1,0:T(8,128)S(1)} %get-tuple-element.50.field.refs_0_.image, ...), custom_call_target="tpu_custom_call" | custom-call | flops 1 | bytes 1 | tf_op jit(solution)/shard_map/last_kernel/pallas_call | solution.py:723
  (10 shorter events, 0.1 us)
Async XLA Ops:
  3.0 14.3 %collective-permute-start.3 = (f32[96,256]{1,0:T(8,128)S(1)}, f32[96,256]{1,0:T(8,128)S(1)}, u32[]{:S(2)}, u32[]{:S(2)}) collective-permute-start(f32[96,256]{1,0:T(8,128)S(1)} %get-tuple-element.35), channel_id=1, source_target_pairs={{0,2},{1,3},{2,0},{3,1},{4,6},{5,7},{6,4},{7,5},{8,10},{9,11},{10,... | collective-permute-start | bytes 294920 | tf_op jit(solution)/shard_map/rows_chips/ppermute | solution.py:542
  6.1 11.3 %collective-permute-start.4 = (f32[96,256]{1,0:T(8,128)S(1)}, f32[96,256]{1,0:T(8,128)S(1)}, u32[]{:S(2)}, u32[]{:S(2)}) collective-permute-start(f32[96,256]{1,0:T(8,128)S(1)} %get-tuple-element.36), channel_id=1, source_target_pairs={{0,4},{1,5},{2,6},{3,7},{4,0},{5,1},{6,2},{7,3},{8,12},{9,13},{10,... | collective-permute-start | bytes 294920 | tf_op jit(solution)/shard_map/rows_chips/ppermute | solution.py:542
  8.7 8.8 %collective-permute-start.5 = (f32[96,256]{1,0:T(8,128)S(1)}, f32[96,256]{1,0:T(8,128)S(1)}, u32[]{:S(2)}, u32[]{:S(2)}) collective-permute-start(f32[96,256]{1,0:T(8,128)S(1)} %get-tuple-element.37), channel_id=1, source_target_pairs={{0,6},{1,7},{2,4},{3,5},{4,2},{5,3},{6,0},{7,1},{8,14},{9,15},{10,... | collective-permute-start | bytes 294920 | tf_op jit(solution)/shard_map/rows_chips/ppermute | solution.py:542
  10.9 11.9 %collective-permute-start.1 = (f32[4,176,128]{2,1,0:T(8,128)S(1)}, f32[4,176,128]{2,1,0:T(8,128)S(1)}, u32[]{:S(2)}, u32[]{:S(2)}) collective-permute-start(f32[4,176,128]{2,1,0:T(8,128)S(1)} %get-tuple-element.32.guess.guess_in), channel_id=1, source_target_pairs={{1,2},{3,4},{5,6},{2,1},{4,3},{6,5},{9,10},{11,12},{13,14},{10,9},... | collective-permute-start | bytes 1081352 | tf_op jit(solution)/shard_map/guess_far/ppermute | solution.py:549
  11.6 11.2 %collective-permute-start = (f32[4,176,128]{2,1,0:T(8,128)S(1)}, f32[4,176,128]{2,1,0:T(8,128)S(1)}, u32[]{:S(2)}, u32[]{:S(2)}) collective-permute-start(f32[4,176,128]{2,1,0:T(8,128)S(1)} %get-tuple-element.32.guess.guess_in), channel_id=1, source_target_pairs={{0,1},{1,0},{2,3},{3,2},{4,5},{5,4},{6,7},{7,6},{8,9},{9,8},{10,11... | collective-permute-start | bytes 1081352 | tf_op jit(solution)/shard_map/guess_near/ppermute | solution.py:542
  13.9 8.9 %copy-start = (f32[4,512]{1,0:T(4,128)S(1)}, f32[4,512]{1,0:T(4,128)}, u32[]{:S(2)}) copy-start(f32[4,512]{1,0:T(4,128)} %coupling.9) | copy-start | bytes 24580
  13.9 8.9 %copy-start.1 = (f32[4,512]{1,0:T(4,128)S(1)}, f32[4,512]{1,0:T(4,128)}, u32[]{:S(2)}) copy-start(f32[4,512]{1,0:T(4,128)} %ramp.7) | copy-start | bytes 24580
  17.3 4.8 %collective-permute-start.2 = (f32[144,256]{1,0:T(8,128)S(1)}, f32[144,256]{1,0:T(8,128)S(1)}, u32[]{:S(2)}, u32[]{:S(2)}) collective-permute-start(f32[144,256]{1,0:T(8,128)S(1)} %get-tuple-element.34), channel_id=1, source_target_pairs={{0,1},{1,0},{2,3},{3,2},{4,5},{5,4},{6,7},{7,6},{8,9},{9,8},{10,11... | collective-permute-start | bytes 442376 | tf_op jit(solution)/shard_map/rows_beside/ppermute | solution.py:542
  17.5 1.5 %collective-permute-start.6 = (f32[144,256]{1,0:T(8,128)S(1)}, f32[144,256]{1,0:T(8,128)S(1)}, u32[]{:S(2)}, u32[]{:S(2)}) collective-permute-start(f32[144,256]{1,0:T(8,128)S(1)} %pad_maximum_fusion), channel_id=1, source_target_pairs={{0,1},{1,0},{2,3},{3,2},{4,5},{5,4},{6,7},{7,6},{8,9},{9,8},{10,11... | collective-permute-start | bytes 442376 | tf_op jit(solution)/shard_map/rows_cores/ppermute | solution.py:542
  19.1 15.1 %collective-permute-start.11 = (f32[192,256]{1,0:T(8,128)S(1)}, f32[192,256]{1,0:T(8,128)S(1)}, u32[]{:S(2)}, u32[]{:S(2)}) collective-permute-start(f32[192,256]{1,0:T(8,128)S(1)} %slice_dynamic-update-slice_fusion.refs_0_), channel_id=1, source_target_pairs={{0,24},{8,16},{16,8},{24,0},{1,25},{9,17},{17,9},{25,1},{2,26},{10... | collective-permute-start | bytes 589832 | tf_op jit(solution)/shard_map/rows_members/ppermute | solution.py:542
  21.6 12.6 %collective-permute-start.10 = (f32[192,256]{1,0:T(8,128)S(1)}, f32[192,256]{1,0:T(8,128)S(1)}, u32[]{:S(2)}, u32[]{:S(2)}) collective-permute-start(f32[192,256]{1,0:T(8,128)S(1)} %slice_dynamic-update-slice_fusion.refs_0_), channel_id=1, source_target_pairs={{0,16},{8,24},{16,0},{24,8},{1,17},{9,25},{17,1},{25,9},{2,18},{10... | collective-permute-start | bytes 589832 | tf_op jit(solution)/shard_map/rows_members/ppermute | solution.py:542
  22.1 12.1 %collective-permute-start.9 = (f32[192,256]{1,0:T(8,128)S(1)}, f32[192,256]{1,0:T(8,128)S(1)}, u32[]{:S(2)}, u32[]{:S(2)}) collective-permute-start(f32[192,256]{1,0:T(8,128)S(1)} %slice_dynamic-update-slice_fusion.refs_0_), channel_id=1, source_target_pairs={{0,8},{8,0},{16,24},{24,16},{1,9},{9,1},{17,25},{25,17},{2,10},{10... | collective-permute-start | bytes 589832 | tf_op jit(solution)/shard_map/rows_members/ppermute | solution.py:542
  24.8 6.8 %collective-permute-start.7 = (f32[4,24,128]{2,1,0:T(8,128)S(1)}, f32[4,24,128]{2,1,0:T(8,128)S(1)}, u32[]{:S(2)}, u32[]{:S(2)}) collective-permute-start(f32[4,24,128]{2,1,0:T(8,128)S(1)} %get-tuple-element.42), channel_id=1, source_target_pairs={{0,8},{8,16},{16,24},{1,9},{9,17},{17,25},{2,10},{10,18},{18,26},{... | collective-permute-start | bytes 147464 | tf_op jit(solution)/shard_map/partial_before/ppermute | solution.py:556
  28.2 6.0 %collective-permute-start.8 = (f32[4,24,128]{2,1,0:T(8,128)S(1)}, f32[4,24,128]{2,1,0:T(8,128)S(1)}, u32[]{:S(2)}, u32[]{:S(2)}) collective-permute-start(f32[4,24,128]{2,1,0:T(8,128)S(1)} %get-tuple-element.43), channel_id=1, source_target_pairs={{8,0},{16,8},{24,16},{9,1},{17,9},{25,17},{10,2},{18,10},{26,18},{... | collective-permute-start | bytes 147464 | tf_op jit(solution)/shard_map/partial_after/ppermute | solution.py:558
  36.6 7.2 %collective-permute-start.13 = (f32[4,176,128]{2,1,0:T(8,128)S(1)}, f32[4,176,128]{2,1,0:T(8,128)S(1)}, u32[]{:S(2)}, u32[]{:S(2)}) collective-permute-start(f32[4,176,128]{2,1,0:T(8,128)S(1)} %get-tuple-element.49), channel_id=1, source_target_pairs={{1,2},{3,4},{5,6},{2,1},{4,3},{6,5},{9,10},{11,12},{13,14},{10,9},... | collective-permute-start | bytes 1081352 | tf_op jit(solution)/shard_map/residual_far/ppermute | solution.py:549
  37.3 6.5 %collective-permute-start.12 = (f32[4,176,128]{2,1,0:T(8,128)S(1)}, f32[4,176,128]{2,1,0:T(8,128)S(1)}, u32[]{:S(2)}, u32[]{:S(2)}) collective-permute-start(f32[4,176,128]{2,1,0:T(8,128)S(1)} %get-tuple-element.49), channel_id=1, source_target_pairs={{0,1},{1,0},{2,3},{3,2},{4,5},{5,4},{6,7},{7,6},{8,9},{9,8},{10,11... | collective-permute-start | bytes 1081352 | tf_op jit(solution)/shard_map/residual_near/ppermute | solution.py:542
  44.8 8.7 %collective-permute-start.15 = (f32[4,168,128]{2,1,0:T(8,128)S(1)}, f32[4,168,128]{2,1,0:T(8,128)S(1)}, u32[]{:S(2)}, u32[]{:S(2)}) collective-permute-start(f32[4,168,128]{2,1,0:T(8,128)S(1)} %get-tuple-element.52), channel_id=1, source_target_pairs={{1,2},{3,4},{5,6},{2,1},{4,3},{6,5},{9,10},{11,12},{13,14},{10,9},... | collective-permute-start | bytes 1032200 | tf_op jit(solution)/shard_map/image_far/ppermute | solution.py:549
  45.5 8.0 %collective-permute-start.14 = (f32[4,168,128]{2,1,0:T(8,128)S(1)}, f32[4,168,128]{2,1,0:T(8,128)S(1)}, u32[]{:S(2)}, u32[]{:S(2)}) collective-permute-start(f32[4,168,128]{2,1,0:T(8,128)S(1)} %get-tuple-element.52), channel_id=1, source_target_pairs={{0,1},{1,0},{2,3},{3,2},{4,5},{5,4},{6,7},{7,6},{8,9},{9,8},{10,11... | collective-permute-start | bytes 1032200 | tf_op jit(solution)/shard_map/image_near/ppermute | solution.py:542

commit v3 on v2

--- a/solution.py
+++ b/solution.py
@@ -116,23 +116,54 @@
     return owner_row * cap + jnp.sum(same, axis=0, keepdims=True)
 
 
+def chip_steps(chips, core):
+    return [k % (chips - 1) + 1 for k in range(core, chips - 1 + core)]
+
+
+def member_steps(members, core):
+    steps = list(range(members))
+    return steps[:1] + steps[2:0:-1] + steps[3:] if core else steps
+
+
+def by_core(steps_of, count, core):
+    return [jnp.where(core == 1, b, a) for a, b in zip(steps_of(count, 0), steps_of(count, 1))]
+
+
+def selected(position, values):
+    total = values[0]
+    for k, value in enumerate(values[1:]):
+        total = jnp.where(position == k + 1, value, total)
+    return total
+
+
 def marks_of(keys, area, rank, cap):
     return jnp.where((area * cap + rank).astype(F32) == keys, 1.0, 0.0).astype(BF16)
 
 
-def pack_kernel(span, cap, hours, index, owner_far, sens_far, weight_far, *outs):
-    *away, here, other, owner, sens, weight, semaphores = outs
-    copies = fetch((owner_far, sens_far, weight_far), (owner, sens, weight), semaphores)
+def pack_kernel(span, cap, index, *refs):
+    *away, here, beside, guess_out = refs[5:-6]
+    owner, sens, weight, guess, coupling, semaphores = refs[-6:]
+    copies = fetch(refs[:5], refs[-6:-1], semaphores)
+    hours = weight.shape[0]
     chip, core, member = index[0], index[1], index[2]
     blocks = owner.shape[1]
     parts = sens.shape[1] // WIDE
     copies[0].wait()
     keys = keys_of(owner, cap)
     slot = lax.broadcasted_iota(jnp.int32, (2 * cap * (len(away) + 1), blocks), 0)
-    group = (chip ^ (slot // (2 * cap))) * 2 + (core ^ (slot // cap % 2))
+    chip_step = selected(
+        slot // (2 * cap), [jnp.int32(0)] + by_core(chip_steps, len(away) + 1, core)
+    )
+    group = (chip ^ chip_step) * 2 + (core ^ (slot // cap % 2))
     local = lax.broadcasted_iota(jnp.int32, (2 * span * cap, blocks), 0)
     local_group = chip * 2 + (core ^ (local // (span * cap)))
-    local_area = local_group * span + (member ^ (local // cap % span))
+    other = local // (span * cap) == 1
+    member_step = jnp.where(
+        other,
+        selected(local // cap % span, by_core(member_steps, span, 1 - core)),
+        selected(local // cap % span, by_core(member_steps, span, core)),
+    )
+    local_area = local_group * span + (member ^ member_step)
     sens_marks = jnp.concatenate(
         [
             marks_of(keys, group * span + member, slot % cap, cap)[2 * cap :],
@@ -167,62 +198,61 @@
                 away[k][pl.ds(at + cap * part, cap), :] = rows[row : row + cap, lanes]
             away[k][pl.ds(at + cap * parts, cap), :] = weights[2 * cap + row :][:cap]
     count = span * cap
-    for core_step, out in ((0, here), (1, other)):
+    for core_step, out in ((0, here), (1, beside)):
         row = 2 * cap * len(away) + count * core_step
         for part in range(parts):
             lanes = slice(WIDE * part, WIDE * (part + 1))
             out[pl.ds(count * part, count), :] = rows[row : row + count, lanes]
         out[pl.ds(count * parts, cap), :] = weights[cap * core_step :][:cap]
-
-
-def fields_kernel(barrier, *refs):
-    guess_out, right_out, diagonal_out = refs[-9:-6]
-    guess, gradient, slack, hess, coupling, semaphores = landed = refs[-6:]
-    for copy in fetch(refs[:5], landed[:5], semaphores):
+    for copy in copies[3:]:
         copy.wait()
     hours, span, width = guess.shape
     rows = hours * span
     shape = (rows, LANES)
     for k in range(width // LANES):
         lanes = pl.ds(LANES * k, LANES)
-        slack_rows = slack[:, :, lanes].reshape(shape)
         guess_out[k, pl.ds(0, rows), :] = guess[:, :, lanes].reshape(shape)
         guess_out[k, pl.ds(rows, span), :] = coupling[:, LANES * k : LANES * (k + 1)]
         guess_out[k, pl.ds(rows + span, span), :] = jnp.zeros((span, LANES), F32)
+
+
+def prepare_kernel(index, barrier, *refs):
+    tile_high, tile_low, right_out, diagonal_out, ties = refs[-12:-7]
+    gradient, slack, hess, offsets, gains, tile, semaphores = refs[-7:]
+    span = tile.shape[0]
+    copies = fetch(
+        refs[:5] + tuple(refs[5].at[i] for i in range(span)),
+        (gradient, slack, hess, offsets, gains) + tuple(tile.at[i] for i in range(span)),
+        semaphores,
+    )
+    for copy in copies[:5]:
+        copy.wait()
+    hours, span, width = slack.shape
+    shape = (hours * span, LANES)
+    for k in range(width // LANES):
+        lanes = pl.ds(LANES * k, LANES)
+        slack_rows = slack[:, :, lanes].reshape(shape)
         right_out[k] = barrier[0] / slack_rows - gradient[:, :, lanes].reshape(shape)
         diagonal_out[k] = hess[:, :, lanes].reshape(shape) + barrier[0] / (
             slack_rows * slack_rows
         )
-
-
-def halves_kernel(index, tile_far, offsets_far, gains_far, after, *refs):
-    tile_high, tile_low, ties, offsets, gains, tile, semaphores = refs
-    span = tile.shape[0]
-    each = [tile_far.at[i] for i in range(span)]
-    copies = fetch(
-        [offsets_far, gains_far] + each,
-        [offsets, gains] + [tile.at[i] for i in range(span)],
-        semaphores,
-    )
-    copies[0].wait()
-    copies[1].wait()
     first = (index[0] * 2 + index[1] - 1) * span
     for i in range(2 * span):
         area = jnp.maximum(first + i, 0)
         for step in range(span):
-            total = 0.0
-            for k in range(offsets.shape[0]):
-                total = total + jnp.where(offsets[k, area] == step + 1, gains[k, area], 0.0)
-            ties[i, step] = total
+            ties[i, step] = 0.0
+        for k in range(offsets.shape[0]):
+            step = offsets[k, area] - 1
+            ties[i, step] = ties[i, step] + gains[k, area]
     for i in range(span):
-        copies[2 + i].wait()
+        copies[5 + i].wait()
         high, low = two_parts(tile[i])
         tile_high[i] = high
         tile_low[i] = low
 
 
-def weights_kernel(span, cap, here, beside, crossed, *refs):
-    *arrived, weights = refs
+def weights_kernel(span, cap, deep, here, beside, crossed, *refs):
+    *arrived, weights, outer = refs
     hours = weights.shape[1]
     chunk = arrived[0].shape[0] // 2
     pieces = [ref[pl.ds(ref.shape[0] - cap, cap), :] for ref in (here, beside)]
@@ -234,6 +264,12 @@
         turned = jnp.transpose(by_slot[:, LANES * pair : LANES * (pair + 1)])
         for half in range(2):
             weights[2 * pair + half] = turned[HOUR_LANES * half :][:hours]
+    for j in range(2 * deep):
+        hour = j if j < deep else hours - 2 * deep + j
+        for area in range(span):
+            outer[
+                pl.ds(span // 2 * j + area // 2, 1), pl.ds(LANES * (area % 2), LANES)
+            ] = weights[area, pl.ds(hour, 1), :]
 
 
 def upper(ties, span, i, j):
@@ -289,7 +325,6 @@
     diagonal_in,
     near,
     far,
-    weights,
     tile_high,
     tile_low,
     ramp,
@@ -338,9 +373,6 @@
                 start = 0 if low else rows - count
                 out[k, pl.ds(at, count), :] = source[k, pl.ds(start, count), :]
                 at += count
-            start = 0 if low else hours - deep
-            out[k, pl.ds(at, deep), :] = weights[k, pl.ds(start, deep), :]
-            out[k, pl.ds(at + deep, deep), :] = jnp.zeros((deep, LANES), F32)
 
 
 def security(own, high, low, weight):
@@ -398,16 +430,39 @@
             partial[k, target, :] = (
                 partial[k, target, :] + edge * guess[k, pl.ds(span * other, span), :]
             )
+    steps = by_core(member_steps, span, index[1])
+    count = pieces[0].shape[0] - span * deep
+
+    def outer_hours(area, other, first):
+        total = jnp.zeros((deep, LANES), F32)
+        for step in range(1, span):
+            value = jnp.concatenate(
+                [
+                    pieces[step][
+                        pl.ds(count + span // 2 * (first + j) + area // 2, 1),
+                        pl.ds(LANES * (area % 2), LANES),
+                    ]
+                    for j in range(deep)
+                ],
+                axis=0,
+            )
+            total = jnp.where(index[2] ^ steps[step] == other, value, total)
+        return total
+
     for area in range(span):
         weights[area] = jnp.concatenate(
-            [before[area, pl.ds(at, deep), :], weights_in[area], after[area, pl.ds(at, deep), :]],
+            [
+                outer_hours(area, index[2] - 1, deep),
+                weights_in[area],
+                outer_hours(area, index[2] + 1, 0),
+            ],
             axis=0,
         )
     parts = guess.shape[0] * LANES // WIDE
-    group = pieces[0].shape[0] // (parts * cap)
+    group = count // (parts * cap)
     terms = []
     for step in range(span):
-        area = index[2] ^ step
+        area = index[2] ^ steps[step]
         wide = []
         for part in range(parts):
             at = cap * (span * part + step)
@@ -422,7 +477,7 @@
         term = security(take(guess, area, span), high, low, weights[area])
         terms.append(take(partial, area, span) - term)
     for step in range(span):
-        put(residual, index[2] ^ step, span, terms[step])
+        put(residual, index[2] ^ steps[step], span, terms[step])
     clear_outside(index, residual, deep * span)
     for k in range(sent.shape[0]):
         sent[k] = residual[k, pl.ds(span, sent.shape[1]), :]
@@ -450,6 +505,7 @@
     else:
         (image,) = refs
     hours = image.shape[1] // span
+    steps = by_core(member_steps, span, index[1])
     for i in range(span):
         value = (
             take(diagonal, i, span, skip - 1, hours) * take(field, i, span, 1, hours)
@@ -460,12 +516,12 @@
         put(image, i, span, value)
     terms = []
     for step in range(span):
-        area = index[2] ^ step
+        area = index[2] ^ steps[step]
         weight = weights[area][skip : skip + hours]
         own = take(field, area, span, 1, hours)
         terms.append(security(own, sens_high[step], sens_low[step], weight))
     for step in range(span):
-        area = index[2] ^ step
+        area = index[2] ^ steps[step]
         put(image, area, span, take(image, area, span) + terms[step])
     if with_sums:
         count = image.shape[1]
@@ -540,6 +596,21 @@
     count = lax.axis_size(axis)
     with jax.named_scope(name):
         return lax.ppermute(value, axis, [(i, i ^ step) for i in range(count)])
+
+
+def swap_by_core(value, axis, steps_of, position, name):
+    members, groups = lax.axis_size("tm"), lax.axis_size("area")
+    pairs = []
+    for member in range(members):
+        for group in range(groups):
+            if axis == "tm":
+                other = (member ^ steps_of(members, group % 2)[position]) * groups + group
+            else:
+                step = steps_of(groups // 2, group % 2)[position]
+                other = member * groups + (group ^ (2 * step))
+            pairs.append((member * groups + group, other))
+    with jax.named_scope(name):
+        return lax.ppermute(value, ("tm", "area"), pairs)
 
 
 def exchange(field, name):
@@ -595,40 +666,38 @@
     parts = width // WIDE
     chunk = (parts + 1) * cap
     local = (parts * span + 1) * cap
-    *away, here, other = call(
-        functools.partial(pack_kernel, span, cap, hours),
+    field_shape = f32_shape(blocks, rows, LANES)
+    sources = (owner, con_sens, weight, step_guess, bus_coupling)
+    *away, here, other, guess = call(
+        functools.partial(pack_kernel, span, cap),
         [f32_shape(2 * chunk, WIDE)] * (chips - 1)
-        + [f32_shape(local, WIDE)] * 2,
-        [SCALARS] + [IN_HBM] * 3,
-        landing(owner, con_sens, weight),
-    )(index, *in_hbm(owner, con_sens, weight))
-    arrived = [swap(a, "area", 2 * (k + 1), "rows_chips") for k, a in enumerate(away)]
+        + [f32_shape(local, WIDE)] * 2
+        + [f32_shape(blocks, rows + 2 * span, LANES)],
+        [SCALARS] + [IN_HBM] * 5,
+        landing(*sources),
+    )(index, *in_hbm(*sources))
+    arrived = [
+        swap_by_core(a, "area", chip_steps, k, "rows_chips") for k, a in enumerate(away)
+    ]
     beside = swap(other, "area", 1, "rows_beside")
     crossed = swap(jnp.concatenate([a[chunk:] for a in arrived], axis=0), "area", 1, "rows_cores")
-    field_shape = f32_shape(blocks, rows, LANES)
-    natural = (step_guess, gradient, slack, hess_diag)
-    guess, right_side, diagonal_in = call(
-        fields_kernel,
-        [f32_shape(blocks, rows + 2 * span, LANES), field_shape, field_shape],
-        [SCALARS] + [IN_HBM] * 5 + [UNREAD],
-        landing(*natural, bus_coupling),
-    )(barrier, *in_hbm(*natural, bus_coupling), here)
+    tile_shape = jax.ShapeDtypeStruct(tile.shape, BF16)
+    natural = (gradient, slack, hess_diag)
+    tables = (tie_offset.T, tie_admittance.T)
+    tile_high, tile_low, right_side, diagonal_in, ties = call(
+        prepare_kernel,
+        [tile_shape, tile_shape, field_shape, field_shape, f32_shape(2 * span, span)],
+        [SCALARS] * 2 + [IN_HBM] * 6 + [UNREAD],
+        [pltpu.VMEM(a.shape, F32) for a in natural]
+        + [pltpu.SMEM(a.shape, a.dtype) for a in tables]
+        + [pltpu.VMEM(tile.shape, F32), pltpu.SemaphoreType.DMA((5 + span,))],
+        out_specs=[WHOLE] * 4 + [SCALARS],
+    )(index, barrier, *in_hbm(*natural, *tables, tile), here)
     near_guess, far_guess = exchange(guess, "guess")
 
-    tile_shape = jax.ShapeDtypeStruct(tile.shape, BF16)
-    tables = (tie_offset.T, tie_admittance.T)
-    tile_high, tile_low, ties = call(
-        halves_kernel,
-        [tile_shape, tile_shape, f32_shape(2 * span, span)],
-        [SCALARS] + [IN_HBM] * 3 + [UNREAD],
-        [pltpu.SMEM(a.shape, a.dtype) for a in tables]
-        + [pltpu.VMEM(tile.shape, F32), pltpu.SemaphoreType.DMA((2 + span,))],
-        out_specs=[WHOLE, WHOLE, SCALARS],
-    )(index, *in_hbm(tile, *tables), right_side)
-
-    weights = call(
-        functools.partial(weights_kernel, span, cap),
-        f32_shape(span, hours, slots),
+    weights, outer = call(
+        functools.partial(weights_kernel, span, cap, deep),
+        [f32_shape(span, hours, slots), f32_shape(span * deep, WIDE)],
         [WHOLE] * (3 + len(arrived)),
     )(here, beside, crossed, *arrived)
     piece = jnp.concatenate(
@@ -636,16 +705,19 @@
             a[at : at + parts * cap]
             for k, ref in enumerate(arrived)
             for a, at in ((ref, 0), (crossed, chunk * k))
-        ],
+        ]
+        + [outer],
         axis=0,
     )
-    pieces = [piece] + [swap(piece, "tm", step, "rows_members") for step in range(1, members)]
-
-    edge_rows = (3 * deep - 1) * span + 2 * deep
+    pieces = [piece] + [
+        swap_by_core(piece, "tm", member_steps, k, "rows_members") for k in range(1, members)
+    ]
+
+    edge_rows = (3 * deep - 1) * span
     partial, diagonal, up, down = call(
         functools.partial(first_kernel, span, deep),
         [field_shape] * 2 + [f32_shape(blocks, edge_rows, LANES)] * 2,
-        [SCALARS] * 2 + [WHOLE] * 10,
+        [SCALARS] * 2 + [WHOLE] * 9,
         flops=FIRST,
     )(
         index,
@@ -655,7 +727,6 @@
         diagonal_in,
         near_guess,
         far_guess,
-        weights,
         tile_high,
         tile_low,
         ramp_weight,

time: 70.3 us -> 69.3 us (0.986)
  Pallas kernels: 22.2 us -> 21.2 us
    ppermute x11 -> x5, starting transfers between devices: 19.7 us -> 10.4 us  [swap(): return lax.ppermute(value, axis, [(i, i ^ step) for i in range(count)])]
    ppermute x0 -> x6, starting transfers between devices: none -> 9.25 us  [swap_by_core(): return lax.ppermute(value, ('tm', 'area'), pairs)]
    pallas_call x4 -> x3, Pallas kernels: 7.32 us -> 6.2 us  [the longest x1 3.77 us: body(): call(prepare_kernel, [tile_shape, tile_shape, field_shape, field_shape, f...]
  transfers between devices with their start and end apart: 16 -> 16, of which waited for: 3 -> 3; matrix products, arithmetic and copies ran while one was open for 0% -> 0% of each run, Pallas kernels for 20% -> 19%
where the time goes in v3:
time: 69.3 us; the launch traced here: 69 us
  starting transfers between devices  26.4 us (38%)
  Pallas kernels  21.2 us (31%)
  blocking collectives  14 us (20%)
  waiting for transfers between devices  5.72 us (8%)
  between operations  1.56 us (2%)
    all_to_all x1, blocking collectives, body(): lax.all_to_all(spread, ('tm', 'area'), split_axis=0, concat_axis=0, tiled...  14 us
    ppermute x5, starting transfers between devices, swap(): return lax.ppermute(value, axis, [(i, i ^ step) for i in range(count)])  10.4 us
    ppermute x6, starting transfers between devices, swap_by_core(): return lax.ppermute(value, ('tm', 'area'), pairs)  9.25 us
    pallas_call x2, Pallas kernels, local_image(): call(functools.partial(local_kernel, span, skip, summed), (shape, f32_sha...  6.98 us
    pallas_call x1, Pallas kernels, body(): call(prepare_kernel, [tile_shape, tile_shape, field_shape, field_shape, f...  3.77 us
    ppermute x1, starting transfers between devices, adjacent_hours(): before = lax.ppermute(up, 'tm', ups)  3.39 us
    ppermute x1, waiting for transfers between devices, adjacent_hours(): before = lax.ppermute(up, 'tm', ups)  2.46 us
    pallas_call x1, Pallas kernels, body(): call(functools.partial(owned_kernel, span, cap, deep), [deep_shape, next_...  2.39 us
  transfers between devices with their start and end apart: 16, of which 3 were waited for; matrix products, arithmetic and copies ran while one was open for 0% of the time, Pallas kernels for 19%

profile of v3, /device:TPU:0, one launch (start us, length us, event | category | flops | bytes accessed | tf_op | source)
XLA Modules:
  0.0 69.0 jit_solution(6722093722250541001)
XLA Ops:
  0.6 0.1 pad_add_fusion.index
  0.7 2.3 %pack_kernel.1 = (f32[96,256]{1,0:T(8,128)S(1)}, f32[96,256]{1,0:T(8,128)S(1)}, f32[96,256]{1,0:T(8,128)S(1)}, f32[144,256]{1,0:T(8,128)S(1)}, f32[144,256]{1,0:T(8,128)S(1)}, /*index=5*/f32[4,176,128]{2,1,0:T(8,128)S(1)}) custom-call(s32[4]{0:T(128)S(1)} %pad_add_fusion.index, s32[1,256]{1,0:T(1,128)} %bitcast.16, f32[256,512]{1,0:T(8,128)} %refs_1_.2, ...), custom_call_target="tpu_custom_call" | custom-call | flops 1 | bytes 1 | tf_op jit(solution)/shard_map/pack_kernel/pallas_call | solution.py:671
  3.1 3.1 %collective-permute-start.3 = (f32[96,256]{1,0:T(8,128)S(1)}, f32[96,256]{1,0:T(8,128)S(1)}, u32[]{:S(2)}, u32[]{:S(2)}) collective-permute-start(f32[96,256]{1,0:T(8,128)S(1)} %get-tuple-element.41), channel_id=1, source_target_pairs={{0,2},{1,5},{2,0},{3,7},{4,6},{5,1},{6,4},{7,3},{8,10},{9,13},{10,... | collective-permute-start | bytes 294920 | tf_op jit(solution)/shard_map/rows_chips/ppermute | solution.py:613
  6.2 2.6 %collective-permute-start.4 = (f32[96,256]{1,0:T(8,128)S(1)}, f32[96,256]{1,0:T(8,128)S(1)}, u32[]{:S(2)}, u32[]{:S(2)}) collective-permute-start(f32[96,256]{1,0:T(8,128)S(1)} %get-tuple-element.42), channel_id=1, source_target_pairs={{0,4},{1,7},{2,6},{3,5},{4,0},{5,3},{6,2},{7,1},{8,12},{9,15},{10,... | collective-permute-start | bytes 294920 | tf_op jit(solution)/shard_map/rows_chips/ppermute | solution.py:613
  8.7 0.0 collective-permute-start.5
  8.7 0.7 collective-permute-start.1
  9.4 2.3 %collective-permute-start = (f32[4,176,128]{2,1,0:T(8,128)S(1)}, f32[4,176,128]{2,1,0:T(8,128)S(1)}, u32[]{:S(2)}, u32[]{:S(2)}) collective-permute-start(f32[4,176,128]{2,1,0:T(8,128)S(1)} %get-tuple-element.33.guess.guess_in), channel_id=1, source_target_pairs={{0,1},{1,0},{2,3},{3,2},{4,5},{5,4},{6,7},{7,6},{8,9},{9,8},{10,11... | collective-permute-start | bytes 1081352 | tf_op jit(solution)/shard_map/guess_near/ppermute | solution.py:598
  12.4 0.0 copy-start
  12.4 0.0 copy-start.1
  12.4 3.8 %prepare_kernel.1 = (bf16[4,512,512]{2,1,0:T(8,128)(2,1)S(1)}, bf16[4,512,512]{2,1,0:T(8,128)(2,1)S(1)}, f32[4,168,128]{2,1,0:T(8,128)S(1)}, f32[4,168,128]{2,1,0:T(8,128)S(1)}, f32[8,4]{1,0:T(8,128)S(1)}) custom-call(s32[4]{0:T(128)S(1)} %pad_add_fusion.index, f32[1]{0:T(128)S(6)} %copy.22.barrier, f32[42,4,512]{2,1,0:T(4,128)} %refs_0_.1, ...), custom_call_target="tpu_custom_call" | custom-call | flops 1 | bytes 1 | tf_op jit(solution)/shard_map/prepare_kernel/pallas_call | solution.py:687
  16.2 0.0 collective-permute-done.3.refs_0_
  16.2 0.1 collective-permute-start.2
  16.3 0.0 collective-permute-done.4.refs_1_
  16.3 0.0 collective-permute-done.5.refs_2_
  16.4 0.5 collective-permute-start.6
  16.9 1.0 %collective-permute-done.6.crossed = f32[144,256]{1,0:T(8,128)S(1)} collective-permute-done((f32[144,256]{1,0:T(8,128)S(1)}, f32[144,256]{1,0:T(8,128)S(1)}, u32[]{:S(2)}, u32[]{:S(2)}) %collective-permute-start.6) | collective-permute-done | bytes 147488 | tf_op jit(solution)/shard_map/rows_cores/ppermute | solution.py:598
  17.9 0.0 collective-permute-done.2.beside
  17.9 0.1 weights_kernel.1
  18.1 2.5 %collective-permute-start.11 = (f32[200,256]{1,0:T(8,128)S(1)}, f32[200,256]{1,0:T(8,128)S(1)}, u32[]{:S(2)}, u32[]{:S(2)}) collective-permute-start(f32[200,256]{1,0:T(8,128)S(1)} %constant_dynamic-update-slice_fusion.refs_0_), channel_id=1, source_target_pairs={{0,24},{1,25},{2,26},{3,27},{4,28},{5,29},{6,30},{7,31},{8,16},{9,... | collective-permute-start | bytes 614408 | tf_op jit(solution)/shard_map/rows_members/ppermute | solution.py:613
  20.6 0.5 collective-permute-start.10
  21.1 0.5 collective-permute-start.9
  21.6 0.0 collective-permute-done.1.far.far_first
  21.6 0.0 collective-permute-done.near.near_first
  21.6 0.0 copy-done
  21.6 0.0 copy-done.1
  21.7 2.1 %first_kernel.1 = (f32[4,168,128]{2,1,0:T(8,128)S(1)}, f32[4,168,128]{2,1,0:T(8,128)S(1)}, f32[4,20,128]{2,1,0:T(8,128)S(1)}, f32[4,20,128]{2,1,0:T(8,128)S(1)}) custom-call(s32[4]{0:T(128)S(1)} %pad_add_fusion.index, f32[8,4]{1,0:T(8,128)S(1)} %get-tuple-element.32.ties, f32[4,176,128]{2,1,0:T(8,128)S(1)} %get-tuple-element.33.guess.guess_in, ...), custom_call_target="tpu_custom_call" | custom-call | flops 10000000000 | bytes 1 | tf_op jit(solution)/shard_map/first_kernel/pallas_call | solution.py:717
  23.8 3.4 %collective-permute-start.7 = (f32[4,20,128]{2,1,0:T(8,128)S(1)}, f32[4,20,128]{2,1,0:T(8,128)S(1)}, u32[]{:S(2)}, u32[]{:S(2)}) collective-permute-start(f32[4,20,128]{2,1,0:T(8,128)S(1)} %get-tuple-element.45), channel_id=1, source_target_pairs={{0,8},{8,16},{16,24},{1,9},{9,17},{17,25},{2,10},{10,18},{18,26},{... | collective-permute-start | bytes 122888 | tf_op jit(solution)/shard_map/partial_before/ppermute | solution.py:627
  27.2 1.3 %collective-permute-start.8 = (f32[4,20,128]{2,1,0:T(8,128)S(1)}, f32[4,20,128]{2,1,0:T(8,128)S(1)}, u32[]{:S(2)}, u32[]{:S(2)}) collective-permute-start(f32[4,20,128]{2,1,0:T(8,128)S(1)} %get-tuple-element.46), channel_id=1, source_target_pairs={{8,0},{16,8},{24,16},{9,1},{17,9},{25,17},{10,2},{18,10},{26,18},{... | collective-permute-start | bytes 122888 | tf_op jit(solution)/shard_map/partial_after/ppermute | solution.py:629
  28.5 2.5 %collective-permute-done.7.before = f32[4,20,128]{2,1,0:T(8,128)S(1)} collective-permute-done((f32[4,20,128]{2,1,0:T(8,128)S(1)}, f32[4,20,128]{2,1,0:T(8,128)S(1)}, u32[]{:S(2)}, u32[]{:S(2)}) %collective-permute-start.7) | collective-permute-done | bytes 40992 | tf_op jit(solution)/shard_map/partial_before/ppermute | solution.py:627
  30.9 2.2 %collective-permute-done.8.after = f32[4,20,128]{2,1,0:T(8,128)S(1)} collective-permute-done((f32[4,20,128]{2,1,0:T(8,128)S(1)}, f32[4,20,128]{2,1,0:T(8,128)S(1)}, u32[]{:S(2)}, u32[]{:S(2)}) %collective-permute-start.8) | collective-permute-done | bytes 40992 | tf_op jit(solution)/shard_map/partial_after/ppermute | solution.py:629
  33.2 0.0 collective-permute-done.11.refs_3_
  33.2 0.0 collective-permute-done.10.refs_2_
  33.2 0.0 collective-permute-done.9.refs_1_
  33.2 2.4 %owned_kernel.1 = (f32[4,184,128]{2,1,0:T(8,128)S(1)}, f32[4,176,128]{2,1,0:T(8,128)S(1)}, bf16[4,128,512]{2,1,0:T(8,128)(2,1)S(1)}, bf16[4,128,512]{2,1,0:T(8,1...) custom-call(s32[4]{0:T(128)S(1)} %pad_add_fusion.index, ...), custom_call_target="tpu_custom_call" | custom-call | flops 1 | bytes 1 | tf_op jit(solution)/shard_map/owned_kernel/pallas_call | solution.py:740
  35.6 0.7 collective-permute-start.13
  36.3 3.0 %collective-permute-start.12 = (f32[4,176,128]{2,1,0:T(8,128)S(1)}, f32[4,176,128]{2,1,0:T(8,128)S(1)}, u32[]{:S(2)}, u32[]{:S(2)}) collective-permute-start(f32[4,176,128]{2,1,0:T(8,128)S(1)} %get-tuple-element.53), channel_id=1, source_target_pairs={{0,1},{1,0},{2,3},{3,2},{4,5},{5,4},{6,7},{7,6},{8,9},{9,8},{10,11... | collective-permute-start | bytes 1081352 | tf_op jit(solution)/shard_map/residual_near/ppermute | solution.py:598
  39.2 3.5 %local_kernel.2.image = f32[4,176,128]{2,1,0:T(8,128)S(1)} custom-call(s32[4]{0:T(128)S(1)} %pad_add_fusion.index, f32[8,4]{1,0:T(8,128)S(1)} %get-tuple-element.32.ties, f32[4,184,128]{2,1,0:T(8,128)S(1)} %get-tuple-element.48.field.refs_0_.residual, f32[4,176,128]{2,1,0:T(8,128)S(1)} %get-tuple-element.49.diagonal, f32[4,512]{1,0:T(4,128)S(1)} %copy-done.1, ...), custom_call_target="tpu_custom_call" | custom-call | flops 1 | bytes 1 | tf_op jit(solution)/shard_map/local_kernel/pallas_call | solution.py:757
  42.7 0.0 collective-permute-done.13.far
  42.7 0.0 collective-permute-done.12.near
  42.8 1.0 %cross_kernel.2 = (f32[4,176,128]{2,1,0:T(8,128)S(1)}, f32[4,168,128]{2,1,0:T(8,128)S(1)}) custom-call(s32[4]{0:T(128)S(1)} %pad_add_fusion.index, f32[8,4]{1,0:T(8,128)S(1)} %get-tuple-element.32.ties, f32[4,176,128]{2,1,0:T(8,128)S(1)} %local_kernel.2.image, f32[4,176,128]{2,1,0:T(8,128)S(1)} %collective-permute-done.12.near, ...), custom_call_target="tpu_custom_call" | custom-call | flops 1 | bytes 1 | tf_op jit(solution)/shard_map/cross_kernel/pallas_call | solution.py:778
  43.7 0.7 collective-permute-start.15
  44.4 4.5 %collective-permute-start.14 = (f32[4,168,128]{2,1,0:T(8,128)S(1)}, f32[4,168,128]{2,1,0:T(8,128)S(1)}, u32[]{:S(2)}, u32[]{:S(2)}) collective-permute-start(f32[4,168,128]{2,1,0:T(8,128)S(1)} %get-tuple-element.56), channel_id=1, source_target_pairs={{0,1},{1,0},{2,3},{3,2},{4,5},{5,4},{6,7},{7,6},{8,9},{9,8},{10,11... | collective-permute-start | bytes 1032200 | tf_op jit(solution)/shard_map/image_near/ppermute | solution.py:598
  49.0 3.5 %local_kernel.3 = (f32[4,168,128]{2,1,0:T(8,128)S(1)}, f32[1,128]{1,0:T(1,128)S(1)}) custom-call(s32[4]{0:T(128)S(1)} %pad_add_fusion.index, f32[8,4]{1,0:T(8,128)S(1)} %get-tuple-element.32.ties, f32[4,176,128]{2,1,0:T(8,128)S(1)} %get-tuple-element.54.field.refs_0_.image, f32[4,176,128]{2,1,0:T(8,128)S(1)} %get-tuple-element.49.diagonal, ...), custom_call_target="tpu_custom_call" | custom-call | flops 1 | bytes 1 | tf_op jit(solution)/shard_map/local_kernel/pallas_call | solution.py:757
  52.5 0.0 collective-permute-done.15.far
  52.5 0.0 collective-permute-done.14.near
  52.5 1.2 %cross_kernel.3 = (f32[4,168,128]{2,1,0:T(8,128)S(1)}, f32[32,128]{1,0:T(8,128)S(1)}) custom-call(s32[4]{0:T(128)S(1)} %pad_add_fusion.index, f32[8,4]{1,0:T(8,128)S(1)} %get-tuple-element.32.ties, f32[4,168,128]{2,1,0:T(8,128)S(1)} %get-tuple-element.55.image, f32[4,168,128]{2,1,0:T(8,128)S(1)} %collective-permute-done.14.near, ...), custom_call_target="tpu_custom_call" | custom-call | flops 1 | bytes 1 | tf_op jit(solution)/shard_map/cross_kernel/pallas_call | solution.py:786
  53.6 14.0 %all_to_all.11 = f32[32,1,128]{2,1,0:T(1,128)S(1)} all-to-all(f32[32,1,128]{2,1,0:T(1,128)S(1)} %bitcast.12), channel_id=1, replica_groups=mesh['tm'=4,'area'=8] {'tm','area'}, dimensions={0} | all-to-all | bytes 32768 | tf_op jit(solution)/shard_map/all_to_all | solution.py:791
  67.6 1.4 %last_kernel.1 = (f32[42,4,512]{2,1,0:T(4,128)}, f32[42,4,512]{2,1,0:T(4,128)}) custom-call(f32[32,128]{1,0:T(8,128)S(1)} %bitcast.11, f32[4,176,128]{2,1,0:T(8,128)S(1)} %get-tuple-element.33.guess.guess_in, f32[4,184,128]{2,1,0:T(8,128)S(1)} %get-tuple-element.48.field.refs_0_.residual, f32[4,176,128]{2,1,0:T(8,128)S(1)} %get-tuple-element.54.field.refs_0_.image, ...), custom_call_target="tpu_custom_call" | custom-call | flops 1 | bytes 1 | tf_op jit(solution)/shard_map/last_kernel/pallas_call | solution.py:794
  (11 shorter events, 0.1 us)
Async XLA Ops:
  3.1 13.1 %collective-permute-start.3 = (f32[96,256]{1,0:T(8,128)S(1)}, f32[96,256]{1,0:T(8,128)S(1)}, u32[]{:S(2)}, u32[]{:S(2)}) collective-permute-start(f32[96,256]{1,0:T(8,128)S(1)} %get-tuple-element.41), channel_id=1, source_target_pairs={{0,2},{1,5},{2,0},{3,7},{4,6},{5,1},{6,4},{7,3},{8,10},{9,13},{10,... | collective-permute-start | bytes 294920 | tf_op jit(solution)/shard_map/rows_chips/ppermute | solution.py:613
  6.2 10.1 %collective-permute-start.4 = (f32[96,256]{1,0:T(8,128)S(1)}, f32[96,256]{1,0:T(8,128)S(1)}, u32[]{:S(2)}, u32[]{:S(2)}) collective-permute-start(f32[96,256]{1,0:T(8,128)S(1)} %get-tuple-element.42), channel_id=1, source_target_pairs={{0,4},{1,7},{2,6},{3,5},{4,0},{5,3},{6,2},{7,1},{8,12},{9,15},{10,... | collective-permute-start | bytes 294920 | tf_op jit(solution)/shard_map/rows_chips/ppermute | solution.py:613
  8.7 7.6 %collective-permute-start.5 = (f32[96,256]{1,0:T(8,128)S(1)}, f32[96,256]{1,0:T(8,128)S(1)}, u32[]{:S(2)}, u32[]{:S(2)}) collective-permute-start(f32[96,256]{1,0:T(8,128)S(1)} %get-tuple-element.43), channel_id=1, source_target_pairs={{0,6},{1,3},{2,4},{3,1},{4,2},{5,7},{6,0},{7,5},{8,14},{9,11},{10,... | collective-permute-start | bytes 294920 | tf_op jit(solution)/shard_map/rows_chips/ppermute | solution.py:613
  8.7 12.9 %collective-permute-start.1 = (f32[4,176,128]{2,1,0:T(8,128)S(1)}, f32[4,176,128]{2,1,0:T(8,128)S(1)}, u32[]{:S(2)}, u32[]{:S(2)}) collective-permute-start(f32[4,176,128]{2,1,0:T(8,128)S(1)} %get-tuple-element.33.guess.guess_in), channel_id=1, source_target_pairs={{1,2},{3,4},{5,6},{2,1},{4,3},{6,5},{9,10},{11,12},{13,14},{10,9},... | collective-permute-start | bytes 1081352 | tf_op jit(solution)/shard_map/guess_far/ppermute | solution.py:620
  9.4 12.2 %collective-permute-start = (f32[4,176,128]{2,1,0:T(8,128)S(1)}, f32[4,176,128]{2,1,0:T(8,128)S(1)}, u32[]{:S(2)}, u32[]{:S(2)}) collective-permute-start(f32[4,176,128]{2,1,0:T(8,128)S(1)} %get-tuple-element.33.guess.guess_in), channel_id=1, source_target_pairs={{0,1},{1,0},{2,3},{3,2},{4,5},{5,4},{6,7},{7,6},{8,9},{9,8},{10,11... | collective-permute-start | bytes 1081352 | tf_op jit(solution)/shard_map/guess_near/ppermute | solution.py:598
  12.4 9.3 %copy-start = (f32[4,512]{1,0:T(4,128)S(1)}, f32[4,512]{1,0:T(4,128)}, u32[]{:S(2)}) copy-start(f32[4,512]{1,0:T(4,128)} %coupling.9) | copy-start | bytes 24580
  12.4 9.3 %copy-start.1 = (f32[4,512]{1,0:T(4,128)S(1)}, f32[4,512]{1,0:T(4,128)}, u32[]{:S(2)}) copy-start(f32[4,512]{1,0:T(4,128)} %ramp.7) | copy-start | bytes 24580
  16.2 1.7 %collective-permute-start.2 = (f32[144,256]{1,0:T(8,128)S(1)}, f32[144,256]{1,0:T(8,128)S(1)}, u32[]{:S(2)}, u32[]{:S(2)}) collective-permute-start(f32[144,256]{1,0:T(8,128)S(1)} %get-tuple-element.40), channel_id=1, source_target_pairs={{0,1},{1,0},{2,3},{3,2},{4,5},{5,4},{6,7},{7,6},{8,9},{9,8},{10,11... | collective-permute-start | bytes 442376 | tf_op jit(solution)/shard_map/rows_beside/ppermute | solution.py:598
  16.4 1.5 %collective-permute-start.6 = (f32[144,256]{1,0:T(8,128)S(1)}, f32[144,256]{1,0:T(8,128)S(1)}, u32[]{:S(2)}, u32[]{:S(2)}) collective-permute-start(f32[144,256]{1,0:T(8,128)S(1)} %pad_maximum_fusion), channel_id=1, source_target_pairs={{0,1},{1,0},{2,3},{3,2},{4,5},{5,4},{6,7},{7,6},{8,9},{9,8},{10,11... | collective-permute-start | bytes 442376 | tf_op jit(solution)/shard_map/rows_cores/ppermute | solution.py:598
  18.1 15.1 %collective-permute-start.11 = (f32[200,256]{1,0:T(8,128)S(1)}, f32[200,256]{1,0:T(8,128)S(1)}, u32[]{:S(2)}, u32[]{:S(2)}) collective-permute-start(f32[200,256]{1,0:T(8,128)S(1)} %constant_dynamic-update-slice_fusion.refs_0_), channel_id=1, source_target_pairs={{0,24},{1,25},{2,26},{3,27},{4,28},{5,29},{6,30},{7,31},{8,16},{9,... | collective-permute-start | bytes 614408 | tf_op jit(solution)/shard_map/rows_members/ppermute | solution.py:613
  20.6 12.6 %collective-permute-start.10 = (f32[200,256]{1,0:T(8,128)S(1)}, f32[200,256]{1,0:T(8,128)S(1)}, u32[]{:S(2)}, u32[]{:S(2)}) collective-permute-start(f32[200,256]{1,0:T(8,128)S(1)} %constant_dynamic-update-slice_fusion.refs_0_), channel_id=1, source_target_pairs={{0,16},{1,9},{2,18},{3,11},{4,20},{5,13},{6,22},{7,15},{8,24},{9,1... | collective-permute-start | bytes 614408 | tf_op jit(solution)/shard_map/rows_members/ppermute | solution.py:613
  21.1 12.1 %collective-permute-start.9 = (f32[200,256]{1,0:T(8,128)S(1)}, f32[200,256]{1,0:T(8,128)S(1)}, u32[]{:S(2)}, u32[]{:S(2)}) collective-permute-start(f32[200,256]{1,0:T(8,128)S(1)} %constant_dynamic-update-slice_fusion.refs_0_), channel_id=1, source_target_pairs={{0,8},{1,17},{2,10},{3,19},{4,12},{5,21},{6,14},{7,23},{8,0},{9,25... | collective-permute-start | bytes 614408 | tf_op jit(solution)/shard_map/rows_members/ppermute | solution.py:613
  23.8 7.2 %collective-permute-start.7 = (f32[4,20,128]{2,1,0:T(8,128)S(1)}, f32[4,20,128]{2,1,0:T(8,128)S(1)}, u32[]{:S(2)}, u32[]{:S(2)}) collective-permute-start(f32[4,20,128]{2,1,0:T(8,128)S(1)} %get-tuple-element.45), channel_id=1, source_target_pairs={{0,8},{8,16},{16,24},{1,9},{9,17},{17,25},{2,10},{10,18},{18,26},{... | collective-permute-start | bytes 122888 | tf_op jit(solution)/shard_map/partial_before/ppermute | solution.py:627
  27.2 6.0 %collective-permute-start.8 = (f32[4,20,128]{2,1,0:T(8,128)S(1)}, f32[4,20,128]{2,1,0:T(8,128)S(1)}, u32[]{:S(2)}, u32[]{:S(2)}) collective-permute-start(f32[4,20,128]{2,1,0:T(8,128)S(1)} %get-tuple-element.46), channel_id=1, source_target_pairs={{8,0},{16,8},{24,16},{9,1},{17,9},{25,17},{10,2},{18,10},{26,18},{... | collective-permute-start | bytes 122888 | tf_op jit(solution)/shard_map/partial_after/ppermute | solution.py:629
  35.6 7.2 %collective-permute-start.13 = (f32[4,176,128]{2,1,0:T(8,128)S(1)}, f32[4,176,128]{2,1,0:T(8,128)S(1)}, u32[]{:S(2)}, u32[]{:S(2)}) collective-permute-start(f32[4,176,128]{2,1,0:T(8,128)S(1)} %get-tuple-element.53), channel_id=1, source_target_pairs={{1,2},{3,4},{5,6},{2,1},{4,3},{6,5},{9,10},{11,12},{13,14},{10,9},... | collective-permute-start | bytes 1081352 | tf_op jit(solution)/shard_map/residual_far/ppermute | solution.py:620
  36.3 6.5 %collective-permute-start.12 = (f32[4,176,128]{2,1,0:T(8,128)S(1)}, f32[4,176,128]{2,1,0:T(8,128)S(1)}, u32[]{:S(2)}, u32[]{:S(2)}) collective-permute-start(f32[4,176,128]{2,1,0:T(8,128)S(1)} %get-tuple-element.53), channel_id=1, source_target_pairs={{0,1},{1,0},{2,3},{3,2},{4,5},{5,4},{6,7},{7,6},{8,9},{9,8},{10,11... | collective-permute-start | bytes 1081352 | tf_op jit(solution)/shard_map/residual_near/ppermute | solution.py:598
  43.7 8.7 %collective-permute-start.15 = (f32[4,168,128]{2,1,0:T(8,128)S(1)}, f32[4,168,128]{2,1,0:T(8,128)S(1)}, u32[]{:S(2)}, u32[]{:S(2)}) collective-permute-start(f32[4,168,128]{2,1,0:T(8,128)S(1)} %get-tuple-element.56), channel_id=1, source_target_pairs={{1,2},{3,4},{5,6},{2,1},{4,3},{6,5},{9,10},{11,12},{13,14},{10,9},... | collective-permute-start | bytes 1032200 | tf_op jit(solution)/shard_map/image_far/ppermute | solution.py:620
  44.4 8.1 %collective-permute-start.14 = (f32[4,168,128]{2,1,0:T(8,128)S(1)}, f32[4,168,128]{2,1,0:T(8,128)S(1)}, u32[]{:S(2)}, u32[]{:S(2)}) collective-permute-start(f32[4,168,128]{2,1,0:T(8,128)S(1)} %get-tuple-element.56), channel_id=1, source_target_pairs={{0,1},{1,0},{2,3},{3,2},{4,5},{5,4},{6,7},{7,6},{8,9},{9,8},{10,11... | collective-permute-start | bytes 1032200 | tf_op jit(solution)/shard_map/image_near/ppermute | solution.py:598

commit v4 on v3

--- a/solution.py
+++ b/solution.py
@@ -232,8 +232,8 @@
     for k in range(width // LANES):
         lanes = pl.ds(LANES * k, LANES)
         slack_rows = slack[:, :, lanes].reshape(shape)
-        right_out[k] = barrier[0] / slack_rows - gradient[:, :, lanes].reshape(shape)
-        diagonal_out[k] = hess[:, :, lanes].reshape(shape) + barrier[0] / (
+        right_out[k] = barrier[...] / slack_rows - gradient[:, :, lanes].reshape(shape)
+        diagonal_out[k] = hess[:, :, lanes].reshape(shape) + barrier[...] / (
             slack_rows * slack_rows
         )
     first = (index[0] * 2 + index[1] - 1) * span
@@ -567,7 +567,9 @@
             sent[k] = total[k, pl.ds(span, sent.shape[1]), :]
 
 
-def last_kernel(gathered, guess, residual, image, second, step_out, residual_out):
+def last_kernel(gathered, guess, residual, image, second, step_far, residual_far, *scratch):
+    step_out, residual_out, semaphores = scratch
+    copies = []
     sums = jnp.sum(gathered[...], axis=0, keepdims=True)
     rr, ra, aa, ab = (sums[:, k : k + 1] for k in range(4))
     alpha = rr / ra
@@ -577,7 +579,7 @@
     alpha_next = rr_next / (product - beta * rr_next / alpha)
     one = alpha + alpha_next * (1.0 + beta)
     two = alpha_next * alpha
-    hours, span, width = step_out.shape
+    hours, span, width = step_far.shape
     rows = hours * span
 
     def inner(ref, k):
@@ -588,8 +590,17 @@
         r, a = inner(residual, k), inner(image, k)
         step = guess[k, pl.ds(0, rows), :] + one * r - two * a
         left = r - one * a + two * second[k]
-        step_out[:, :, lanes] = step.reshape(hours, span, LANES)
-        residual_out[:, :, lanes] = left.reshape(hours, span, LANES)
+        step_out[k] = step.reshape(hours, span, LANES)
+        residual_out[k] = left.reshape(hours, span, LANES)
+        for source, target in ((step_out, step_far), (residual_out, residual_far)):
+            copies.append(
+                pltpu.make_async_copy(
+                    source.at[k], target.at[:, :, lanes], semaphores.at[len(copies)]
+                )
+            )
+            copies[-1].start()
+    for copy in copies:
+        copy.wait()
 
 
 def swap(value, axis, step, name):
@@ -687,12 +698,12 @@
     tile_high, tile_low, right_side, diagonal_in, ties = call(
         prepare_kernel,
         [tile_shape, tile_shape, field_shape, field_shape, f32_shape(2 * span, span)],
-        [SCALARS] * 2 + [IN_HBM] * 6 + [UNREAD],
+        [SCALARS, WHOLE] + [IN_HBM] * 6 + [UNREAD],
         [pltpu.VMEM(a.shape, F32) for a in natural]
         + [pltpu.SMEM(a.shape, a.dtype) for a in tables]
         + [pltpu.VMEM(tile.shape, F32), pltpu.SemaphoreType.DMA((5 + span,))],
         out_specs=[WHOLE] * 4 + [SCALARS],
-    )(index, barrier, *in_hbm(*natural, *tables, tile), here)
+    )(index, barrier.reshape(1, 1), *in_hbm(*natural, *tables, tile), here)
     near_guess, far_guess = exchange(guess, "guess")
 
     weights, outer = call(
@@ -795,6 +806,9 @@
             last_kernel,
             (out_shape, out_shape),
             [WHOLE] * 5,
+            [pltpu.VMEM((blocks, hours, span, LANES), F32)] * 2
+            + [pltpu.SemaphoreType.DMA((2 * blocks,))],
+            out_specs=[IN_HBM] * 2,
         )(gathered, guess, residual, image, second)
     )
 

time: 69.3 us -> 69.1 us (level)
  no operation moved by 1% of the time
where the time goes in v4:
time: 69.1 us; the launch traced here: 68.9 us
  starting transfers between devices  26.4 us (38%)
  Pallas kernels  21 us (30%)
  blocking collectives  14 us (20%)
  waiting for transfers between devices  5.72 us (8%)
  between operations  1.56 us (2%)
    all_to_all x1, blocking collectives, body(): lax.all_to_all(spread, ('tm', 'area'), split_axis=0, concat_axis=0, tiled...  14 us
    ppermute x5, starting transfers between devices, swap(): return lax.ppermute(value, axis, [(i, i ^ step) for i in range(count)])  10.4 us
    ppermute x6, starting transfers between devices, swap_by_core(): return lax.ppermute(value, ('tm', 'area'), pairs)  9.25 us
    pallas_call x2, Pallas kernels, local_image(): call(functools.partial(local_kernel, span, skip, summed), (shape, f32_sha...  6.99 us
    pallas_call x1, Pallas kernels, body(): call(prepare_kernel, [tile_shape, tile_shape, field_shape, field_shape, f...  3.77 us
    ppermute x1, starting transfers between devices, adjacent_hours(): before = lax.ppermute(up, 'tm', ups)  3.39 us
    ppermute x1, waiting for transfers between devices, adjacent_hours(): before = lax.ppermute(up, 'tm', ups)  2.47 us
    pallas_call x1, Pallas kernels, body(): call(functools.partial(owned_kernel, span, cap, deep), [deep_shape, next_...  2.39 us
  transfers between devices with their start and end apart: 16, of which 3 were waited for; matrix products, arithmetic and copies ran while one was open for 0% of the time, Pallas kernels for 19%

profile of v4, /device:TPU:0, one launch (start us, length us, event | category | flops | bytes accessed | tf_op | source)
XLA Modules:
  0.0 68.9 jit_solution(18167351195918301556)
XLA Ops:
  0.6 0.1 pad_add_fusion.index
  0.7 2.3 %pack_kernel.1 = (f32[96,256]{1,0:T(8,128)S(1)}, f32[96,256]{1,0:T(8,128)S(1)}, f32[96,256]{1,0:T(8,128)S(1)}, f32[144,256]{1,0:T(8,128)S(1)}, f32[144,256]{1,0:T(8,128)S(1)}, /*index=5*/f32[4,176,128]{2,1,0:T(8,128)S(1)}) custom-call(s32[4]{0:T(128)S(1)} %pad_add_fusion.index, s32[1,256]{1,0:T(1,128)} %bitcast.18, f32[256,512]{1,0:T(8,128)} %refs_1_.2, ...), custom_call_target="tpu_custom_call" | custom-call | flops 1 | bytes 1 | tf_op jit(solution)/shard_map/pack_kernel/pallas_call | solution.py:682
  3.1 3.1 %collective-permute-start.3 = (f32[96,256]{1,0:T(8,128)S(1)}, f32[96,256]{1,0:T(8,128)S(1)}, u32[]{:S(2)}, u32[]{:S(2)}) collective-permute-start(f32[96,256]{1,0:T(8,128)S(1)} %get-tuple-element.41), channel_id=1, source_target_pairs={{0,2},{1,5},{2,0},{3,7},{4,6},{5,1},{6,4},{7,3},{8,10},{9,13},{10,... | collective-permute-start | bytes 294920 | tf_op jit(solution)/shard_map/rows_chips/ppermute | solution.py:624
  6.2 2.6 %collective-permute-start.4 = (f32[96,256]{1,0:T(8,128)S(1)}, f32[96,256]{1,0:T(8,128)S(1)}, u32[]{:S(2)}, u32[]{:S(2)}) collective-permute-start(f32[96,256]{1,0:T(8,128)S(1)} %get-tuple-element.42), channel_id=1, source_target_pairs={{0,4},{1,7},{2,6},{3,5},{4,0},{5,3},{6,2},{7,1},{8,12},{9,15},{10,... | collective-permute-start | bytes 294920 | tf_op jit(solution)/shard_map/rows_chips/ppermute | solution.py:624
  8.7 0.0 collective-permute-start.5
  8.7 0.7 collective-permute-start.1
  9.4 2.3 %collective-permute-start = (f32[4,176,128]{2,1,0:T(8,128)S(1)}, f32[4,176,128]{2,1,0:T(8,128)S(1)}, u32[]{:S(2)}, u32[]{:S(2)}) collective-permute-start(f32[4,176,128]{2,1,0:T(8,128)S(1)} %get-tuple-element.33.guess.guess_in), channel_id=1, source_target_pairs={{0,1},{1,0},{2,3},{3,2},{4,5},{5,4},{6,7},{7,6},{8,9},{9,8},{10,11... | collective-permute-start | bytes 1081352 | tf_op jit(solution)/shard_map/guess_near/ppermute | solution.py:609
  12.4 0.0 copy-start
  12.4 0.0 copy-start.1
  12.4 3.8 %prepare_kernel.1 = (bf16[4,512,512]{2,1,0:T(8,128)(2,1)S(1)}, bf16[4,512,512]{2,1,0:T(8,128)(2,1)S(1)}, f32[4,168,128]{2,1,0:T(8,128)S(1)}, f32[4,168,128]{2,1,0:T(8,128)S(1)}, f32[8,4]{1,0:T(8,128)S(1)}) custom-call(s32[4]{0:T(128)S(1)} %pad_add_fusion.index, f32[1,1]{1,0:T(1,128)} %bitcast.12.barrier, f32[42,4,512]{2,1,0:T(4,128)} %refs_0_.1, ...), custom_call_target="tpu_custom_call" | custom-call | flops 1 | bytes 1 | tf_op jit(solution)/shard_map/prepare_kernel/pallas_call | solution.py:698
  16.2 0.0 collective-permute-done.3.refs_0_
  16.2 0.1 collective-permute-start.2
  16.3 0.0 collective-permute-done.4.refs_1_
  16.3 0.0 collective-permute-done.5.refs_2_
  16.4 0.5 collective-permute-start.6
  16.9 1.0 %collective-permute-done.6.crossed = f32[144,256]{1,0:T(8,128)S(1)} collective-permute-done((f32[144,256]{1,0:T(8,128)S(1)}, f32[144,256]{1,0:T(8,128)S(1)}, u32[]{:S(2)}, u32[]{:S(2)}) %collective-permute-start.6) | collective-permute-done | bytes 147488 | tf_op jit(solution)/shard_map/rows_cores/ppermute | solution.py:609
  17.9 0.0 collective-permute-done.2.beside
  17.9 0.1 weights_kernel.1
  18.1 2.5 %collective-permute-start.11 = (f32[200,256]{1,0:T(8,128)S(1)}, f32[200,256]{1,0:T(8,128)S(1)}, u32[]{:S(2)}, u32[]{:S(2)}) collective-permute-start(f32[200,256]{1,0:T(8,128)S(1)} %constant_dynamic-update-slice_fusion.refs_0_), channel_id=1, source_target_pairs={{0,24},{1,25},{2,26},{3,27},{4,28},{5,29},{6,30},{7,31},{8,16},{9,... | collective-permute-start | bytes 614408 | tf_op jit(solution)/shard_map/rows_members/ppermute | solution.py:624
  20.6 0.5 collective-permute-start.10
  21.1 0.5 collective-permute-start.9
  21.6 0.0 collective-permute-done.1.far.far_first
  21.6 0.0 collective-permute-done.near.near_first
  21.6 0.0 copy-done
  21.7 0.0 copy-done.1
  21.7 2.1 %first_kernel.1 = (f32[4,168,128]{2,1,0:T(8,128)S(1)}, f32[4,168,128]{2,1,0:T(8,128)S(1)}, f32[4,20,128]{2,1,0:T(8,128)S(1)}, f32[4,20,128]{2,1,0:T(8,128)S(1)}) custom-call(s32[4]{0:T(128)S(1)} %pad_add_fusion.index, f32[8,4]{1,0:T(8,128)S(1)} %get-tuple-element.32.ties, f32[4,176,128]{2,1,0:T(8,128)S(1)} %get-tuple-element.33.guess.guess_in, ...), custom_call_target="tpu_custom_call" | custom-call | flops 10000000000 | bytes 1 | tf_op jit(solution)/shard_map/first_kernel/pallas_call | solution.py:728
  23.8 3.4 %collective-permute-start.7 = (f32[4,20,128]{2,1,0:T(8,128)S(1)}, f32[4,20,128]{2,1,0:T(8,128)S(1)}, u32[]{:S(2)}, u32[]{:S(2)}) collective-permute-start(f32[4,20,128]{2,1,0:T(8,128)S(1)} %get-tuple-element.45), channel_id=1, source_target_pairs={{0,8},{8,16},{16,24},{1,9},{9,17},{17,25},{2,10},{10,18},{18,26},{... | collective-permute-start | bytes 122888 | tf_op jit(solution)/shard_map/partial_before/ppermute | solution.py:638
  27.2 1.3 %collective-permute-start.8 = (f32[4,20,128]{2,1,0:T(8,128)S(1)}, f32[4,20,128]{2,1,0:T(8,128)S(1)}, u32[]{:S(2)}, u32[]{:S(2)}) collective-permute-start(f32[4,20,128]{2,1,0:T(8,128)S(1)} %get-tuple-element.46), channel_id=1, source_target_pairs={{8,0},{16,8},{24,16},{9,1},{17,9},{25,17},{10,2},{18,10},{26,18},{... | collective-permute-start | bytes 122888 | tf_op jit(solution)/shard_map/partial_after/ppermute | solution.py:640
  28.5 2.5 %collective-permute-done.7.before = f32[4,20,128]{2,1,0:T(8,128)S(1)} collective-permute-done((f32[4,20,128]{2,1,0:T(8,128)S(1)}, f32[4,20,128]{2,1,0:T(8,128)S(1)}, u32[]{:S(2)}, u32[]{:S(2)}) %collective-permute-start.7) | collective-permute-done | bytes 40992 | tf_op jit(solution)/shard_map/partial_before/ppermute | solution.py:638
  30.9 2.2 %collective-permute-done.8.after = f32[4,20,128]{2,1,0:T(8,128)S(1)} collective-permute-done((f32[4,20,128]{2,1,0:T(8,128)S(1)}, f32[4,20,128]{2,1,0:T(8,128)S(1)}, u32[]{:S(2)}, u32[]{:S(2)}) %collective-permute-start.8) | collective-permute-done | bytes 40992 | tf_op jit(solution)/shard_map/partial_after/ppermute | solution.py:640
  33.2 0.0 collective-permute-done.11.refs_3_
  33.2 0.0 collective-permute-done.10.refs_2_
  33.2 0.0 collective-permute-done.9.refs_1_
  33.2 2.4 %owned_kernel.1 = (f32[4,184,128]{2,1,0:T(8,128)S(1)}, f32[4,176,128]{2,1,0:T(8,128)S(1)}, bf16[4,128,512]{2,1,0:T(8,128)(2,1)S(1)}, bf16[4,128,512]{2,1,0:T(8,1...) custom-call(s32[4]{0:T(128)S(1)} %pad_add_fusion.index, ...), custom_call_target="tpu_custom_call" | custom-call | flops 1 | bytes 1 | tf_op jit(solution)/shard_map/owned_kernel/pallas_call | solution.py:751
  35.6 0.7 collective-permute-start.13
  36.3 3.0 %collective-permute-start.12 = (f32[4,176,128]{2,1,0:T(8,128)S(1)}, f32[4,176,128]{2,1,0:T(8,128)S(1)}, u32[]{:S(2)}, u32[]{:S(2)}) collective-permute-start(f32[4,176,128]{2,1,0:T(8,128)S(1)} %get-tuple-element.53), channel_id=1, source_target_pairs={{0,1},{1,0},{2,3},{3,2},{4,5},{5,4},{6,7},{7,6},{8,9},{9,8},{10,11... | collective-permute-start | bytes 1081352 | tf_op jit(solution)/shard_map/residual_near/ppermute | solution.py:609
  39.2 3.5 %local_kernel.2.image = f32[4,176,128]{2,1,0:T(8,128)S(1)} custom-call(s32[4]{0:T(128)S(1)} %pad_add_fusion.index, f32[8,4]{1,0:T(8,128)S(1)} %get-tuple-element.32.ties, f32[4,184,128]{2,1,0:T(8,128)S(1)} %get-tuple-element.48.field.refs_0_.residual, f32[4,176,128]{2,1,0:T(8,128)S(1)} %get-tuple-element.49.diagonal, f32[4,512]{1,0:T(4,128)S(1)} %copy-done.1, ...), custom_call_target="tpu_custom_call" | custom-call | flops 1 | bytes 1 | tf_op jit(solution)/shard_map/local_kernel/pallas_call | solution.py:768
  42.7 0.0 collective-permute-done.13.far
  42.8 0.0 collective-permute-done.12.near
  42.8 1.0 %cross_kernel.2 = (f32[4,176,128]{2,1,0:T(8,128)S(1)}, f32[4,168,128]{2,1,0:T(8,128)S(1)}) custom-call(s32[4]{0:T(128)S(1)} %pad_add_fusion.index, f32[8,4]{1,0:T(8,128)S(1)} %get-tuple-element.32.ties, f32[4,176,128]{2,1,0:T(8,128)S(1)} %local_kernel.2.image, f32[4,176,128]{2,1,0:T(8,128)S(1)} %collective-permute-done.12.near, ...), custom_call_target="tpu_custom_call" | custom-call | flops 1 | bytes 1 | tf_op jit(solution)/shard_map/cross_kernel/pallas_call | solution.py:789
  43.7 0.7 collective-permute-start.15
  44.4 4.5 %collective-permute-start.14 = (f32[4,168,128]{2,1,0:T(8,128)S(1)}, f32[4,168,128]{2,1,0:T(8,128)S(1)}, u32[]{:S(2)}, u32[]{:S(2)}) collective-permute-start(f32[4,168,128]{2,1,0:T(8,128)S(1)} %get-tuple-element.56), channel_id=1, source_target_pairs={{0,1},{1,0},{2,3},{3,2},{4,5},{5,4},{6,7},{7,6},{8,9},{9,8},{10,11... | collective-permute-start | bytes 1032200 | tf_op jit(solution)/shard_map/image_near/ppermute | solution.py:609
  49.0 3.5 %local_kernel.3 = (f32[4,168,128]{2,1,0:T(8,128)S(1)}, f32[1,128]{1,0:T(1,128)S(1)}) custom-call(s32[4]{0:T(128)S(1)} %pad_add_fusion.index, f32[8,4]{1,0:T(8,128)S(1)} %get-tuple-element.32.ties, f32[4,176,128]{2,1,0:T(8,128)S(1)} %get-tuple-element.54.field.refs_0_.image, f32[4,176,128]{2,1,0:T(8,128)S(1)} %get-tuple-element.49.diagonal, ...), custom_call_target="tpu_custom_call" | custom-call | flops 1 | bytes 1 | tf_op jit(solution)/shard_map/local_kernel/pallas_call | solution.py:768
  52.5 0.0 collective-permute-done.15.far
  52.5 0.0 collective-permute-done.14.near
  52.5 1.2 %cross_kernel.3 = (f32[4,168,128]{2,1,0:T(8,128)S(1)}, f32[32,128]{1,0:T(8,128)S(1)}) custom-call(s32[4]{0:T(128)S(1)} %pad_add_fusion.index, f32[8,4]{1,0:T(8,128)S(1)} %get-tuple-element.32.ties, f32[4,168,128]{2,1,0:T(8,128)S(1)} %get-tuple-element.55.image, f32[4,168,128]{2,1,0:T(8,128)S(1)} %collective-permute-done.14.near, ...), custom_call_target="tpu_custom_call" | custom-call | flops 1 | bytes 1 | tf_op jit(solution)/shard_map/cross_kernel/pallas_call | solution.py:797
  53.6 14.0 %all_to_all.11 = f32[32,1,128]{2,1,0:T(1,128)S(1)} all-to-all(f32[32,1,128]{2,1,0:T(1,128)S(1)} %bitcast.14), channel_id=1, replica_groups=mesh['tm'=4,'area'=8] {'tm','area'}, dimensions={0} | all-to-all | bytes 32768 | tf_op jit(solution)/shard_map/all_to_all | solution.py:802
  67.7 1.2 %last_kernel.1 = (f32[42,4,512]{2,1,0:T(4,128)}, f32[42,4,512]{2,1,0:T(4,128)}) custom-call(f32[32,128]{1,0:T(8,128)S(1)} %bitcast.13, f32[4,176,128]{2,1,0:T(8,128)S(1)} %get-tuple-element.33.guess.guess_in, f32[4,184,128]{2,1,0:T(8,128)S(1)} %get-tuple-element.48.field.refs_0_.residual, f32[4,176,128]{2,1,0:T(8,128)S(1)} %get-tuple-element.54.field.refs_0_.image, ...), custom_call_target="tpu_custom_call" | custom-call | flops 1 | bytes 1 | tf_op jit(solution)/shard_map/last_kernel/pallas_call | solution.py:805
  (11 shorter events, 0.1 us)
Async XLA Ops:
  3.1 13.1 %collective-permute-start.3 = (f32[96,256]{1,0:T(8,128)S(1)}, f32[96,256]{1,0:T(8,128)S(1)}, u32[]{:S(2)}, u32[]{:S(2)}) collective-permute-start(f32[96,256]{1,0:T(8,128)S(1)} %get-tuple-element.41), channel_id=1, source_target_pairs={{0,2},{1,5},{2,0},{3,7},{4,6},{5,1},{6,4},{7,3},{8,10},{9,13},{10,... | collective-permute-start | bytes 294920 | tf_op jit(solution)/shard_map/rows_chips/ppermute | solution.py:624
  6.2 10.1 %collective-permute-start.4 = (f32[96,256]{1,0:T(8,128)S(1)}, f32[96,256]{1,0:T(8,128)S(1)}, u32[]{:S(2)}, u32[]{:S(2)}) collective-permute-start(f32[96,256]{1,0:T(8,128)S(1)} %get-tuple-element.42), channel_id=1, source_target_pairs={{0,4},{1,7},{2,6},{3,5},{4,0},{5,3},{6,2},{7,1},{8,12},{9,15},{10,... | collective-permute-start | bytes 294920 | tf_op jit(solution)/shard_map/rows_chips/ppermute | solution.py:624
  8.7 7.6 %collective-permute-start.5 = (f32[96,256]{1,0:T(8,128)S(1)}, f32[96,256]{1,0:T(8,128)S(1)}, u32[]{:S(2)}, u32[]{:S(2)}) collective-permute-start(f32[96,256]{1,0:T(8,128)S(1)} %get-tuple-element.43), channel_id=1, source_target_pairs={{0,6},{1,3},{2,4},{3,1},{4,2},{5,7},{6,0},{7,5},{8,14},{9,11},{10,... | collective-permute-start | bytes 294920 | tf_op jit(solution)/shard_map/rows_chips/ppermute | solution.py:624
  8.7 12.9 %collective-permute-start.1 = (f32[4,176,128]{2,1,0:T(8,128)S(1)}, f32[4,176,128]{2,1,0:T(8,128)S(1)}, u32[]{:S(2)}, u32[]{:S(2)}) collective-permute-start(f32[4,176,128]{2,1,0:T(8,128)S(1)} %get-tuple-element.33.guess.guess_in), channel_id=1, source_target_pairs={{1,2},{3,4},{5,6},{2,1},{4,3},{6,5},{9,10},{11,12},{13,14},{10,9},... | collective-permute-start | bytes 1081352 | tf_op jit(solution)/shard_map/guess_far/ppermute | solution.py:631
  9.4 12.2 %collective-permute-start = (f32[4,176,128]{2,1,0:T(8,128)S(1)}, f32[4,176,128]{2,1,0:T(8,128)S(1)}, u32[]{:S(2)}, u32[]{:S(2)}) collective-permute-start(f32[4,176,128]{2,1,0:T(8,128)S(1)} %get-tuple-element.33.guess.guess_in), channel_id=1, source_target_pairs={{0,1},{1,0},{2,3},{3,2},{4,5},{5,4},{6,7},{7,6},{8,9},{9,8},{10,11... | collective-permute-start | bytes 1081352 | tf_op jit(solution)/shard_map/guess_near/ppermute | solution.py:609
  12.4 9.3 %copy-start = (f32[4,512]{1,0:T(4,128)S(1)}, f32[4,512]{1,0:T(4,128)}, u32[]{:S(2)}) copy-start(f32[4,512]{1,0:T(4,128)} %coupling.9) | copy-start | bytes 24580
  12.4 9.3 %copy-start.1 = (f32[4,512]{1,0:T(4,128)S(1)}, f32[4,512]{1,0:T(4,128)}, u32[]{:S(2)}) copy-start(f32[4,512]{1,0:T(4,128)} %ramp.7) | copy-start | bytes 24580
  16.2 1.7 %collective-permute-start.2 = (f32[144,256]{1,0:T(8,128)S(1)}, f32[144,256]{1,0:T(8,128)S(1)}, u32[]{:S(2)}, u32[]{:S(2)}) collective-permute-start(f32[144,256]{1,0:T(8,128)S(1)} %get-tuple-element.40), channel_id=1, source_target_pairs={{0,1},{1,0},{2,3},{3,2},{4,5},{5,4},{6,7},{7,6},{8,9},{9,8},{10,11... | collective-permute-start | bytes 442376 | tf_op jit(solution)/shard_map/rows_beside/ppermute | solution.py:609
  16.4 1.5 %collective-permute-start.6 = (f32[144,256]{1,0:T(8,128)S(1)}, f32[144,256]{1,0:T(8,128)S(1)}, u32[]{:S(2)}, u32[]{:S(2)}) collective-permute-start(f32[144,256]{1,0:T(8,128)S(1)} %pad_maximum_fusion), channel_id=1, source_target_pairs={{0,1},{1,0},{2,3},{3,2},{4,5},{5,4},{6,7},{7,6},{8,9},{9,8},{10,11... | collective-permute-start | bytes 442376 | tf_op jit(solution)/shard_map/rows_cores/ppermute | solution.py:609
  18.1 15.1 %collective-permute-start.11 = (f32[200,256]{1,0:T(8,128)S(1)}, f32[200,256]{1,0:T(8,128)S(1)}, u32[]{:S(2)}, u32[]{:S(2)}) collective-permute-start(f32[200,256]{1,0:T(8,128)S(1)} %constant_dynamic-update-slice_fusion.refs_0_), channel_id=1, source_target_pairs={{0,24},{1,25},{2,26},{3,27},{4,28},{5,29},{6,30},{7,31},{8,16},{9,... | collective-permute-start | bytes 614408 | tf_op jit(solution)/shard_map/rows_members/ppermute | solution.py:624
  20.6 12.6 %collective-permute-start.10 = (f32[200,256]{1,0:T(8,128)S(1)}, f32[200,256]{1,0:T(8,128)S(1)}, u32[]{:S(2)}, u32[]{:S(2)}) collective-permute-start(f32[200,256]{1,0:T(8,128)S(1)} %constant_dynamic-update-slice_fusion.refs_0_), channel_id=1, source_target_pairs={{0,16},{1,9},{2,18},{3,11},{4,20},{5,13},{6,22},{7,15},{8,24},{9,1... | collective-permute-start | bytes 614408 | tf_op jit(solution)/shard_map/rows_members/ppermute | solution.py:624
  21.1 12.1 %collective-permute-start.9 = (f32[200,256]{1,0:T(8,128)S(1)}, f32[200,256]{1,0:T(8,128)S(1)}, u32[]{:S(2)}, u32[]{:S(2)}) collective-permute-start(f32[200,256]{1,0:T(8,128)S(1)} %constant_dynamic-update-slice_fusion.refs_0_), channel_id=1, source_target_pairs={{0,8},{1,17},{2,10},{3,19},{4,12},{5,21},{6,14},{7,23},{8,0},{9,25... | collective-permute-start | bytes 614408 | tf_op jit(solution)/shard_map/rows_members/ppermute | solution.py:624
  23.8 7.2 %collective-permute-start.7 = (f32[4,20,128]{2,1,0:T(8,128)S(1)}, f32[4,20,128]{2,1,0:T(8,128)S(1)}, u32[]{:S(2)}, u32[]{:S(2)}) collective-permute-start(f32[4,20,128]{2,1,0:T(8,128)S(1)} %get-tuple-element.45), channel_id=1, source_target_pairs={{0,8},{8,16},{16,24},{1,9},{9,17},{17,25},{2,10},{10,18},{18,26},{... | collective-permute-start | bytes 122888 | tf_op jit(solution)/shard_map/partial_before/ppermute | solution.py:638
  27.2 6.0 %collective-permute-start.8 = (f32[4,20,128]{2,1,0:T(8,128)S(1)}, f32[4,20,128]{2,1,0:T(8,128)S(1)}, u32[]{:S(2)}, u32[]{:S(2)}) collective-permute-start(f32[4,20,128]{2,1,0:T(8,128)S(1)} %get-tuple-element.46), channel_id=1, source_target_pairs={{8,0},{16,8},{24,16},{9,1},{17,9},{25,17},{10,2},{18,10},{26,18},{... | collective-permute-start | bytes 122888 | tf_op jit(solution)/shard_map/partial_after/ppermute | solution.py:640
  35.6 7.2 %collective-permute-start.13 = (f32[4,176,128]{2,1,0:T(8,128)S(1)}, f32[4,176,128]{2,1,0:T(8,128)S(1)}, u32[]{:S(2)}, u32[]{:S(2)}) collective-permute-start(f32[4,176,128]{2,1,0:T(8,128)S(1)} %get-tuple-element.53), channel_id=1, source_target_pairs={{1,2},{3,4},{5,6},{2,1},{4,3},{6,5},{9,10},{11,12},{13,14},{10,9},... | collective-permute-start | bytes 1081352 | tf_op jit(solution)/shard_map/residual_far/ppermute | solution.py:631
  36.3 6.5 %collective-permute-start.12 = (f32[4,176,128]{2,1,0:T(8,128)S(1)}, f32[4,176,128]{2,1,0:T(8,128)S(1)}, u32[]{:S(2)}, u32[]{:S(2)}) collective-permute-start(f32[4,176,128]{2,1,0:T(8,128)S(1)} %get-tuple-element.53), channel_id=1, source_target_pairs={{0,1},{1,0},{2,3},{3,2},{4,5},{5,4},{6,7},{7,6},{8,9},{9,8},{10,11... | collective-permute-start | bytes 1081352 | tf_op jit(solution)/shard_map/residual_near/ppermute | solution.py:609
  43.7 8.7 %collective-permute-start.15 = (f32[4,168,128]{2,1,0:T(8,128)S(1)}, f32[4,168,128]{2,1,0:T(8,128)S(1)}, u32[]{:S(2)}, u32[]{:S(2)}) collective-permute-start(f32[4,168,128]{2,1,0:T(8,128)S(1)} %get-tuple-element.56), channel_id=1, source_target_pairs={{1,2},{3,4},{5,6},{2,1},{4,3},{6,5},{9,10},{11,12},{13,14},{10,9},... | collective-permute-start | bytes 1032200 | tf_op jit(solution)/shard_map/image_far/ppermute | solution.py:631
  44.4 8.1 %collective-permute-start.14 = (f32[4,168,128]{2,1,0:T(8,128)S(1)}, f32[4,168,128]{2,1,0:T(8,128)S(1)}, u32[]{:S(2)}, u32[]{:S(2)}) collective-permute-start(f32[4,168,128]{2,1,0:T(8,128)S(1)} %get-tuple-element.56), channel_id=1, source_target_pairs={{0,1},{1,0},{2,3},{3,2},{4,5},{5,4},{6,7},{7,6},{8,9},{9,8},{10,11... | collective-permute-start | bytes 1032200 | tf_op jit(solution)/shard_map/image_near/ppermute | solution.py:609
